TPU v7x, 32 devices: a whole 2x2x4 slice. The times are simulated.
32 devices in a mesh: expert: 4 (over y, x), cuts: 8 (over z, core).
Axes of the slice: x: 2, y: 2, z: 4, core: 2. Of those that a mesh axis runs over, the one named last changes fastest.
Arguments:
- out_grad: bfloat16 [512, 6144], P('expert', 'cuts'), may hold values from -6 to 6
- gate_probs: float32 [512, 2], P('expert'), may hold values from 0.2 to 1
- expert_ids: int32 [512, 2], P('expert'), may hold values from 0 to 3, all different within a row; in each aligned block of 128 rows (0 to 127, 128 to 255, ...) at most 64 rows name the same one
- gate_pre: bfloat16 [4, 4, 64, 8192], P('expert', None, None, 'cuts'), may hold values from -6 to 6
- up_pre: bfloat16 [4, 4, 64, 8192], P('expert', None, None, 'cuts'), may hold values from -6 to 6
- w_gate: bfloat16 [4, 6144, 8192], P('expert', None, 'cuts'), may hold values from -0.109375 to 0.109375
- w_up: bfloat16 [4, 6144, 8192], P('expert', None, 'cuts'), may hold values from -0.109375 to 0.109375
- w_down: bfloat16 [4, 8192, 6144], P('expert', 'cuts'), may hold values from -0.0625 to 0.0625
Outputs:
- input_grad: bfloat16 [512, 6144], P('expert', 'cuts')
- w_down_grad: bfloat16 [4, 8192, 6144], P('expert', 'cuts')
Inputs may be any that keep to these rules, and one draw needn't show every extreme that they name: `expert_ids`: each row names 2 different experts. Among the 128 tokens of one index of the expert axis no expert is named more than 64 times.
All inputs are finite; a program needn't handle non-finite values.
Results may differ from a plain program's by a relative error of at most 0.034.
Values may be sent and summed in bfloat16 or wider, within the bound.
No kernel may reach another device: no remote copies, remote signals or barrier semaphores. Data moves between devices by JAX's collectives and lax.ppermute only.
A program may use at most 128 MiB of HBM per device.

v0:
```python
import jax
import jax.numpy as jnp
from jax import lax
from jax.sharding import PartitionSpec as P


def slot_tables(routing, experts, capacity):
    chosen = routing.reshape(-1)
    onehot = (chosen[:, None] == jnp.arange(experts, dtype=jnp.int32)[None, :]).astype(jnp.int32)
    earlier = jnp.cumsum(onehot, axis=0) - onehot
    position = jnp.sum(earlier * onehot, axis=1)
    target = chosen * capacity + position
    source = jnp.full((experts * capacity,), chosen.shape[0], jnp.int32)
    source = source.at[target].set(jnp.arange(chosen.shape[0], dtype=jnp.int32))
    return (target, source)


def pack_rows(out_rows, gate_values, source, experts, capacity):
    columns = out_rows.shape[1]
    weighted = (gate_values[:, :, None] * out_rows[:, None, :].astype(jnp.float32)).astype(
        jnp.bfloat16
    )
    weighted = weighted.reshape(-1, columns)
    weighted = jnp.concatenate([weighted, jnp.zeros((1, columns), jnp.bfloat16)], axis=0)
    return jnp.take(weighted, source, axis=0).reshape(experts, capacity, columns)


def on_device(out_grad, gate_probs, expert_ids, gate_pre, up_pre, w_gate, w_up, w_down):
    tokens_here = expert_ids.shape[0]
    experts = lax.axis_size("expert") * w_gate.shape[0]
    groups = gate_pre.shape[1]
    capacity = gate_pre.shape[2]
    units = gate_pre.shape[3]
    local_cols = out_grad.shape[1]
    slot_rows = groups * capacity
    target, source = slot_tables(expert_ids, experts, capacity)
    down_weight = w_down[0]
    contract_last = (((1,), (1,)), ((), ()))
    contract_first = (((0,), (0,)), ((), ()))
    gate_act = gate_pre[0].reshape(slot_rows, units).astype(jnp.float32)
    up_act = up_pre[0].reshape(slot_rows, units).astype(jnp.float32)
    logistic = jax.nn.sigmoid(gate_act)
    hidden_act = (gate_act * logistic * up_act).astype(jnp.bfloat16)
    features = lax.all_gather(out_grad, "cuts", axis=1, tiled=True)
    outgoing = pack_rows(features, gate_probs, source, experts, capacity)
    routed = lax.all_to_all(outgoing, "expert", split_axis=0, concat_axis=0, tiled=True)
    routed = routed.reshape(slot_rows, routed.shape[2])
    hidden_grad = lax.dot_general(
        routed, down_weight, contract_last, preferred_element_type=jnp.float32
    )
    down_grad = lax.dot_general(
        hidden_act, routed, contract_first, preferred_element_type=jnp.float32
    )
    w_down_grad = down_grad.astype(jnp.bfloat16)[None]
    up_grad = (hidden_grad * gate_act * logistic).astype(jnp.bfloat16)
    gate_grad = (hidden_grad * up_act * logistic * (1.0 + gate_act * (1.0 - logistic))).astype(
        jnp.bfloat16
    )
    gate_weight = w_gate[0]
    up_weight = w_up[0]
    partial_value = lax.dot_general(
        gate_weight, gate_grad, contract_last, preferred_element_type=jnp.float32
    )
    partial_value = partial_value + lax.dot_general(
        up_weight, up_grad, contract_last, preferred_element_type=jnp.float32
    )
    summed = lax.psum_scatter(
        lax.optimization_barrier(partial_value.astype(jnp.bfloat16))
        .astype(jnp.float32)
        .astype(jnp.bfloat16),
        "cuts",
        scatter_dimension=0,
        tiled=True,
    ).astype(jnp.float32)
    summed = summed.reshape(local_cols, groups, capacity)
    returned = lax.all_to_all(
        summed.astype(jnp.bfloat16), "expert", split_axis=1, concat_axis=1, tiled=True
    ).astype(summed.dtype)
    flat_back = returned.reshape(local_cols, experts * capacity)
    picked = jnp.take(flat_back, target, axis=1).reshape(local_cols, tokens_here, -1)
    input_grad = jnp.sum(picked, axis=2)
    return (input_grad.T.astype(jnp.bfloat16), w_down_grad)


def solution(mesh):
    return jax.shard_map(
        on_device,
        mesh=mesh,
        in_specs=(
            P("expert", "cuts"),
            P("expert", None),
            P("expert", None),
            P("expert", None, None, "cuts"),
            P("expert", None, None, "cuts"),
            P("expert", None, "cuts"),
            P("expert", None, "cuts"),
            P("expert", "cuts", None),
        ),
        out_specs=(P("expert", "cuts"), P("expert", "cuts", None)),
        check_vma=False,
    )
```

profile of v0, /device:TPU:0, one launch (start us, length us, event | category | flops | bytes accessed | tf_op | source)
XLA Modules:
  0.0 199.0 jit_solution(7018377187101171257)
XLA Ops:
  7.2 0.0 all-gather.2.cloned.1.call-start
  7.2 0.7 all-gather.2.cloned.1.call-update
  7.9 0.0 reduce-scatter.2.cloned.1.call-start
  7.9 0.8 copy.19
  8.7 0.1 eq.26
  8.9 0.1 reshape.101
  9.0 0.7 broadcast_multiply_fusion
  9.7 0.1 copy.25
  9.8 0.1 mul.69
  10.0 1.2 reduce-window.6
  11.2 0.1 slice.12
  11.3 0.1 copy.21
  11.4 0.1 copy.22
  11.5 0.1 add_bitcast_fusion
  11.6 1.4 scatter_custom_fusion
  13.0 0.1 broadcast_in_dim.33
  13.1 0.8 copy.26
  13.9 0.1 mul.70
  14.1 23.3 %all-gather.2.cloned.1.call-done = bf16[128,6144]{1,0:T(8,128)(2,1)} async-done(((bf16[128,768]{1,0:T(8,128)(2,1)}), bf16[128,6144]{1,0:T(8,128)(2,1)}) %all-gather.2.cloned.1.call-update) | async-done | bytes 1572880 | tf_op jit(solution)/shard_map/all_gather | solution.py:44
  37.4 6.7 %mul.72 = f32[128,2,6144]{2,1,0:T(2,128)} broadcast(bf16[128,6144]{1,0:T(8,128)(2,1)} %all-gather.2.cloned.1.call-done), dimensions={0,2} | broadcast | bytes 7864320 | tf_op jit(solution)/shard_map/mul | solution.py:20
  44.1 8.3 %mul.73 = f32[256,6144]{1,0:T(8,128)} reshape(f32[128,2,6144]{2,1,0:T(2,128)} %mul.72) | data formatting | bytes 12582912 | tf_op jit(solution)/shard_map/mul | solution.py:20
  52.5 3.5 %multiply_convert_fusion = bf16[256,6144]{1,0:T(8,128)(2,1)S(1)} fusion(f32[256,6144]{1,0:T(8,128)} %mul.73, f32[256]{0:T(256)S(1)} %mul.70), kind=kLoop, calls=%fused_computation.13 | loop fusion | flops 3145728 | bytes 9438208 | tf_op jit(solution)/shard_map/convert_element_type | solution.py:20
  55.9 0.3 concatenate.3
  56.3 4.1 %gather_fusion = bf16[256,6144]{1,0:T(8,128)(2,1)} fusion(bf16[257,6144]{1,0:T(8,128)(2,1)S(1)} %concatenate.3, s32[1024]{0:T(1024)S(1)} %pad_clamp_fusion.1), kind=kCustom, calls=%fused_computation | custom fusion | bytes 6292480 | tf_op jit(solution)/shard_map/jit(_take)/gather | solution.py:25
  60.4 0.0 copy-start
  60.4 0.0 copy-start.1
  60.4 2.3 %broadcast_select_fusion = bf16[4,64,6144]{2,1,0:T(8,128)(2,1)S(1)} fusion(bf16[4,64,6144]{2,1,0:T(8,128)(2,1)} %bitcast.93, pred[4,64]{1,0:T(4,128)(4,1)S(1)} %broadcast_in_dim.33), kind=kLoop, calls=%fused_computation.14 | loop fusion | flops 1572864 | bytes 6291712 | tf_op jit(solution)/shard_map/jit(_take)/select_n | solution.py:25
  62.7 40.5 %all_to_all.10 = bf16[4,64,6144]{2,1,0:T(8,128)(2,1)S(1)} all-to-all(bf16[4,64,6144]{2,1,0:T(8,128)(2,1)S(1)} %broadcast_select_fusion), channel_id=1, replica_groups=mesh['expert'=4,'cuts'=8] {'expert'}, dimensions={0} | all-to-all | bytes 6291456 | tf_op jit(solution)/shard_map/all_to_all | solution.py:46
  103.2 0.0 copy-done
  103.2 0.0 copy-done.1
  103.2 9.2 %fusion.24 = (bf16[256,1024]{1,0:T(8,128)(2,1)}, bf16[256,1024]{1,0:T(8,128)(2,1)S(1)}) fusion(bf16[1,4,64,1024]{3,2,1,0:T(8,128)(2,1)S(1)} %copy-done, bf16[1,4,64,1024]{3,2,1,0:T(8,128)(2,1)S(1)} %copy-done.1, bf16[256,6144]{1,0:T(8,128)(2,1)S(1)} %bitcast.91, bf16[1,1024,6144]{2,1,0:T(8,128)(2,1)} %param.15), kind=kOutput, calls=%fused_computation.29 | convolution fusion | flops 3225157632 | bytes 17825792 | tf_op jit(solution)/shard_map/dot_general | solution.py:48
  112.4 14.7 %fusion = f32[256,6144]{1,0:T(8,128)} fusion(bf16[256,1024]{1,0:T(8,128)(2,1)S(1)} %get-tuple-element.3, bf16[1,6144,1024]{2,1,0:T(8,128)(2,1)} %param.14), kind=kOutput, calls=%fused_computation.3 | convolution fusion | flops 3221225472 | bytes 19398656 | tf_op jit(solution)/shard_map/dot_general | solution.py:64
  127.0 11.6 %fusion.12 = bf16[6144,256]{0,1:T(8,128)(2,1)} fusion(f32[256,6144]{1,0:T(8,128)} %fusion, bf16[256,1024]{1,0:T(8,128)(2,1)} %get-tuple-element.2, bf16[1,6144,1024]{2,1,0:T(8,128)(2,1)} %param.13), kind=kOutput, calls=%fused_computation.12 | convolution fusion | flops 3224371200 | bytes 22544384 | tf_op jit(solution)/shard_map/dot_general | solution.py:61
  138.7 0.0 reduce-scatter.2.cloned.1.call-update
  138.7 0.1 reduce_sum.23
  138.8 0.1 copy.23
  138.9 0.0 copy-done.2
  138.9 0.1 copy.24
  139.1 0.6 pad_clamp_fusion
  139.7 2.3 %fusion.28 = bf16[1,4,64,1024]{3,2,1,0:T(8,128)(2,1)} fusion(bf16[1,4,64,1024]{3,2,1,0:T(8,128)(2,1)} %param.11, bf16[1,4,64,1024]{3,2,1,0:T(8,128)(2,1)} %param.12), kind=kLoop, calls=%fused_computation.34 | loop fusion | flops 2097152 | bytes 1572864 | tf_op jit(solution)/shard_map/convert_element_type | solution.py:43
  142.0 35.2 %reduce-scatter.2.cloned.1.call-done = bf16[768,256]{0,1:T(8,128)(2,1)} async-done(((bf16[6144,256]{0,1:T(8,128)(2,1)}), bf16[768,256]{0,1:T(8,128)(2,1)}) %reduce-scatter.2.cloned.1.call-update) | async-done | bytes 393232 | tf_op jit(solution)/shard_map/reduce_scatter | solution.py:67
  177.2 3.7 %all-to-all-start.1 = ((bf16[768,4,64]{0,2,1:T(8,128)(2,1)}), bf16[768,4,64]{0,2,1:T(8,128)(2,1)S(1)}, u32[]{:S(2)}, u32[]{:S(2)}) async-start(bf16[768,4,64]{0,2,1:T(8,128)(2,1)} %bitcast.96), calls=%async_computation.2 | async-start | bytes 786432 | tf_op jit(solution)/shard_map/all_to_all | solution.py:76
  180.9 7.7 %convert_bitcast_fusion = bf16[1,1024,6144]{2,1,0:T(8,128)(2,1)} fusion(bf16[256,1024]{1,0:T(8,128)(2,1)} %bitcast.95, bf16[256,6144]{1,0:T(8,128)(2,1)S(1)} %bitcast.92), kind=kOutput, calls=%fused_computation.9 | convolution fusion | flops 3227516928 | bytes 16252928 | tf_op jit(solution)/shard_map/dot_general | solution.py:51
  188.6 0.0 all-to-all-done.1
  188.6 0.1 bitcast_convert_fusion
  188.7 1.2 gather_fusion.1
  189.9 0.5 gather.15
  190.4 1.8 select_reduce_fusion
  (11 shorter events, 0.1 us)
Async XLA Ops:
  7.2 30.2 %all-gather.2.cloned.1.call-start = ((), (), s32[]{:S(2)}) async-start(), calls=%async_computation.3 | async-start | bytes 1769472 | tf_op jit(solution)/shard_map/all_gather | solution.py:44
  7.9 169.3 %reduce-scatter.2.cloned.1.call-start = ((), (), s32[]{:S(2)}) async-start(), calls=%async_computation.4 | async-start | bytes 3538944 | tf_op jit(solution)/shard_map/reduce_scatter | solution.py:67
  60.4 42.8 %copy-start = (bf16[1,4,64,1024]{3,2,1,0:T(8,128)(2,1)S(1)}, bf16[1,4,64,1024]{3,2,1,0:T(8,128)(2,1)}, u32[]{:S(2)}) copy-start(bf16[1,4,64,1024]{3,2,1,0:T(8,128)(2,1)} %param.11) | copy-start | bytes 1572868
  60.4 42.8 %copy-start.1 = (bf16[1,4,64,1024]{3,2,1,0:T(8,128)(2,1)S(1)}, bf16[1,4,64,1024]{3,2,1,0:T(8,128)(2,1)}, u32[]{:S(2)}) copy-start(bf16[1,4,64,1024]{3,2,1,0:T(8,128)(2,1)} %param.12) | copy-start | bytes 1572868
  127.0 11.9 %copy-start.2 = (s32[128,2]{0,1:T(2,128)S(1)}, s32[128,2]{0,1:T(2,128)}, u32[]{:S(2)}) copy-start(s32[128,2]{0,1:T(2,128)} %param.10) | copy-start | bytes 3076
  177.2 11.4 %all-to-all-start.1 = ((bf16[768,4,64]{0,2,1:T(8,128)(2,1)}), bf16[768,4,64]{0,2,1:T(8,128)(2,1)S(1)}, u32[]{:S(2)}, u32[]{:S(2)}) async-start(bf16[768,4,64]{0,2,1:T(8,128)(2,1)} %bitcast.96), calls=%async_computation.2 | async-start | bytes 786432 | tf_op jit(solution)/shard_map/all_to_all | solution.py:76
Sparse Core Ops, SparseCore 0:
  9.6 27.7 all-gather.1
  138.8 38.3 reduce-scatter.1
where the time goes:
time: 200 us; the launch traced here: 199 us
  waiting for transfers between devices  59.3 us (30%)
  matrix products  43.1 us (22%)
  blocking collectives  40.5 us (20%)
  local copies, waits for them, and re-layouts  25.5 us (13%)
  between operations  14.2 us (7%)
  other arithmetic  12.7 us (6%)
  starting transfers between devices  3.76 us (2%)
    all_to_all x1, blocking collectives, on_device(): lax.all_to_all(outgoing, 'expert', split_axis=0, concat_axis=0, tiled=True)  40.5 us
    reduce_scatter x1, waiting for transfers between devices, on_device(): lax.psum_scatter(lax.optimization_barrier(partial_value.astype(jnp.bfloat...  35.2 us
    all_gather x1, waiting for transfers between devices, on_device(): features = lax.all_gather(out_grad, 'cuts', axis=1, tiled=True)  23.3 us
    mul x3, local copies, waits for them, and re-layouts, pack_rows(): gate_values[:, :, None] * out_rows[:, None, :].astype(jnp.float32)  15.2 us
    dot_general x1, matrix products, on_device(): lax.dot_general(up_weight, up_grad, contract_last, preferred_element_type...  14.7 us
    dot_general x1, matrix products, on_device(): lax.dot_general(gate_weight, gate_grad, contract_last, preferred_element_...  11.6 us
    dot_general x1, matrix products, on_device(): lax.dot_general(routed, down_weight, contract_last, preferred_element_typ...  9.16 us
    dot_general x1, matrix products, on_device(): lax.dot_general(hidden_act, routed, contract_first, preferred_element_typ...  7.68 us
  transfers between devices with their start and end apart: 3, of which 2 were waited for; matrix products, arithmetic and copies ran while one was open for 9% of the time, Pallas kernels for 0%

commit v1 on v0

--- a/solution.py
+++ b/solution.py
@@ -1,7 +1,357 @@
+import functools
 import jax
 import jax.numpy as jnp
 from jax import lax
+from jax.experimental import pallas as pl
+from jax.experimental.pallas import tpu as pltpu
 from jax.sharding import PartitionSpec as P
+
+BF16 = jnp.bfloat16
+F32 = jnp.float32
+VMEM = pl.BlockSpec(memory_space=pltpu.VMEM)
+SMEM = pl.BlockSpec(memory_space=pltpu.SMEM)
+NT = (((1,), (1,)), ((), ()))
+TN = (((0,), (0,)), ((), ()))
+NN = (((1,), (0,)), ((), ()))
+MIB = 1 << 20
+
+
+def dot(a, b, dims):
+    return lax.dot_general(a, b, dims, preferred_element_type=F32)
+
+
+def cost(flops, bytes_accessed):
+    return pl.CostEstimate(flops=int(flops), bytes_accessed=int(bytes_accessed), transcendentals=0)
+
+
+def params(mib, axes=0):
+    return pltpu.CompilerParams(
+        vmem_limit_bytes=mib * MIB,
+        dimension_semantics=("arbitrary",) * axes if axes else None,
+    )
+
+
+def route(where, ids, probs, experts, capacity):
+    tokens = ids.shape[1]
+    lines = max(8, experts)
+    rows = experts * capacity
+
+    def kernel(where_ref, ids_ref, probs_ref, sel_ref, gate_ref):
+        me = where_ref[0]
+        expert = lax.broadcasted_iota(jnp.int32, (lines, tokens), 0) ^ me
+        first = (ids_ref[0:1, :] == expert).astype(F32)
+        second = (ids_ref[1:2, :] == expert).astype(F32)
+        hit = first + second
+        before = lax.broadcasted_iota(jnp.int32, (tokens, tokens), 0)
+        after = lax.broadcasted_iota(jnp.int32, (tokens, tokens), 1)
+        earlier = (before < after).astype(F32).astype(BF16)
+        place = dot(hit.astype(BF16), earlier, NN)
+        place = jnp.where(hit > 0.0, place, -1.0)
+        gate = first * probs_ref[0:1, :] + second * probs_ref[1:2, :]
+        slot = lax.broadcasted_iota(jnp.int32, (capacity, tokens), 0).astype(F32)
+        for r in range(experts):
+            match = place[r : r + 1, :] == slot
+            span = pl.ds(r * capacity, capacity)
+            sel_ref[span, :] = jnp.where(match, 1.0, 0.0).astype(BF16)
+            gate_ref[span, :] = jnp.sum(
+                jnp.where(match, gate[r : r + 1, :], 0.0), axis=1, keepdims=True
+            )
+
+    return pl.pallas_call(
+        kernel,
+        out_shape=(
+            jax.ShapeDtypeStruct((rows, tokens), BF16),
+            jax.ShapeDtypeStruct((rows, 1), F32),
+        ),
+        in_specs=[SMEM, VMEM, VMEM],
+        out_specs=(VMEM, VMEM),
+        cost_estimate=cost(1e6, 2e5),
+        name="route",
+    )(where, ids, probs)
+
+
+def pack(raws, sel, gate, experts, capacity):
+    blocks = len(raws)
+    columns = raws[0].shape[1]
+
+    def kernel(*refs):
+        raw_refs, (sel_ref, gate_ref), out_refs = (
+            refs[:blocks],
+            refs[blocks : blocks + 2],
+            refs[blocks + 2 :],
+        )
+        for b in range(blocks):
+            rows = (dot(sel_ref[...], raw_refs[b][...], NN) * gate_ref[...]).astype(BF16)
+            for r in range(experts):
+                out_refs[r][b] = rows[r * capacity : (r + 1) * capacity]
+
+    return pl.pallas_call(
+        kernel,
+        out_shape=[jax.ShapeDtypeStruct((blocks, capacity, columns), BF16)] * experts,
+        in_specs=[VMEM] * (blocks + 2),
+        out_specs=[VMEM] * experts,
+        compiler_params=params(32),
+        cost_estimate=cost(
+            2 * blocks * sel.shape[0] * sel.shape[1] * columns, 4e5 * blocks
+        ),
+        name="pack",
+    )(*raws, sel, gate)
+
+
+def activations(where, gate_pre, up_pre):
+    _, groups, capacity, units = gate_pre.shape
+    rows = groups * capacity
+    tile = 256
+
+    def kernel(where_ref, gate_ref, up_ref, up_factor, gate_factor, act):
+        me = where_ref[0]
+        for r in range(groups):
+            a = gate_ref[0, me ^ r].astype(F32)
+            b = up_ref[0, me ^ r].astype(F32)
+            sig = 1.0 / (1.0 + jnp.exp(-a))
+            span = pl.ds(r * capacity, capacity)
+            swish = a * sig
+            up_factor[span, :] = swish
+            gate_factor[span, :] = b * sig * (1.0 + a * (1.0 - sig))
+            act[span, :] = (swish * b).astype(BF16)
+
+    spec = pl.BlockSpec((1, groups, capacity, tile), lambda i, w: (0, 0, 0, i))
+    out = pl.BlockSpec((rows, tile), lambda i, w: (0, i))
+    return pl.pallas_call(
+        kernel,
+        out_shape=(
+            jax.ShapeDtypeStruct((rows, units), F32),
+            jax.ShapeDtypeStruct((rows, units), F32),
+            jax.ShapeDtypeStruct((rows, units), BF16),
+        ),
+        grid_spec=pltpu.PrefetchScalarGridSpec(
+            num_scalar_prefetch=1,
+            grid=(units // tile,),
+            in_specs=[spec, spec],
+            out_specs=(out, out, out),
+        ),
+        compiler_params=params(24, 1),
+        cost_estimate=cost(1e7, 14 * rows * units),
+        name="activations",
+    )(where, gate_pre, up_pre)
+
+
+def block_of(where, shift, line, sibling):
+    cut = where[1]
+    z = lax.rem(lax.div(cut, 2) + (shift + line), line)
+    core = lax.rem(cut, 2)
+    return z * 2 + (1 - core if sibling else core)
+
+
+def pick(step, values):
+    result = jnp.int32(values[0])
+    for i, value in enumerate(values[1:], 1):
+        result = jnp.where(step == i, jnp.int32(value), result)
+    return result
+
+
+def hidden_part(where, x, w_down, shifts, line, sibling, total, factors):
+    blocks, rows, columns = x.shape
+    units = w_down.shape[1]
+    tile = 256
+    tiles = units // tile
+    has_total = total is not None
+    last = factors is not None
+
+    def kernel(where_ref, *refs):
+        refs = list(refs)
+        x_ref, w_ref = refs.pop(0), refs.pop(0)
+        total_ref = refs.pop(0) if has_total else None
+        factor_refs = (refs.pop(0), refs.pop(0)) if last else None
+        b, i = pl.program_id(0), pl.program_id(1)
+        acc = refs[-1]
+        span = pl.ds(pl.multiple_of(i * tile, tile), tile)
+        value = dot(x_ref[0], w_ref[0], NT)
+
+        def finish(value):
+            if not last:
+                acc[:, span] = value
+                return
+            if blocks > 1:
+                acc[:, span] = value
+
+            @pl.when(b == blocks - 1)
+            def _():
+                refs[0][:, span] = (value * factor_refs[0][:, span]).astype(BF16)
+                refs[1][:, span] = (value * factor_refs[1][:, span]).astype(BF16)
+
+        @pl.when(b == 0)
+        def _():
+            finish(value + total_ref[:, span] if has_total else value)
+
+        if blocks > 1:
+
+            @pl.when(b > 0)
+            def _():
+                finish(acc[:, span] + value)
+
+    whole = pl.BlockSpec((rows, units), lambda b, i, w: (0, 0))
+    in_specs = [
+        pl.BlockSpec((1, rows, columns), lambda b, i, w: (b, 0, 0)),
+        pl.BlockSpec(
+            (1, tile, columns),
+            lambda b, i, w: (0, i, block_of(w, pick(b, [-s for s in shifts]), line, sibling)),
+        ),
+    ]
+    operands = [x, w_down]
+    if has_total:
+        in_specs.append(whole)
+        operands.append(total)
+    scratch = []
+    if last:
+        in_specs += [whole, whole]
+        operands += list(factors)
+        out_shape = [jax.ShapeDtypeStruct((rows, units), BF16)] * 2
+        out_specs = [whole, whole]
+        scratch = [pltpu.VMEM((rows, units), F32)]
+    else:
+        out_shape = jax.ShapeDtypeStruct((rows, units), F32)
+        out_specs = whole
+    return pl.pallas_call(
+        kernel,
+        out_shape=out_shape,
+        grid_spec=pltpu.PrefetchScalarGridSpec(
+            num_scalar_prefetch=1,
+            grid=(blocks, tiles),
+            in_specs=in_specs,
+            out_specs=out_specs,
+            scratch_shapes=scratch,
+        ),
+        compiler_params=params(32, 2),
+        cost_estimate=cost(
+            2 * blocks * rows * columns * units, 2 * blocks * columns * units + 8 * rows * units
+        ),
+        name="hidden_part",
+    )(where, *operands)
+
+
+def down_part(where, act, mine, theirs, shifts, line, before, out_shape):
+    blocks, rows, columns = mine.shape
+    units = act.shape[1]
+
+    def kernel(where_ref, act_ref, mine_ref, theirs_ref, *refs):
+        out_ref = refs[-1]
+        i = pl.program_id(0)
+
+        @pl.when(i < blocks)
+        def _():
+            out_ref[0] = dot(act_ref[...], mine_ref[0], TN).astype(BF16)
+
+        @pl.when(i >= blocks)
+        def _():
+            out_ref[0] = dot(act_ref[...], theirs_ref[0], TN).astype(BF16)
+
+    def out_map(i, w):
+        shift = pick(lax.rem(i, blocks), [-s for s in shifts])
+        own = block_of(w, shift, line, False)
+        other = block_of(w, shift, line, True)
+        return (0, 0, jnp.where(i < blocks, own, other))
+
+    in_specs = [
+        pl.BlockSpec((rows, units), lambda i, w: (0, 0)),
+        pl.BlockSpec((1, rows, columns), lambda i, w: (jnp.minimum(i, blocks - 1), 0, 0)),
+        pl.BlockSpec((1, rows, columns), lambda i, w: (jnp.maximum(i - blocks, 0), 0, 0)),
+    ]
+    operands = [act, mine, theirs]
+    if before is not None:
+        in_specs.append(pl.BlockSpec(memory_space=pl.ANY))
+        operands.append(before)
+    return pl.pallas_call(
+        kernel,
+        out_shape=jax.ShapeDtypeStruct(out_shape, BF16),
+        grid_spec=pltpu.PrefetchScalarGridSpec(
+            num_scalar_prefetch=1,
+            grid=(2 * blocks,),
+            in_specs=in_specs,
+            out_specs=pl.BlockSpec((1, units, columns), out_map),
+        ),
+        input_output_aliases={} if before is None else {4: 0},
+        compiler_params=params(24, 1),
+        cost_estimate=cost(4 * blocks * rows * columns * units, 4 * blocks * columns * units),
+        name="down_part",
+    )(where, *operands)
+
+
+def slot_part(where, gate_grad, up_grad, w_gate, w_up, shifts, line, sibling, arrived, experts):
+    rows, units = gate_grad.shape
+    blocks = len(shifts)
+    columns = w_gate.shape[1] // (2 * line)
+    tile = 256
+    capacity = rows // experts
+
+    def kernel(where_ref, gate_ref, up_ref, wg_ref, wu_ref, *refs):
+        value = dot(gate_ref[...], wg_ref[0], NT) + dot(up_ref[...], wu_ref[0], NT)
+        if arrived is None:
+            refs[0][0] = value.astype(BF16)
+        else:
+            value = (value + refs[0][0].astype(F32)).astype(BF16)
+            for r in range(experts):
+                refs[1 + r][0] = value[r * capacity : (r + 1) * capacity]
+
+    tiles = columns // tile
+    whole = pl.BlockSpec((rows, units), lambda b, i, w: (0, 0))
+    weight = pl.BlockSpec(
+        (1, tile, units),
+        lambda b, i, w: (0, block_of(w, pick(b, shifts), line, sibling) * tiles + i, 0),
+    )
+    part = pl.BlockSpec((1, rows, tile), lambda b, i, w: (b, 0, i))
+    in_specs = [whole, whole, weight, weight]
+    operands = [gate_grad, up_grad, w_gate, w_up]
+    if arrived is None:
+        out_shape = jax.ShapeDtypeStruct((blocks, rows, columns), BF16)
+        out_specs = part
+    else:
+        in_specs.append(part)
+        operands.append(arrived)
+        out_shape = [jax.ShapeDtypeStruct((blocks, capacity, columns), BF16)] * experts
+        out_specs = [pl.BlockSpec((1, capacity, tile), lambda b, i, w: (b, 0, i))] * experts
+    return pl.pallas_call(
+        kernel,
+        out_shape=out_shape,
+        grid_spec=pltpu.PrefetchScalarGridSpec(
+            num_scalar_prefetch=1, grid=(blocks, tiles), in_specs=in_specs, out_specs=out_specs
+        ),
+        compiler_params=params(24, 2),
+        cost_estimate=cost(
+            4 * blocks * rows * columns * units, 4 * blocks * columns * units + 4 * rows * units
+        ),
+        name="slot_part",
+    )(where, *operands)
+
+
+def combine(pieces, sel, others):
+    experts = len(pieces)
+    blocks, capacity, columns = pieces[0].shape
+    tokens = sel.shape[1]
+    count = len(others)
+
+    def kernel(*refs):
+        piece_refs, sel_ref = refs[:experts], refs[experts]
+        other_refs = refs[experts + 1 : experts + 1 + count]
+        out_refs = refs[experts + 1 + count :]
+        for b in range(blocks):
+            rows = jnp.concatenate([piece[b] for piece in piece_refs], axis=0)
+            value = dot(sel_ref[...], rows, TN)
+            for other in other_refs:
+                value = value + other[...].astype(F32)
+            out_refs[b][...] = value.astype(BF16)
+
+    return pl.pallas_call(
+        kernel,
+        out_shape=[jax.ShapeDtypeStruct((tokens, columns), BF16)] * blocks,
+        in_specs=[VMEM] * (experts + 1 + count),
+        out_specs=[VMEM] * blocks,
+        compiler_params=params(32),
+        cost_estimate=cost(
+            2 * blocks * experts * capacity * tokens * columns, 6e5 * blocks + 2e5 * count
+        ),
+        name="combine",
+    )(*pieces, sel, *others)
 
 
 def slot_tables(routing, experts, capacity):
@@ -25,7 +375,7 @@
     return jnp.take(weighted, source, axis=0).reshape(experts, capacity, columns)
 
 
-def on_device(out_grad, gate_probs, expert_ids, gate_pre, up_pre, w_gate, w_up, w_down):
+def on_any_tiling(out_grad, gate_probs, expert_ids, gate_pre, up_pre, w_gate, w_up, w_down):
     tokens_here = expert_ids.shape[0]
     experts = lax.axis_size("expert") * w_gate.shape[0]
     groups = gate_pre.shape[1]
@@ -82,6 +432,68 @@
     return (input_grad.T.astype(jnp.bfloat16), w_down_grad)
 
 
+def on_device(out_grad, gate_probs, expert_ids, gate_pre, up_pre, w_gate, w_up, w_down):
+    experts = lax.axis_size("expert")
+    cuts = lax.axis_size("cuts")
+    line = cuts // 2
+    capacity = gate_pre.shape[2]
+    if out_grad.shape[1] % 256 or gate_pre.shape[3] % 256 or capacity % 16 or cuts % 2:
+        return on_any_tiling(
+            out_grad, gate_probs, expert_ids, gate_pre, up_pre, w_gate, w_up, w_down
+        )
+    where = jnp.stack([lax.axis_index("expert"), lax.axis_index("cuts")]).astype(jnp.int32)
+    groups = [g for g in ([0], sorted({1, line - 1}), list(range(2, line - 1))) if g]
+
+    def along(x, shift):
+        pairs = [(i, (i + 2 * shift) % cuts) for i in range(cuts)]
+        return lax.ppermute(x, "cuts", pairs)
+
+    def swap(x):
+        return lax.ppermute(x, "cuts", [(i, i ^ 1) for i in range(cuts)])
+
+    def exchange(pieces):
+        moved = [
+            lax.ppermute(pieces[r], "expert", [(i, i ^ r) for i in range(experts)])
+            for r in range(1, experts)
+        ]
+        return [pieces[0]] + moved
+
+    sel, gate = route(where, expert_ids.T, gate_probs.T, experts, capacity)
+    up_factor, gate_factor, act = activations(where, gate_pre, up_pre)
+    total = None
+    routed = []
+    for group in groups:
+        raws = [along(out_grad, shift) if shift else out_grad for shift in group]
+        pieces = exchange(pack(raws, sel, gate, experts, capacity))
+        mine = jnp.concatenate(pieces, axis=1)
+        theirs = swap(mine)
+        routed.append((mine, theirs))
+        total = hidden_part(where, mine, w_down, group, line, False, total, None)
+        last = group is groups[-1]
+        total = hidden_part(
+            where, theirs, w_down, group, line, True, total,
+            (gate_factor, up_factor) if last else None,
+        )
+    gate_grad, up_grad = total
+
+    order = groups[::-1]
+    back = functools.partial(slot_part, where, gate_grad, up_grad, w_gate, w_up)
+    arrived = [swap(back(group, line, True, None, experts)) for group in order]
+    landed = []
+    result = None
+    for group, other in zip(order, arrived):
+        pieces = exchange(back(group, line, False, other, experts))
+        if group != [0]:
+            for shift, part in zip(group, combine(pieces, sel, [])):
+                landed.append(along(part, shift))
+        else:
+            result = combine(pieces, sel, landed)[0]
+    down = None
+    for group, (mine, theirs) in zip(groups, routed):
+        down = down_part(where, act, mine, theirs, group, line, down, w_down.shape)
+    return result, down
+
+
 def solution(mesh):
     return jax.shard_map(
         on_device,

time: 200 us -> 138 us (0.69)
  Pallas kernels: 0 us -> 47.6 us
  matrix products: 43.1 us -> 0 us
  blocking collectives: 40.5 us -> 0 us
  starting transfers between devices: 3.76 us -> 41.2 us
  waiting for transfers between devices: 59.3 us -> 22.4 us
  between operations: 14.2 us -> 1.06 us
  other arithmetic: 12.7 us -> 0.58 us
    pallas_call x0 -> x23, Pallas kernels: none -> 47.6 us  [the longest x6 15.8 us: slot_part(): pl.pallas_call(kernel, out_shape=out_shape, grid_spec=pltpu.PrefetchScala...]
    dot_general x4 -> x0, matrix products: 43.1 us -> none  [the longest x1 14.7 us: on_device(): lax.dot_general(up_weight, up_grad, contract_last, preferred_element_type...]
    ppermute x0 -> x30, starting transfers between devices: none -> 41.2 us  [the longest x18 23.4 us: exchange(): lax.ppermute(pieces[r], 'expert', [(i, i ^ r) for i in range(experts)])]
    all_to_all x1 -> x0, blocking collectives: 40.5 us -> none  [on_device(): lax.all_to_all(outgoing, 'expert', split_axis=0, concat_axis=0, tiled=True)]
    reduce_scatter x1 -> x0, waiting for transfers between devices: 35.2 us -> none  [on_device(): lax.psum_scatter(lax.optimization_barrier(partial_value.astype(jnp.bfloat...]
    all_gather x1 -> x0, waiting for transfers between devices: 23.3 us -> none  [on_device(): features = lax.all_gather(out_grad, 'cuts', axis=1, tiled=True)]
    unnamed x8 -> x55, local copies, waits for them, and re-layouts: 1.58 us -> 24.4 us
    ppermute x0 -> x30, waiting for transfers between devices: none -> 22.4 us  [the longest x18 20.6 us: exchange(): lax.ppermute(pieces[r], 'expert', [(i, i ^ r) for i in range(experts)])]
  transfers between devices with their start and end apart: 3 -> 30, of which waited for: 2 -> 7; matrix products, arithmetic and copies ran while one was open for 9% -> 1% of each run, Pallas kernels for 0% -> 30%
where the time goes in v1:
time: 138 us; the launch traced here: 137 us
  Pallas kernels  47.6 us (34%)
  starting transfers between devices  41.2 us (30%)
  local copies, waits for them, and re-layouts  24.5 us (18%)
  waiting for transfers between devices  22.4 us (16%)
    unnamed x55, local copies, waits for them, and re-layouts  24.4 us
    ppermute x18, starting transfers between devices, exchange(): lax.ppermute(pieces[r], 'expert', [(i, i ^ r) for i in range(experts)])  23.4 us
    ppermute x18, waiting for transfers between devices, exchange(): lax.ppermute(pieces[r], 'expert', [(i, i ^ r) for i in range(experts)])  20.6 us
    ppermute x6, starting transfers between devices, along(): return lax.ppermute(x, 'cuts', pairs)  16 us
    pallas_call x6, Pallas kernels, slot_part(): pl.pallas_call(kernel, out_shape=out_shape, grid_spec=pltpu.PrefetchScala...  15.8 us
    pallas_call x6, Pallas kernels, hidden_part(): pl.pallas_call(kernel, out_shape=out_shape, grid_spec=pltpu.PrefetchScala...  15.5 us
    pallas_call x3, Pallas kernels, down_part(): pl.pallas_call(kernel, out_shape=jax.ShapeDtypeStruct(out_shape, BF16), g...  10.9 us
  transfers between devices with their start and end apart: 30, of which 7 were waited for; matrix products, arithmetic and copies ran while one was open for 1% of the time, Pallas kernels for 30%

profile of v1, /device:TPU:0, one launch (start us, length us, event | category | flops | bytes accessed | tf_op | source)
XLA Modules:
  0.0 137.3 jit_solution(6719062845755618060)
XLA Ops:
  0.6 3.1 %collective-permute-start.5 = (bf16[128,768]{1,0:T(8,128)(2,1)}, bf16[128,768]{1,0:T(8,128)(2,1)S(1)}, u32[]{:S(2)}, u32[]{:S(2)}) collective-permute-start(bf16[128,768]{1,0:T(8,128)(2,1)} %refs_0_.1), channel_id=1, source_target_pairs={{0,2},{1,3},{2,4},{3,5},{4,6},{5,7},{6,0},{7,1},{8,10},{9,11},{10,... | collective-permute-start | bytes 589832 | tf_op jit(solution)/shard_map/ppermute | solution.py:449
  3.7 2.6 %collective-permute-start = (bf16[128,768]{1,0:T(8,128)(2,1)}, bf16[128,768]{1,0:T(8,128)(2,1)S(1)}, u32[]{:S(2)}, u32[]{:S(2)}) collective-permute-start(bf16[128,768]{1,0:T(8,128)(2,1)} %refs_0_.1), channel_id=1, source_target_pairs={{0,4},{1,5},{2,6},{3,7},{4,0},{5,1},{6,2},{7,3},{8,12},{9,13},{10,... | collective-permute-start | bytes 589832 | tf_op jit(solution)/shard_map/ppermute | solution.py:449
  6.3 1.3 collective-permute-start.6
  8.2 1.6 %route.1 = (bf16[256,128]{1,0:T(8,128)(2,1)}, f32[256,1]{1,0:T(8,128)}) custom-call(s32[2]{0:T(128)} %pad_add_fusion.where_ref, s32[2,128]{1,0:T(2,128)} %bitcast.4, f32[2,128]{1,0:T(2,128)} %bitcast.5), custom_call_target="tpu_custom_call" | custom-call | flops 1000000 | bytes 200000 | tf_op jit(solution)/shard_map/route/pallas_call | solution.py:60
  12.7 1.6 %collective-permute-start.11 = (bf16[1,64,768]{2,1,0:T(8,128)(2,1)S(1)}, bf16[1,64,768]{2,1,0:T(8,128)(2,1)S(1)}, u32[]{:S(2)}, u32[]{:S(2)}) collective-permute-start(bf16[1,64,768]{2,1,0:T(8,128)(2,1)S(1)} %get-tuple-element.46), channel_id=1, source_target_pairs={{0,8},{8,0},{16,24},{24,16},{1,9},{9,1},{17,25},{25,17},{2,10},{10... | collective-permute-start | bytes 294920 | tf_op jit(solution)/shard_map/ppermute | solution.py:456
  14.3 1.5 %collective-permute-start.12 = (bf16[1,64,768]{2,1,0:T(8,128)(2,1)S(1)}, bf16[1,64,768]{2,1,0:T(8,128)(2,1)S(1)}, u32[]{:S(2)}, u32[]{:S(2)}) collective-permute-start(bf16[1,64,768]{2,1,0:T(8,128)(2,1)S(1)} %get-tuple-element.47), channel_id=1, source_target_pairs={{0,16},{8,24},{16,0},{24,8},{1,17},{9,25},{17,1},{25,9},{2,18},{10... | collective-permute-start | bytes 294920 | tf_op jit(solution)/shard_map/ppermute | solution.py:456
  15.8 1.6 %collective-permute-done.11 = bf16[1,64,768]{2,1,0:T(8,128)(2,1)S(1)} collective-permute-done((bf16[1,64,768]{2,1,0:T(8,128)(2,1)S(1)}, bf16[1,64,768]{2,1,0:T(8,128)(2,1)S(1)}, u32[]{:S(2)}, u32[]{:S(2)}) %collective-permute-start.11) | collective-permute-done | bytes 98336 | tf_op jit(solution)/shard_map/ppermute | solution.py:456
  17.4 2.5 %collective-permute-start.13 = (bf16[1,64,768]{2,1,0:T(8,128)(2,1)S(1)}, bf16[1,64,768]{2,1,0:T(8,128)(2,1)S(1)}, u32[]{:S(2)}, u32[]{:S(2)}) collective-permute-start(bf16[1,64,768]{2,1,0:T(8,128)(2,1)S(1)} %get-tuple-element.48), channel_id=1, source_target_pairs={{0,24},{8,16},{16,8},{24,0},{1,25},{9,17},{17,9},{25,1},{2,26},{10... | collective-permute-start | bytes 294920 | tf_op jit(solution)/shard_map/ppermute | solution.py:456
  21.4 2.5 %collective-permute-start.9 = (bf16[2,64,768]{2,1,0:T(8,128)(2,1)S(1)}, bf16[2,64,768]{2,1,0:T(8,128)(2,1)S(1)}, u32[]{:S(2)}, u32[]{:S(2)}) collective-permute-start(bf16[2,64,768]{2,1,0:T(8,128)(2,1)S(1)} %get-tuple-element.44), channel_id=1, source_target_pairs={{0,24},{8,16},{16,8},{24,0},{1,25},{9,17},{17,9},{25,1},{2,26},{10... | collective-permute-start | bytes 589832 | tf_op jit(solution)/shard_map/ppermute | solution.py:456
  23.9 4.2 %collective-permute-done.7 = bf16[2,64,768]{2,1,0:T(8,128)(2,1)S(1)} collective-permute-done((bf16[2,64,768]{2,1,0:T(8,128)(2,1)S(1)}, bf16[2,64,768]{2,1,0:T(8,128)(2,1)S(1)}, u32[]{:S(2)}, u32[]{:S(2)}) %collective-permute-start.7) | collective-permute-done | bytes 196640 | tf_op jit(solution)/shard_map/ppermute | solution.py:456
  28.2 2.4 %collective-permute-done.8 = bf16[2,64,768]{2,1,0:T(8,128)(2,1)S(1)} collective-permute-done((bf16[2,64,768]{2,1,0:T(8,128)(2,1)S(1)}, bf16[2,64,768]{2,1,0:T(8,128)(2,1)S(1)}, u32[]{:S(2)}, u32[]{:S(2)}) %collective-permute-start.8) | collective-permute-done | bytes 196640 | tf_op jit(solution)/shard_map/ppermute | solution.py:456
  31.6 1.6 %collective-permute-start.1 = (bf16[1,64,768]{2,1,0:T(8,128)(2,1)S(1)}, bf16[1,64,768]{2,1,0:T(8,128)(2,1)S(1)}, u32[]{:S(2)}, u32[]{:S(2)}) collective-permute-start(bf16[1,64,768]{2,1,0:T(8,128)(2,1)S(1)} %get-tuple-element.38), channel_id=1, source_target_pairs={{0,8},{8,0},{16,24},{24,16},{1,9},{9,1},{17,25},{25,17},{2,10},{10... | collective-permute-start | bytes 294920 | tf_op jit(solution)/shard_map/ppermute | solution.py:456
  33.6 1.5 %collective-permute-start.3 = (bf16[1,64,768]{2,1,0:T(8,128)(2,1)S(1)}, bf16[1,64,768]{2,1,0:T(8,128)(2,1)S(1)}, u32[]{:S(2)}, u32[]{:S(2)}) collective-permute-start(bf16[1,64,768]{2,1,0:T(8,128)(2,1)S(1)} %get-tuple-element.40), channel_id=1, source_target_pairs={{0,24},{8,16},{16,8},{24,0},{1,25},{9,17},{17,9},{25,1},{2,26},{10... | collective-permute-start | bytes 294920 | tf_op jit(solution)/shard_map/ppermute | solution.py:456
  35.1 1.2 collective-permute-done.1
  36.4 3.4 %collective-permute-done.2 = bf16[1,64,768]{2,1,0:T(8,128)(2,1)S(1)} collective-permute-done((bf16[1,64,768]{2,1,0:T(8,128)(2,1)S(1)}, bf16[1,64,768]{2,1,0:T(8,128)(2,1)S(1)}, u32[]{:S(2)}, u32[]{:S(2)}) %collective-permute-start.2) | collective-permute-done | bytes 98336 | tf_op jit(solution)/shard_map/ppermute | solution.py:456
  39.9 1.1 copy-done.17
  41.0 1.0 copy-done.18
  42.6 1.5 %activations.1 = (f32[256,1024]{1,0:T(8,128)S(1)}, f32[256,1024]{1,0:T(8,128)S(1)}, bf16[256,1024]{1,0:T(8,128)(2,1)S(1)}) custom-call(s32[2]{0:T(128)S(1)} %copy-done.20, bf16[1,4,64,1024]{3,2,1,0:T(8,128)(2,1)S(1)} %copy-done.17, bf16[1,4,64,1024]{3,2,1,0:T(8,128)(2,1)S(1)} %copy-done.18), custom_call_target="tpu_custom_call" | custom-call | flops 10000000 | bytes 3670016 | tf_op jit(solution)/shard_map/activations/pallas_call | solution.py:120
  44.2 1.0 copy-done.13
  46.2 4.6 %copy-done = bf16[1,1024,6144]{2,1,0:T(8,128)(2,1)S(1)} copy-done((bf16[1,1024,6144]{2,1,0:T(8,128)(2,1)S(1)}, bf16[1,1024,6144]{2,1,0:T(8,128)(2,1)}, u32[]{:S(2)}) %copy-start) | copy-done | bytes 12582936
  51.3 2.0 %hidden_part.6.refs_2_ = f32[256,1024]{1,0:T(8,128)S(1)} custom-call(s32[2]{0:T(128)S(1)} %copy-done.21, bf16[1,256,768]{2,1,0:T(8,128)(2,1)S(1)} %constant_dynamic-update-slice_fusion.8.refs_0_.mine_ref, bf16[1,1024,6144]{2,1,0:T(8,128)(2,1)S(1)} %copy-done), custom_call_target="tpu_custom_call" | custom-call | flops 402653184 | bytes 3670016 | tf_op jit(solution)/shard_map/hidden_part/pallas_call | solution.py:215
  53.3 2.6 %copy-done.1 = bf16[1,1024,6144]{2,1,0:T(8,128)(2,1)S(1)} copy-done((bf16[1,1024,6144]{2,1,0:T(8,128)(2,1)S(1)}, bf16[1,1024,6144]{2,1,0:T(8,128)(2,1)}, u32[]{:S(2)}) %copy-start.1) | copy-done | bytes 12582936
  55.9 2.0 %hidden_part.7.refs_2_ = f32[256,1024]{1,0:T(8,128)S(1)} custom-call(s32[2]{0:T(128)S(1)} %copy-done.21, bf16[1,256,768]{2,1,0:T(8,128)(2,1)S(1)} %collective-permute-done.14.refs_0_.theirs_ref, bf16[1,1024,6144]{2,1,0:T(8,128)(2,1)S(1)} %copy-done.1, f32[256,1024]{1,0:T(8,128)S(1)} %hidden_part.6.refs_2_), custom_call_target="tpu_custom_call" | custom-call | flops 402653184 | bytes 3670016 | tf_op jit(solution)/shard_map/hidden_part/pallas_call | solution.py:215
  57.9 3.7 %hidden_part.8.refs_2_ = f32[256,1024]{1,0:T(8,128)S(1)} custom-call(s32[2]{0:T(128)S(1)} %copy-done.21, bf16[2,256,768]{2,1,0:T(8,128)(2,1)S(1)} %constant_dynamic-update-slice_fusion.4.refs_0_.mine_ref, bf16[1,1024,6144]{2,1,0:T(8,128)(2,1)S(1)} %copy-done.1, f32[256,1024]{1,0:T(8,128)S(1)} %hidden_part.7.refs_2_), custom_call_target="tpu_custom_call" | custom-call | flops 805306368 | bytes 5242880 | tf_op jit(solution)/shard_map/hidden_part/pallas_call | solution.py:215
  61.7 3.7 %hidden_part.9.refs_2_ = f32[256,1024]{1,0:T(8,128)S(1)} custom-call(s32[2]{0:T(128)S(1)} %copy-done.21, bf16[2,256,768]{2,1,0:T(8,128)(2,1)S(1)} %collective-permute-done.10.refs_0_.theirs_ref, bf16[1,1024,6144]{2,1,0:T(8,128)(2,1)S(1)} %copy-done.1, f32[256,1024]{1,0:T(8,128)S(1)} %hidden_part.8.refs_2_), custom_call_target="tpu_custom_call" | custom-call | flops 805306368 | bytes 5242880 | tf_op jit(solution)/shard_map/hidden_part/pallas_call | solution.py:215
  65.5 2.0 %hidden_part.10.refs_2_ = f32[256,1024]{1,0:T(8,128)S(1)} custom-call(s32[2]{0:T(128)S(1)} %copy-done.21, bf16[1,256,768]{2,1,0:T(8,128)(2,1)S(1)} %constant_dynamic-update-slice_fusion.refs_0_.mine_ref, bf16[1,1024,6144]{2,1,0:T(8,128)(2,1)S(1)} %copy-done.1, f32[256,1024]{1,0:T(8,128)S(1)} %hidden_part.9.refs_2_), custom_call_target="tpu_custom_call" | custom-call | flops 402653184 | bytes 3670016 | tf_op jit(solution)/shard_map/hidden_part/pallas_call | solution.py:215
  67.5 2.1 %hidden_part.11 = (bf16[256,1024]{1,0:T(8,128)(2,1)S(1)}, bf16[256,1024]{1,0:T(8,128)(2,1)S(1)}) custom-call(s32[2]{0:T(128)S(1)} %copy-done.21, bf16[1,256,768]{2,1,0:T(8,128)(2,1)S(1)} %collective-permute-done.4.refs_0_.theirs_ref, bf16[1,1024,6144]{2,1,0:T(8,128)(2,1)S(1)} %copy-done.1, f32[256,1024]{1,0:T(8,128)S(1)} %hidden_part.10.refs_2_, ...), custom_call_target="tpu_custom_call" | custom-call | flops 402653184 | bytes 3670016 | tf_op jit(solution)/shard_map/hidden_part/pallas_call | solution.py:215
  69.6 4.6 %copy-done.2 = bf16[1,6144,1024]{2,1,0:T(8,128)(2,1)S(1)} copy-done((bf16[1,6144,1024]{2,1,0:T(8,128)(2,1)S(1)}, bf16[1,6144,1024]{2,1,0:T(8,128)(2,1)}, u32[]{:S(2)}) %copy-start.2) | copy-done | bytes 12582936
  74.2 4.6 %copy-done.3 = bf16[1,6144,1024]{2,1,0:T(8,128)(2,1)S(1)} copy-done((bf16[1,6144,1024]{2,1,0:T(8,128)(2,1)S(1)}, bf16[1,6144,1024]{2,1,0:T(8,128)(2,1)}, u32[]{:S(2)}) %copy-start.3) | copy-done | bytes 12582936
  78.7 3.6 %slot_part.10 = bf16[2,256,768]{2,1,0:T(8,128)(2,1)S(1)} custom-call(s32[2]{0:T(128)S(1)} %copy-done.22, bf16[256,1024]{1,0:T(8,128)(2,1)S(1)} %get-tuple-element.51.gate_ref, bf16[256,1024]{1,0:T(8,128)(2,1)S(1)} %get-tuple-element.52.up_ref, bf16[1,6144,1024]{2,1,0:T(8,128)(2,1)S(1)} %copy-done.2, bf16[1,6144,1024]{2,1,0:T(8,128)(2,1)S(1)} %copy-done.3), custom_call_target="tpu_custom_call" | custom-call | flops 1610612736 | bytes 7340032 | tf_op jit(solution)/shard_map/slot_part/pallas_call | solution.py:313
  82.8 2.1 %slot_part.8 = bf16[1,256,768]{2,1,0:T(8,128)(2,1)S(1)} custom-call(s32[2]{0:T(128)S(1)} %copy-done.22, bf16[256,1024]{1,0:T(8,128)(2,1)S(1)} %get-tuple-element.51.gate_ref, bf16[256,1024]{1,0:T(8,128)(2,1)S(1)} %get-tuple-element.52.up_ref, bf16[1,6144,1024]{2,1,0:T(8,128)(2,1)S(1)} %copy-done.2, bf16[1,6144,1024]{2,1,0:T(8,128)(2,1)S(1)} %copy-done.3), custom_call_target="tpu_custom_call" | custom-call | flops 805306368 | bytes 4194304 | tf_op jit(solution)/shard_map/slot_part/pallas_call | solution.py:313
  85.1 2.1 %slot_part.6 = bf16[1,256,768]{2,1,0:T(8,128)(2,1)S(1)} custom-call(s32[2]{0:T(128)S(1)} %copy-done.22, bf16[256,1024]{1,0:T(8,128)(2,1)S(1)} %get-tuple-element.51.gate_ref, bf16[256,1024]{1,0:T(8,128)(2,1)S(1)} %get-tuple-element.52.up_ref, bf16[1,6144,1024]{2,1,0:T(8,128)(2,1)S(1)} %copy-done.2, bf16[1,6144,1024]{2,1,0:T(8,128)(2,1)S(1)} %copy-done.3), custom_call_target="tpu_custom_call" | custom-call | flops 805306368 | bytes 4194304 | tf_op jit(solution)/shard_map/slot_part/pallas_call | solution.py:313
  87.6 2.1 %slot_part.9 = (bf16[1,64,768]{2,1,0:T(8,128)(2,1)S(1)}, bf16[1,64,768]{2,1,0:T(8,128)(2,1)S(1)}, bf16[1,64,768]{2,1,0:T(8,128)(2,1)S(1)}, bf16[1,64,768]{2,1,0:T(8,128)(2,1)S(1)}) custom-call(s32[2]{0:T(128)S(1)} %copy-done.22, bf16[256,1024]{1,0:T(8,128)(2,1)S(1)} %get-tuple-element.51.gate_ref, bf16[256,1024]{1,0:T(8,128)(2,1)S(1)} %get-tuple-element.52.up_ref, ...), custom_call_target="tpu_custom_call" | custom-call | flops 805306368 | bytes 4194304 | tf_op jit(solution)/shard_map/slot_part/pallas_call | solution.py:313
  90.4 3.8 %slot_part.11 = (bf16[2,64,768]{2,1,0:T(8,128)(2,1)S(1)}, bf16[2,64,768]{2,1,0:T(8,128)(2,1)S(1)}, bf16[2,64,768]{2,1,0:T(8,128)(2,1)S(1)}, bf16[2,64,768]{2,1,0:T(8,128)(2,1)S(1)}) custom-call(s32[2]{0:T(128)S(1)} %copy-done.22, bf16[256,1024]{1,0:T(8,128)(2,1)S(1)} %get-tuple-element.51.gate_ref, bf16[256,1024]{1,0:T(8,128)(2,1)S(1)} %get-tuple-element.52.up_ref, ...), custom_call_target="tpu_custom_call" | custom-call | flops 1610612736 | bytes 7340032 | tf_op jit(solution)/shard_map/slot_part/pallas_call | solution.py:313
  94.2 1.5 %collective-permute-start.25 = (bf16[2,64,768]{2,1,0:T(8,128)(2,1)S(1)}, bf16[2,64,768]{2,1,0:T(8,128)(2,1)S(1)}, u32[]{:S(2)}, u32[]{:S(2)}) collective-permute-start(bf16[2,64,768]{2,1,0:T(8,128)(2,1)S(1)} %get-tuple-element.62), channel_id=1, source_target_pairs={{0,8},{8,0},{16,24},{24,16},{1,9},{9,1},{17,25},{25,17},{2,10},{10... | collective-permute-start | bytes 589832 | tf_op jit(solution)/shard_map/ppermute | solution.py:456
  96.6 1.2 collective-permute-start.27
  97.8 1.1 collective-permute-start.21
  98.9 1.8 %collective-permute-start.22 = (bf16[1,64,768]{2,1,0:T(8,128)(2,1)S(1)}, bf16[1,64,768]{2,1,0:T(8,128)(2,1)S(1)}, u32[]{:S(2)}, u32[]{:S(2)}) collective-permute-start(bf16[1,64,768]{2,1,0:T(8,128)(2,1)S(1)} %get-tuple-element.60), channel_id=1, source_target_pairs={{0,24},{8,16},{16,8},{24,0},{1,25},{9,17},{17,9},{25,1},{2,26},{10... | collective-permute-start | bytes 294920 | tf_op jit(solution)/shard_map/ppermute | solution.py:456
  100.7 2.1 %slot_part.7 = (bf16[1,64,768]{2,1,0:T(8,128)(2,1)S(1)}, bf16[1,64,768]{2,1,0:T(8,128)(2,1)S(1)}, bf16[1,64,768]{2,1,0:T(8,128)(2,1)S(1)}, bf16[1,64,768]{2,1,0:T(8,128)(2,1)S(1)}) custom-call(s32[2]{0:T(128)S(1)} %copy-done.22, bf16[256,1024]{1,0:T(8,128)(2,1)S(1)} %get-tuple-element.51.gate_ref, bf16[256,1024]{1,0:T(8,128)(2,1)S(1)} %get-tuple-element.52.up_ref, ...), custom_call_target="tpu_custom_call" | custom-call | flops 805306368 | bytes 4194304 | tf_op jit(solution)/shard_map/slot_part/pallas_call | solution.py:313
  102.8 7.6 %collective-permute-done.21.refs_2_ = bf16[1,64,768]{2,1,0:T(8,128)(2,1)S(1)} collective-permute-done((bf16[1,64,768]{2,1,0:T(8,128)(2,1)S(1)}, bf16[1,64,768]{2,1,0:T(8,128)(2,1)S(1)}, u32[]{:S(2)}, u32[]{:S(2)}) %collective-permute-start.21) | collective-permute-done | bytes 98336 | tf_op jit(solution)/shard_map/ppermute | solution.py:456
  111.1 3.0 %down_part.3.refs_0_ = bf16[1,1024,6144]{2,1,0:T(8,128)(2,1)} custom-call(s32[2]{0:T(128)S(1)} %copy-done.22, bf16[256,1024]{1,0:T(8,128)(2,1)S(1)} %get-tuple-element.67.act_ref, bf16[1,256,768]{2,1,0:T(8,128)(2,1)S(1)} %constant_dynamic-update-slice_fusion.8.refs_0_.mine_ref, bf16[1,256,768]{2,1,0:T(8,128)(2,1)S(1)} %copy-done.9), custom_call_target="tpu_custom_call" | custom-call | flops 805306368 | bytes 3145728 | tf_op jit(solution)/shard_map/down_part/pallas_call | solution.py:264
  114.1 1.1 collective-permute-start.17
  115.5 1.8 %collective-permute-start.18 = (bf16[1,64,768]{2,1,0:T(8,128)(2,1)S(1)}, bf16[1,64,768]{2,1,0:T(8,128)(2,1)S(1)}, u32[]{:S(2)}, u32[]{:S(2)}) collective-permute-start(bf16[1,64,768]{2,1,0:T(8,128)(2,1)S(1)} %get-tuple-element.56), channel_id=1, source_target_pairs={{0,24},{8,16},{16,8},{24,0},{1,25},{9,17},{17,9},{25,1},{2,26},{10... | collective-permute-start | bytes 294920 | tf_op jit(solution)/shard_map/ppermute | solution.py:456
  117.3 5.0 %collective-permute-start.23 = (bf16[128,768]{1,0:T(8,128)(2,1)S(1)}, bf16[128,768]{1,0:T(8,128)(2,1)S(1)}, u32[]{:S(2)}, u32[]{:S(2)}) collective-permute-start(bf16[128,768]{1,0:T(8,128)(2,1)S(1)} %combine.3), channel_id=1, source_target_pairs={{0,4},{1,5},{2,6},{3,7},{4,0},{5,1},{6,2},{7,3},{8,12},{9,13},{10,... | collective-permute-start | bytes 589832 | tf_op jit(solution)/shard_map/ppermute | solution.py:449
  123.6 3.0 %collective-permute-start.29 = (bf16[128,768]{1,0:T(8,128)(2,1)S(1)}, bf16[128,768]{1,0:T(8,128)(2,1)S(1)}, u32[]{:S(2)}, u32[]{:S(2)}) collective-permute-start(bf16[128,768]{1,0:T(8,128)(2,1)S(1)} %get-tuple-element.66), channel_id=1, source_target_pairs={{0,6},{1,7},{2,0},{3,1},{4,2},{5,3},{6,4},{7,5},{8,14},{9,15},{10,... | collective-permute-start | bytes 589832 | tf_op jit(solution)/shard_map/ppermute | solution.py:449
  126.6 4.9 %down_part.4.refs_0_ = bf16[1,1024,6144]{2,1,0:T(8,128)(2,1)} custom-call(s32[2]{0:T(128)S(1)} %copy-done.22, bf16[256,1024]{1,0:T(8,128)(2,1)S(1)} %get-tuple-element.67.act_ref, bf16[2,256,768]{2,1,0:T(8,128)(2,1)S(1)} %constant_dynamic-update-slice_fusion.4.refs_0_.mine_ref, ...), custom_call_target="tpu_custom_call", output_to_operand_aliasing={{}: (4, {})} | custom-call | flops 1610612736 | bytes 6291456 | tf_op jit(solution)/shard_map/down_part/pallas_call | solution.py:264
  131.4 3.0 %down_part.5 = bf16[1,1024,6144]{2,1,0:T(8,128)(2,1)} custom-call(s32[2]{0:T(128)S(1)} %copy-done.22, bf16[256,1024]{1,0:T(8,128)(2,1)S(1)} %get-tuple-element.67.act_ref, bf16[1,256,768]{2,1,0:T(8,128)(2,1)S(1)} %copy-done.7, bf16[1,256,768]{2,1,0:T(8,128)(2,1)S(1)} %copy-done.11, ...), custom_call_target="tpu_custom_call", output_to_operand_aliasing={{}: (4, {})} | custom-call | flops 805306368 | bytes 3145728 | tf_op jit(solution)/shard_map/down_part/pallas_call | solution.py:264
  134.5 1.8 %collective-permute-done.23.refs_5_ = bf16[128,768]{1,0:T(8,128)(2,1)S(1)} collective-permute-done((bf16[128,768]{1,0:T(8,128)(2,1)S(1)}, bf16[128,768]{1,0:T(8,128)(2,1)S(1)}, u32[]{:S(2)}, u32[]{:S(2)}) %collective-permute-start.23) | collective-permute-done | bytes 196640 | tf_op jit(solution)/shard_map/ppermute | solution.py:449
  (94 shorter events, 14.5 us)
Async XLA Ops:
  0.6 19.3 %collective-permute-start.5 = (bf16[128,768]{1,0:T(8,128)(2,1)}, bf16[128,768]{1,0:T(8,128)(2,1)S(1)}, u32[]{:S(2)}, u32[]{:S(2)}) collective-permute-start(bf16[128,768]{1,0:T(8,128)(2,1)} %refs_0_.1), channel_id=1, source_target_pairs={{0,2},{1,3},{2,4},{3,5},{4,6},{5,7},{6,0},{7,1},{8,10},{9,11},{10,... | collective-permute-start | bytes 589832 | tf_op jit(solution)/shard_map/ppermute | solution.py:449
  3.7 27.6 %collective-permute-start = (bf16[128,768]{1,0:T(8,128)(2,1)}, bf16[128,768]{1,0:T(8,128)(2,1)S(1)}, u32[]{:S(2)}, u32[]{:S(2)}) collective-permute-start(bf16[128,768]{1,0:T(8,128)(2,1)} %refs_0_.1), channel_id=1, source_target_pairs={{0,4},{1,5},{2,6},{3,7},{4,0},{5,1},{6,2},{7,3},{8,12},{9,13},{10,... | collective-permute-start | bytes 589832 | tf_op jit(solution)/shard_map/ppermute | solution.py:449
  6.3 13.6 %collective-permute-start.6 = (bf16[128,768]{1,0:T(8,128)(2,1)}, bf16[128,768]{1,0:T(8,128)(2,1)S(1)}, u32[]{:S(2)}, u32[]{:S(2)}) collective-permute-start(bf16[128,768]{1,0:T(8,128)(2,1)} %refs_0_.1), channel_id=1, source_target_pairs={{0,6},{1,7},{2,0},{3,1},{4,2},{5,3},{6,4},{7,5},{8,14},{9,15},{10,... | collective-permute-start | bytes 589832 | tf_op jit(solution)/shard_map/ppermute | solution.py:449
  12.7 4.7 %collective-permute-start.11 = (bf16[1,64,768]{2,1,0:T(8,128)(2,1)S(1)}, bf16[1,64,768]{2,1,0:T(8,128)(2,1)S(1)}, u32[]{:S(2)}, u32[]{:S(2)}) collective-permute-start(bf16[1,64,768]{2,1,0:T(8,128)(2,1)S(1)} %get-tuple-element.46), channel_id=1, source_target_pairs={{0,8},{8,0},{16,24},{24,16},{1,9},{9,1},{17,25},{25,17},{2,10},{10... | collective-permute-start | bytes 294920 | tf_op jit(solution)/shard_map/ppermute | solution.py:456
  14.3 6.6 %collective-permute-start.12 = (bf16[1,64,768]{2,1,0:T(8,128)(2,1)S(1)}, bf16[1,64,768]{2,1,0:T(8,128)(2,1)S(1)}, u32[]{:S(2)}, u32[]{:S(2)}) collective-permute-start(bf16[1,64,768]{2,1,0:T(8,128)(2,1)S(1)} %get-tuple-element.47), channel_id=1, source_target_pairs={{0,16},{8,24},{16,0},{24,8},{1,17},{9,25},{17,1},{25,9},{2,18},{10... | collective-permute-start | bytes 294920 | tf_op jit(solution)/shard_map/ppermute | solution.py:456
  17.4 13.3 %collective-permute-start.13 = (bf16[1,64,768]{2,1,0:T(8,128)(2,1)S(1)}, bf16[1,64,768]{2,1,0:T(8,128)(2,1)S(1)}, u32[]{:S(2)}, u32[]{:S(2)}) collective-permute-start(bf16[1,64,768]{2,1,0:T(8,128)(2,1)S(1)} %get-tuple-element.48), channel_id=1, source_target_pairs={{0,24},{8,16},{16,8},{24,0},{1,25},{9,17},{17,9},{25,1},{2,26},{10... | collective-permute-start | bytes 294920 | tf_op jit(solution)/shard_map/ppermute | solution.py:456
  20.3 7.9 %collective-permute-start.7 = (bf16[2,64,768]{2,1,0:T(8,128)(2,1)S(1)}, bf16[2,64,768]{2,1,0:T(8,128)(2,1)S(1)}, u32[]{:S(2)}, u32[]{:S(2)}) collective-permute-start(bf16[2,64,768]{2,1,0:T(8,128)(2,1)S(1)} %get-tuple-element.42), channel_id=1, source_target_pairs={{0,8},{8,0},{16,24},{24,16},{1,9},{9,1},{17,25},{25,17},{2,10},{10... | collective-permute-start | bytes 589832 | tf_op jit(solution)/shard_map/ppermute | solution.py:456
  20.9 9.7 %collective-permute-start.8 = (bf16[2,64,768]{2,1,0:T(8,128)(2,1)S(1)}, bf16[2,64,768]{2,1,0:T(8,128)(2,1)S(1)}, u32[]{:S(2)}, u32[]{:S(2)}) collective-permute-start(bf16[2,64,768]{2,1,0:T(8,128)(2,1)S(1)} %get-tuple-element.43), channel_id=1, source_target_pairs={{0,16},{8,24},{16,0},{24,8},{1,17},{9,25},{17,1},{25,9},{2,18},{10... | collective-permute-start | bytes 589832 | tf_op jit(solution)/shard_map/ppermute | solution.py:456
  21.4 9.2 %collective-permute-start.9 = (bf16[2,64,768]{2,1,0:T(8,128)(2,1)S(1)}, bf16[2,64,768]{2,1,0:T(8,128)(2,1)S(1)}, u32[]{:S(2)}, u32[]{:S(2)}) collective-permute-start(bf16[2,64,768]{2,1,0:T(8,128)(2,1)S(1)} %get-tuple-element.44), channel_id=1, source_target_pairs={{0,24},{8,16},{16,8},{24,0},{1,25},{9,17},{17,9},{25,1},{2,26},{10... | collective-permute-start | bytes 589832 | tf_op jit(solution)/shard_map/ppermute | solution.py:456
  30.6 31.0 %collective-permute-start.10 = (bf16[2,256,768]{2,1,0:T(8,128)(2,1)S(1)}, bf16[2,256,768]{2,1,0:T(8,128)(2,1)S(1)}, u32[]{:S(2)}, u32[]{:S(2)}) collective-permute-start(bf16[2,256,768]{2,1,0:T(8,128)(2,1)S(1)} %constant_dynamic-update-slice_fusion.4.refs_0_.mine_ref), channel_id=1, source_target_pairs={{0,1},{1,0},{2,3},{3,2},{4,5},{5,4},{6,7},{7,6},{8,9},{9,8},{10,11... | collective-permute-start | bytes 2359304 | tf_op jit(solution)/shard_map/ppermute | solution.py:452
  30.8 22.6 %collective-permute-start.14 = (bf16[1,256,768]{2,1,0:T(8,128)(2,1)S(1)}, bf16[1,256,768]{2,1,0:T(8,128)(2,1)S(1)}, u32[]{:S(2)}, u32[]{:S(2)}) collective-permute-start(bf16[1,256,768]{2,1,0:T(8,128)(2,1)S(1)} %constant_dynamic-update-slice_fusion.8.refs_0_.mine_ref), channel_id=1, source_target_pairs={{0,1},{1,0},{2,3},{3,2},{4,5},{5,4},{6,7},{7,6},{8,9},{9,8},{10,11... | collective-permute-start | bytes 1179656 | tf_op jit(solution)/shard_map/ppermute | solution.py:452
  31.6 4.8 %collective-permute-start.1 = (bf16[1,64,768]{2,1,0:T(8,128)(2,1)S(1)}, bf16[1,64,768]{2,1,0:T(8,128)(2,1)S(1)}, u32[]{:S(2)}, u32[]{:S(2)}) collective-permute-start(bf16[1,64,768]{2,1,0:T(8,128)(2,1)S(1)} %get-tuple-element.38), channel_id=1, source_target_pairs={{0,8},{8,0},{16,24},{24,16},{1,9},{9,1},{17,25},{25,17},{2,10},{10... | collective-permute-start | bytes 294920 | tf_op jit(solution)/shard_map/ppermute | solution.py:456
  33.1 6.7 %collective-permute-start.2 = (bf16[1,64,768]{2,1,0:T(8,128)(2,1)S(1)}, bf16[1,64,768]{2,1,0:T(8,128)(2,1)S(1)}, u32[]{:S(2)}, u32[]{:S(2)}) collective-permute-start(bf16[1,64,768]{2,1,0:T(8,128)(2,1)S(1)} %get-tuple-element.39), channel_id=1, source_target_pairs={{0,16},{8,24},{16,0},{24,8},{1,17},{9,25},{17,1},{25,9},{2,18},{10... | collective-permute-start | bytes 294920 | tf_op jit(solution)/shard_map/ppermute | solution.py:456
  33.6 6.2 %collective-permute-start.3 = (bf16[1,64,768]{2,1,0:T(8,128)(2,1)S(1)}, bf16[1,64,768]{2,1,0:T(8,128)(2,1)S(1)}, u32[]{:S(2)}, u32[]{:S(2)}) collective-permute-start(bf16[1,64,768]{2,1,0:T(8,128)(2,1)S(1)} %get-tuple-element.40), channel_id=1, source_target_pairs={{0,24},{8,16},{16,8},{24,0},{1,25},{9,17},{17,9},{25,1},{2,26},{10... | collective-permute-start | bytes 294920 | tf_op jit(solution)/shard_map/ppermute | solution.py:456
  39.8 25.6 %copy-start.6 = (bf16[1,256,768]{2,1,0:T(8,128)(2,1)}, bf16[1,256,768]{2,1,0:T(8,128)(2,1)S(1)}, u32[]{:S(2)}) copy-start(bf16[1,256,768]{2,1,0:T(8,128)(2,1)S(1)} %constant_dynamic-update-slice_fusion.refs_0_.mine_ref) | copy-start | bytes 1179652
  39.8 27.6 %collective-permute-start.4 = (bf16[1,256,768]{2,1,0:T(8,128)(2,1)S(1)}, bf16[1,256,768]{2,1,0:T(8,128)(2,1)S(1)}, u32[]{:S(2)}, u32[]{:S(2)}) collective-permute-start(bf16[1,256,768]{2,1,0:T(8,128)(2,1)S(1)} %constant_dynamic-update-slice_fusion.refs_0_.mine_ref), channel_id=1, source_target_pairs={{0,1},{1,0},{2,3},{3,2},{4,5},{5,4},{6,7},{7,6},{8,9},{9,8},{10,11... | collective-permute-start | bytes 1179656 | tf_op jit(solution)/shard_map/ppermute | solution.py:452
  39.9 1.1 copy-start.17
  41.0 1.0 copy-start.18
  44.2 1.0 copy-start.13
  45.2 1.0 copy-start.15
  46.2 4.6 %copy-start = (bf16[1,1024,6144]{2,1,0:T(8,128)(2,1)S(1)}, bf16[1,1024,6144]{2,1,0:T(8,128)(2,1)}, u32[]{:S(2)}) copy-start(bf16[1,1024,6144]{2,1,0:T(8,128)(2,1)} %refs_1_.11) | copy-start | bytes 37748740
  51.3 4.6 %copy-start.1 = (bf16[1,1024,6144]{2,1,0:T(8,128)(2,1)S(1)}, bf16[1,1024,6144]{2,1,0:T(8,128)(2,1)}, u32[]{:S(2)}) copy-start(bf16[1,1024,6144]{2,1,0:T(8,128)(2,1)} %refs_1_.11) | copy-start | bytes 37748740
  55.9 5.7 %copy-start.8 = (bf16[1,256,768]{2,1,0:T(8,128)(2,1)}, bf16[1,256,768]{2,1,0:T(8,128)(2,1)S(1)}, u32[]{:S(2)}) copy-start(bf16[1,256,768]{2,1,0:T(8,128)(2,1)S(1)} %collective-permute-done.14.refs_0_.theirs_ref) | copy-start | bytes 1179652
  61.7 5.8 %copy-start.14 = (f32[256,1024]{1,0:T(8,128)S(1)}, f32[256,1024]{1,0:T(8,128)}, u32[]{:S(2)}) copy-start(f32[256,1024]{1,0:T(8,128)} %copy-done.13) | copy-start | bytes 3145732
  61.7 5.8 %copy-start.16 = (f32[256,1024]{1,0:T(8,128)S(1)}, f32[256,1024]{1,0:T(8,128)}, u32[]{:S(2)}) copy-start(f32[256,1024]{1,0:T(8,128)} %copy-done.15) | copy-start | bytes 3145732
  65.5 4.1 %copy-start.22 = (s32[2]{0:T(128)S(1)}, s32[2]{0:T(128)}, u32[]{:S(2)}) copy-start(s32[2]{0:T(128)} %pad_add_fusion.where_ref) | copy-start | bytes 28
  67.5 2.1 %copy-start.10 = (bf16[1,256,768]{2,1,0:T(8,128)(2,1)}, bf16[1,256,768]{2,1,0:T(8,128)(2,1)S(1)}, u32[]{:S(2)}) copy-start(bf16[1,256,768]{2,1,0:T(8,128)(2,1)S(1)} %collective-permute-done.4.refs_0_.theirs_ref) | copy-start | bytes 1179652
  69.6 4.6 %copy-start.2 = (bf16[1,6144,1024]{2,1,0:T(8,128)(2,1)S(1)}, bf16[1,6144,1024]{2,1,0:T(8,128)(2,1)}, u32[]{:S(2)}) copy-start(bf16[1,6144,1024]{2,1,0:T(8,128)(2,1)} %wg_ref.11) | copy-start | bytes 37748740
  74.2 4.6 %copy-start.3 = (bf16[1,6144,1024]{2,1,0:T(8,128)(2,1)S(1)}, bf16[1,6144,1024]{2,1,0:T(8,128)(2,1)}, u32[]{:S(2)}) copy-start(bf16[1,6144,1024]{2,1,0:T(8,128)(2,1)} %wu_ref.11) | copy-start | bytes 37748740
  82.3 8.1 %collective-permute-start.24 = (bf16[2,256,768]{2,1,0:T(8,128)(2,1)S(1)}, bf16[2,256,768]{2,1,0:T(8,128)(2,1)S(1)}, u32[]{:S(2)}, u32[]{:S(2)}) collective-permute-start(bf16[2,256,768]{2,1,0:T(8,128)(2,1)S(1)} %slot_part.10), channel_id=1, source_target_pairs={{0,1},{1,0},{2,3},{3,2},{4,5},{5,4},{6,7},{7,6},{8,9},{9,8},{10,11... | collective-permute-start | bytes 2359304 | tf_op jit(solution)/shard_map/ppermute | solution.py:452
  84.9 2.7 %collective-permute-start.19 = (bf16[1,256,768]{2,1,0:T(8,128)(2,1)S(1)}, bf16[1,256,768]{2,1,0:T(8,128)(2,1)S(1)}, u32[]{:S(2)}, u32[]{:S(2)}) collective-permute-start(bf16[1,256,768]{2,1,0:T(8,128)(2,1)S(1)} %slot_part.8), channel_id=1, source_target_pairs={{0,1},{1,0},{2,3},{3,2},{4,5},{5,4},{6,7},{7,6},{8,9},{9,8},{10,11... | collective-permute-start | bytes 1179656 | tf_op jit(solution)/shard_map/ppermute | solution.py:452
  87.1 10.7 %collective-permute-start.15 = (bf16[1,256,768]{2,1,0:T(8,128)(2,1)S(1)}, bf16[1,256,768]{2,1,0:T(8,128)(2,1)S(1)}, u32[]{:S(2)}, u32[]{:S(2)}) collective-permute-start(bf16[1,256,768]{2,1,0:T(8,128)(2,1)S(1)} %slot_part.6), channel_id=1, source_target_pairs={{0,1},{1,0},{2,3},{3,2},{4,5},{5,4},{6,7},{7,6},{8,9},{9,8},{10,11... | collective-permute-start | bytes 1179656 | tf_op jit(solution)/shard_map/ppermute | solution.py:452
  89.8 9.1 %collective-permute-start.20 = (bf16[1,64,768]{2,1,0:T(8,128)(2,1)S(1)}, bf16[1,64,768]{2,1,0:T(8,128)(2,1)S(1)}, u32[]{:S(2)}, u32[]{:S(2)}) collective-permute-start(bf16[1,64,768]{2,1,0:T(8,128)(2,1)S(1)} %get-tuple-element.58), channel_id=1, source_target_pairs={{0,8},{8,0},{16,24},{24,16},{1,9},{9,1},{17,25},{25,17},{2,10},{10... | collective-permute-start | bytes 294920 | tf_op jit(solution)/shard_map/ppermute | solution.py:456
  94.2 21.2 %collective-permute-start.25 = (bf16[2,64,768]{2,1,0:T(8,128)(2,1)S(1)}, bf16[2,64,768]{2,1,0:T(8,128)(2,1)S(1)}, u32[]{:S(2)}, u32[]{:S(2)}) collective-permute-start(bf16[2,64,768]{2,1,0:T(8,128)(2,1)S(1)} %get-tuple-element.62), channel_id=1, source_target_pairs={{0,8},{8,0},{16,24},{24,16},{1,9},{9,1},{17,25},{25,17},{2,10},{10... | collective-permute-start | bytes 589832 | tf_op jit(solution)/shard_map/ppermute | solution.py:456
  95.7 21.6 %collective-permute-start.26 = (bf16[2,64,768]{2,1,0:T(8,128)(2,1)S(1)}, bf16[2,64,768]{2,1,0:T(8,128)(2,1)S(1)}, u32[]{:S(2)}, u32[]{:S(2)}) collective-permute-start(bf16[2,64,768]{2,1,0:T(8,128)(2,1)S(1)} %get-tuple-element.63), channel_id=1, source_target_pairs={{0,16},{8,24},{16,0},{24,8},{1,17},{9,25},{17,1},{25,9},{2,18},{10... | collective-permute-start | bytes 589832 | tf_op jit(solution)/shard_map/ppermute | solution.py:456
  96.6 25.7 %collective-permute-start.27 = (bf16[2,64,768]{2,1,0:T(8,128)(2,1)S(1)}, bf16[2,64,768]{2,1,0:T(8,128)(2,1)S(1)}, u32[]{:S(2)}, u32[]{:S(2)}) collective-permute-start(bf16[2,64,768]{2,1,0:T(8,128)(2,1)S(1)} %get-tuple-element.64), channel_id=1, source_target_pairs={{0,24},{8,16},{16,8},{24,0},{1,25},{9,17},{17,9},{25,1},{2,26},{10... | collective-permute-start | bytes 589832 | tf_op jit(solution)/shard_map/ppermute | solution.py:456
  97.8 12.7 %collective-permute-start.21 = (bf16[1,64,768]{2,1,0:T(8,128)(2,1)S(1)}, bf16[1,64,768]{2,1,0:T(8,128)(2,1)S(1)}, u32[]{:S(2)}, u32[]{:S(2)}) collective-permute-start(bf16[1,64,768]{2,1,0:T(8,128)(2,1)S(1)} %get-tuple-element.59), channel_id=1, source_target_pairs={{0,16},{8,24},{16,0},{24,8},{1,17},{9,25},{17,1},{25,9},{2,18},{10... | collective-permute-start | bytes 294920 | tf_op jit(solution)/shard_map/ppermute | solution.py:456
  98.9 12.2 %copy-start.9 = (bf16[1,256,768]{2,1,0:T(8,128)(2,1)S(1)}, bf16[1,256,768]{2,1,0:T(8,128)(2,1)}, u32[]{:S(2)}) copy-start(bf16[1,256,768]{2,1,0:T(8,128)(2,1)} %copy-done.8) | copy-start | bytes 1179652
  98.9 15.2 %collective-permute-start.22 = (bf16[1,64,768]{2,1,0:T(8,128)(2,1)S(1)}, bf16[1,64,768]{2,1,0:T(8,128)(2,1)S(1)}, u32[]{:S(2)}, u32[]{:S(2)}) collective-permute-start(bf16[1,64,768]{2,1,0:T(8,128)(2,1)S(1)} %get-tuple-element.60), channel_id=1, source_target_pairs={{0,24},{8,16},{16,8},{24,0},{1,25},{9,17},{17,9},{25,1},{2,26},{10... | collective-permute-start | bytes 294920 | tf_op jit(solution)/shard_map/ppermute | solution.py:456
  102.8 12.4 %copy-start.5 = (bf16[256,128]{1,0:T(8,128)(2,1)S(1)}, bf16[256,128]{1,0:T(8,128)(2,1)}, u32[]{:S(2)}) copy-start(bf16[256,128]{1,0:T(8,128)(2,1)} %get-tuple-element.35.refs_1_.refs_2_.refs_4_) | copy-start | bytes 196612
  110.5 13.1 %collective-permute-start.16 = (bf16[1,64,768]{2,1,0:T(8,128)(2,1)S(1)}, bf16[1,64,768]{2,1,0:T(8,128)(2,1)S(1)}, u32[]{:S(2)}, u32[]{:S(2)}) collective-permute-start(bf16[1,64,768]{2,1,0:T(8,128)(2,1)S(1)} %get-tuple-element.54), channel_id=1, source_target_pairs={{0,8},{8,0},{16,24},{24,16},{1,9},{9,1},{17,25},{25,17},{2,10},{10... | collective-permute-start | bytes 294920 | tf_op jit(solution)/shard_map/ppermute | solution.py:456
  114.1 20.4 %collective-permute-start.17 = (bf16[1,64,768]{2,1,0:T(8,128)(2,1)S(1)}, bf16[1,64,768]{2,1,0:T(8,128)(2,1)S(1)}, u32[]{:S(2)}, u32[]{:S(2)}) collective-permute-start(bf16[1,64,768]{2,1,0:T(8,128)(2,1)S(1)} %get-tuple-element.55), channel_id=1, source_target_pairs={{0,16},{8,24},{16,0},{24,8},{1,17},{9,25},{17,1},{25,9},{2,18},{10... | collective-permute-start | bytes 294920 | tf_op jit(solution)/shard_map/ppermute | solution.py:456
  115.5 19.0 %collective-permute-start.18 = (bf16[1,64,768]{2,1,0:T(8,128)(2,1)S(1)}, bf16[1,64,768]{2,1,0:T(8,128)(2,1)S(1)}, u32[]{:S(2)}, u32[]{:S(2)}) collective-permute-start(bf16[1,64,768]{2,1,0:T(8,128)(2,1)S(1)} %get-tuple-element.56), channel_id=1, source_target_pairs={{0,24},{8,16},{16,8},{24,0},{1,25},{9,17},{17,9},{25,1},{2,26},{10... | collective-permute-start | bytes 294920 | tf_op jit(solution)/shard_map/ppermute | solution.py:456
  117.3 19.0 %collective-permute-start.23 = (bf16[128,768]{1,0:T(8,128)(2,1)S(1)}, bf16[128,768]{1,0:T(8,128)(2,1)S(1)}, u32[]{:S(2)}, u32[]{:S(2)}) collective-permute-start(bf16[128,768]{1,0:T(8,128)(2,1)S(1)} %combine.3), channel_id=1, source_target_pairs={{0,4},{1,5},{2,6},{3,7},{4,0},{5,1},{6,2},{7,3},{8,12},{9,13},{10,... | collective-permute-start | bytes 589832 | tf_op jit(solution)/shard_map/ppermute | solution.py:449
  122.6 13.7 %collective-permute-start.28 = (bf16[128,768]{1,0:T(8,128)(2,1)S(1)}, bf16[128,768]{1,0:T(8,128)(2,1)S(1)}, u32[]{:S(2)}, u32[]{:S(2)}) collective-permute-start(bf16[128,768]{1,0:T(8,128)(2,1)S(1)} %get-tuple-element.65), channel_id=1, source_target_pairs={{0,2},{1,3},{2,4},{3,5},{4,6},{5,7},{6,0},{7,1},{8,10},{9,11},{10,... | collective-permute-start | bytes 589832 | tf_op jit(solution)/shard_map/ppermute | solution.py:449
  123.6 7.9 %copy-start.7 = (bf16[1,256,768]{2,1,0:T(8,128)(2,1)S(1)}, bf16[1,256,768]{2,1,0:T(8,128)(2,1)}, u32[]{:S(2)}) copy-start(bf16[1,256,768]{2,1,0:T(8,128)(2,1)} %copy-done.6) | copy-start | bytes 1179652
  123.6 7.9 %copy-start.11 = (bf16[1,256,768]{2,1,0:T(8,128)(2,1)S(1)}, bf16[1,256,768]{2,1,0:T(8,128)(2,1)}, u32[]{:S(2)}) copy-start(bf16[1,256,768]{2,1,0:T(8,128)(2,1)} %copy-done.10) | copy-start | bytes 1179652
  123.6 12.7 %collective-permute-start.29 = (bf16[128,768]{1,0:T(8,128)(2,1)S(1)}, bf16[128,768]{1,0:T(8,128)(2,1)S(1)}, u32[]{:S(2)}, u32[]{:S(2)}) collective-permute-start(bf16[128,768]{1,0:T(8,128)(2,1)S(1)} %get-tuple-element.66), channel_id=1, source_target_pairs={{0,6},{1,7},{2,0},{3,1},{4,2},{5,3},{6,4},{7,5},{8,14},{9,15},{10,... | collective-permute-start | bytes 589832 | tf_op jit(solution)/shard_map/ppermute | solution.py:449
  (5 other events, 3.9 us)

commit v2 on v0

--- a/solution.py
+++ b/solution.py
@@ -1,7 +1,312 @@
+import functools
 import jax
 import jax.numpy as jnp
 from jax import lax
+from jax.experimental import pallas as pl
+from jax.experimental.pallas import tpu as pltpu
 from jax.sharding import PartitionSpec as P
+
+BF16 = jnp.bfloat16
+F32 = jnp.float32
+VMEM = pl.BlockSpec(memory_space=pltpu.VMEM)
+ANY = pl.BlockSpec(memory_space=pl.ANY)
+NT = (((1,), (1,)), ((), ()))
+TN = (((0,), (0,)), ((), ()))
+NN = (((1,), (0,)), ((), ()))
+MIB = 1 << 20
+
+
+def dot(a, b, dims):
+    return lax.dot_general(a, b, dims, preferred_element_type=F32)
+
+
+def shaped(shape, dtype):
+    return jax.ShapeDtypeStruct(shape, dtype)
+
+
+def call(kernel, name, operands, out_shape, after=(), flops=0, moved=0, mib=8, out_specs=None, **more):
+    count, extra, results = len(operands), len(after), len(out_shape)
+
+    def body(*refs):
+        outs = refs[count + extra :]
+        kernel(*refs[:count], *outs[:results], *outs[results + 1 :])
+        outs[results][...] = jnp.zeros((8, 128), F32)
+
+    out_shape = list(out_shape) + [shaped((8, 128), F32)]
+    out_specs = list(out_specs or [VMEM] * results) + [VMEM]
+    specs = more.pop("in_specs", [VMEM] * count)
+    return pl.pallas_call(
+        body,
+        out_shape=out_shape,
+        in_specs=list(specs) + [VMEM] * extra,
+        out_specs=out_specs,
+        compiler_params=pltpu.CompilerParams(vmem_limit_bytes=mib * MIB),
+        cost_estimate=pl.CostEstimate(
+            flops=int(flops), bytes_accessed=int(moved), transcendentals=0
+        ),
+        name=name,
+        **more,
+    )(*operands, *after)
+
+
+def fill(raw, sel, gate, outs, b, capacity):
+    rows = (dot(sel, raw, NN) * gate).astype(BF16)
+    for r, out in enumerate(outs):
+        out[b] = rows[r * capacity : (r + 1) * capacity]
+
+
+def first_pack(raw, ids, probs, experts, capacity):
+    tokens, columns = raw.shape
+    lines = max(8, experts)
+    rows = experts * capacity
+
+    def kernel(raw_ref, ids_ref, probs_ref, sel_ref, gate_ref, copy_ref, *outs):
+        copy_ref[...] = raw_ref[...]
+        me = lax.axis_index("expert")
+        expert = lax.broadcasted_iota(jnp.int32, (lines, tokens), 0) ^ me
+        first = (ids_ref[0:1, :] == expert).astype(F32)
+        second = (ids_ref[1:2, :] == expert).astype(F32)
+        hit = first + second
+        before = lax.broadcasted_iota(jnp.int32, (tokens, tokens), 0)
+        here = lax.broadcasted_iota(jnp.int32, (tokens, tokens), 1)
+        earlier = (before < here).astype(F32).astype(BF16)
+        place = dot(hit.astype(BF16), earlier, NN)
+        place = jnp.where(hit > 0.0, place, -1.0)
+        gate = first * probs_ref[0:1, :] + second * probs_ref[1:2, :]
+        slot = lax.broadcasted_iota(jnp.int32, (capacity, tokens), 0).astype(F32)
+        for r in range(experts):
+            match = place[r : r + 1, :] == slot
+            span = pl.ds(r * capacity, capacity)
+            sel_ref[span, :] = jnp.where(match, 1.0, 0.0).astype(BF16)
+            gate_ref[span, :] = jnp.sum(
+                jnp.where(match, gate[r : r + 1, :], 0.0), axis=1, keepdims=True
+            )
+        fill(raw_ref[...], sel_ref[...], gate_ref[...], outs, 0, capacity)
+
+    return call(
+        kernel,
+        "first_pack",
+        [raw, ids, probs],
+        [shaped((rows, tokens), BF16), shaped((rows, 1), F32), shaped(raw.shape, BF16)]
+        + [shaped((1, capacity, columns), BF16)] * experts,
+        flops=2 * rows * tokens * columns,
+        moved=1e6,
+    )
+
+
+def pack(raws, sel, gate, experts, capacity, after):
+    blocks = len(raws)
+    columns = raws[0].shape[1]
+
+    def kernel(*refs):
+        sel_ref, gate_ref = refs[blocks : blocks + 2]
+        for b in range(blocks):
+            fill(refs[b][...], sel_ref[...], gate_ref[...], refs[blocks + 2 :], b, capacity)
+
+    return call(
+        kernel,
+        "pack",
+        [*raws, sel, gate],
+        [shaped((blocks, capacity, columns), BF16)] * experts,
+        after,
+        flops=2 * blocks * sel.shape[0] * sel.shape[1] * columns,
+        moved=6e5 * blocks,
+    )
+
+
+def activations(gate_pre, up_pre, after):
+    _, groups, capacity, units = gate_pre.shape
+    rows = groups * capacity
+
+    def kernel(gate_ref, up_ref, up_factor, gate_factor, act):
+        me = lax.axis_index("expert")
+        tile = 256
+
+        def step(i, unused):
+            span = pl.ds(pl.multiple_of(i * tile, tile), tile)
+            a = jnp.concatenate([gate_ref[0, me ^ r, :, span] for r in range(groups)], axis=0)
+            b = jnp.concatenate([up_ref[0, me ^ r, :, span] for r in range(groups)], axis=0)
+            a = a.astype(F32).T
+            b = b.astype(F32).T
+            sig = 1.0 / (1.0 + jnp.exp(-a))
+            swish = a * sig
+            up_factor[span, :] = swish
+            gate_factor[span, :] = b * sig * (1.0 + a * (1.0 - sig))
+            act[span, :] = (swish * b).astype(BF16)
+            return unused
+
+        lax.fori_loop(0, units // tile, step, 0)
+
+    return call(
+        kernel,
+        "activations",
+        [gate_pre, up_pre],
+        [shaped((units, rows), F32), shaped((units, rows), F32), shaped((units, rows), BF16)],
+        after,
+        flops=3e7,
+        moved=14 * rows * units,
+    )
+
+
+def block_of(shift, line, sibling):
+    cut = lax.axis_index("cuts")
+    z = lax.rem(lax.div(cut, 2) + (shift + line), line)
+    core = lax.rem(cut, 2)
+    return z * 2 + (1 - core if sibling else core)
+
+
+def hidden_part(x, w_down, shifts, line, sibling, total, factors, after):
+    blocks, rows, columns = x.shape
+    units = w_down.shape[1]
+    tile = 256
+    has_total = total is not None
+
+    def kernel(x_ref, w_ref, *refs):
+        outs = refs[has_total + len(factors) :]
+        factor_refs = refs[has_total : has_total + len(factors)]
+        starts = [
+            pl.multiple_of(block_of(-s, line, sibling) * columns, 128) for s in shifts
+        ]
+
+        def step(i, unused):
+            span = pl.ds(pl.multiple_of(i * tile, tile), tile)
+            value = refs[0][span, :] if has_total else 0.0
+            for b, start in enumerate(starts):
+                value = value + dot(w_ref[0, span, pl.ds(start, columns)], x_ref[b], NT)
+            if factors:
+                for out, factor in zip(outs, factor_refs):
+                    out[span, :] = (value * factor[span, :]).astype(BF16)
+            else:
+                outs[0][span, :] = value
+            return unused
+
+        lax.fori_loop(0, units // tile, step, 0)
+
+    return call(
+        kernel,
+        "hidden_part",
+        [x, w_down] + ([total] if has_total else []) + list(factors),
+        [shaped((units, rows), BF16)] * 2 if factors else [shaped((units, rows), F32)],
+        after,
+        flops=2 * blocks * rows * columns * units,
+        moved=2 * blocks * columns * units + 8 * rows * units,
+    )
+
+
+def down_part(act, mine, theirs, shifts, line, before, out_shape, after):
+    blocks, rows, columns = mine.shape
+    units = act.shape[0]
+    split = 4
+    part = units // split
+    steps = [(half, b) for half in range(2) for b in range(blocks)]
+
+    def kernel(act_ref, mine_ref, theirs_ref, *refs):
+        out_ref, held, sems = refs[-3:]
+        copies = []
+        for i, (half, b) in enumerate(steps):
+            start = pl.multiple_of(block_of(-shifts[b], line, bool(half)) * columns, 128)
+            now = i % 2
+            x = (theirs_ref if half else mine_ref)[b]
+            for j in range(split):
+                if i >= 2:
+                    copies[(i - 2) * split + j].wait()
+                span = pl.ds(j * part, part)
+                held[now, span, :] = dot(act_ref[span, :], x, NN).astype(BF16)
+                copy = pltpu.make_async_copy(
+                    held.at[now, span, :],
+                    out_ref.at[0, span, pl.ds(start, columns)],
+                    sems.at[now, j],
+                )
+                copy.start()
+                copies.append(copy)
+        for copy in copies[-2 * split :]:
+            copy.wait()
+
+    operands = [act, mine, theirs]
+    if before is not None:
+        operands.append(before)
+    return call(
+        kernel,
+        "down_part",
+        operands,
+        [shaped(out_shape, BF16)],
+        after,
+        flops=4 * blocks * rows * columns * units,
+        moved=4 * blocks * columns * units,
+        in_specs=[VMEM] * 3 + [ANY] * (len(operands) - 3),
+        out_specs=[ANY],
+        input_output_aliases={} if before is None else {3: 0},
+        scratch_shapes=[
+            pltpu.VMEM((2, units, columns), BF16),
+            pltpu.SemaphoreType.DMA((2, split)),
+        ],
+    )
+
+
+def slot_part(gate_grad, up_grad, w_gate, w_up, shifts, line, sibling, arrived, experts, after):
+    units, rows = gate_grad.shape
+    blocks = len(shifts)
+    columns = w_gate.shape[1] // (2 * line)
+    tile = 256
+    capacity = rows // experts
+    split = arrived is not None
+
+    def kernel(gate_ref, up_ref, wg_ref, wu_ref, *refs):
+        for b, shift in enumerate(shifts):
+            base = block_of(shift, line, sibling) * columns
+            for i in range(columns // tile):
+                span = pl.ds(pl.multiple_of(base + i * tile, tile), tile)
+                value = dot(wg_ref[0, span, :], gate_ref[...], NN)
+                value = (value + dot(wu_ref[0, span, :], up_ref[...], NN)).T
+                out = pl.ds(i * tile, tile)
+                if not split:
+                    refs[0][b, :, out] = value.astype(BF16)
+                    continue
+                value = (value + refs[0][b, :, out].astype(F32)).astype(BF16)
+                for r in range(experts):
+                    refs[1 + r][b, :, out] = value[r * capacity : (r + 1) * capacity]
+
+    if split:
+        out_shape = [shaped((blocks, capacity, columns), BF16)] * experts
+    else:
+        out_shape = [shaped((blocks, rows, columns), BF16)]
+    return call(
+        kernel,
+        "slot_part",
+        [gate_grad, up_grad, w_gate, w_up] + ([arrived] if split else []),
+        out_shape,
+        after,
+        flops=4 * blocks * rows * columns * units,
+        moved=4 * blocks * columns * units + 4 * rows * units,
+    )
+
+
+def combine(pieces, sel, others, after):
+    experts = len(pieces)
+    blocks, _, columns = pieces[0].shape
+    tokens = sel.shape[1]
+    count = len(others)
+
+    def kernel(*refs):
+        piece_refs, sel_ref = refs[:experts], refs[experts]
+        other_refs = refs[experts + 1 : experts + 1 + count]
+        out_refs = refs[experts + 1 + count :]
+        for b in range(blocks):
+            rows = jnp.concatenate([piece[b] for piece in piece_refs], axis=0)
+            value = dot(sel_ref[...], rows, TN)
+            for other in other_refs:
+                value = value + other[...].astype(F32)
+            out_refs[b][...] = value.astype(BF16)
+
+    return call(
+        kernel,
+        "combine",
+        [*pieces, sel, *others],
+        [shaped((tokens, columns), BF16)] * blocks,
+        after,
+        flops=2 * blocks * sel.shape[0] * tokens * columns,
+        moved=6e5 * blocks + 2e5 * count,
+    )
 
 
 def slot_tables(routing, experts, capacity):
@@ -25,7 +330,7 @@
     return jnp.take(weighted, source, axis=0).reshape(experts, capacity, columns)
 
 
-def on_device(out_grad, gate_probs, expert_ids, gate_pre, up_pre, w_gate, w_up, w_down):
+def on_any_tiling(out_grad, gate_probs, expert_ids, gate_pre, up_pre, w_gate, w_up, w_down):
     tokens_here = expert_ids.shape[0]
     experts = lax.axis_size("expert") * w_gate.shape[0]
     groups = gate_pre.shape[1]
@@ -82,6 +387,82 @@
     return (input_grad.T.astype(jnp.bfloat16), w_down_grad)
 
 
+def on_device(out_grad, gate_probs, expert_ids, gate_pre, up_pre, w_gate, w_up, w_down):
+    experts = lax.axis_size("expert")
+    cuts = lax.axis_size("cuts")
+    line = cuts // 2
+    capacity = gate_pre.shape[2]
+    if out_grad.shape[1] % 256 or gate_pre.shape[3] % 256 or capacity % 16 or cuts != 8:
+        return on_any_tiling(
+            out_grad, gate_probs, expert_ids, gate_pre, up_pre, w_gate, w_up, w_down
+        )
+
+    def along(x, shift):
+        pairs = [(i, (i + 2 * shift) % cuts) for i in range(cuts)]
+        return lax.ppermute(x, "cuts", pairs)
+
+    def swap(x):
+        return lax.ppermute(x, "cuts", [(i, i ^ 1) for i in range(cuts)])
+
+    def exchange(pieces):
+        moved = [
+            lax.ppermute(pieces[r], "expert", [(i, i ^ r) for i in range(experts)])
+            for r in range(1, experts)
+        ]
+        return [pieces[0]] + moved
+
+    near = [1, line - 1]
+    far = [2]
+    raws = [along(out_grad, shift) for shift in near]
+    sel, gate, again, *pieces, t = first_pack(
+        out_grad, expert_ids.T, gate_probs.T, experts, capacity
+    )
+    pieces0 = exchange(pieces)
+    raw2 = along(again, 2)
+    up_factor, gate_factor, act, t = activations(gate_pre, up_pre, [t])
+    mine0 = jnp.concatenate(pieces0, axis=1)
+    theirs0 = swap(mine0)
+    total, t = hidden_part(mine0, w_down, [0], line, False, None, (), [t])
+    *pieces, t = pack(raws, sel, gate, experts, capacity, [t])
+    pieces1 = exchange(pieces)
+    total, t = hidden_part(theirs0, w_down, [0], line, True, total, (), [t])
+    down, t = down_part(act, mine0, theirs0, [0], line, None, w_down.shape, [t])
+    *pieces, t = pack([raw2], sel, gate, experts, capacity, [t])
+    pieces2 = exchange(pieces)
+    mine1 = jnp.concatenate(pieces1, axis=1)
+    theirs1 = swap(mine1)
+    total, t = hidden_part(mine1, w_down, near, line, False, total, (), [t])
+    total, t = hidden_part(theirs1, w_down, near, line, True, total, (), [t])
+    mine2 = jnp.concatenate(pieces2, axis=1)
+    theirs2 = swap(mine2)
+    total, t = hidden_part(mine2, w_down, far, line, False, total, (), [t])
+    gate_grad, up_grad, t = hidden_part(
+        theirs2, w_down, far, line, True, total, (gate_factor, up_factor), [t]
+    )
+
+    back = functools.partial(slot_part, gate_grad, up_grad, w_gate, w_up)
+    part2, t = back(far, line, True, None, experts, [t])
+    other2 = swap(part2)
+    part1, t = back(near, line, True, None, experts, [t])
+    other1 = swap(part1)
+    *send2, t = back(far, line, False, other2, experts, [t])
+    got2 = exchange(send2)
+    part0, t = back([0], line, True, None, experts, [t])
+    other0 = swap(part0)
+    far_out, t = combine(got2, sel, [], [t])
+    landed = [along(far_out, 2)]
+    *send1, t = back(near, line, False, other1, experts, [t])
+    got1 = exchange(send1)
+    *send0, t = back([0], line, False, other0, experts, [t])
+    got0 = exchange(send0)
+    down, t = down_part(act, mine1, theirs1, near, line, down, w_down.shape, [t])
+    *near_out, t = combine(got1, sel, [], [t])
+    landed += [along(part, shift) for part, shift in zip(near_out, near)]
+    down, t = down_part(act, mine2, theirs2, far, line, down, w_down.shape, [t])
+    result, t = combine(got0, sel, landed, [t])
+    return result, down
+
+
 def solution(mesh):
     return jax.shard_map(
         on_device,

time: 200 us -> 104 us (0.52)
  matrix products: 43.1 us -> 0 us
  blocking collectives: 40.5 us -> 0 us
  waiting for transfers between devices: 59.3 us -> 25.9 us
  starting transfers between devices: 3.76 us -> 34.5 us
  Pallas kernels: 0 us -> 28.6 us
  between operations: 14.2 us -> 1.07 us
  other arithmetic: 12.7 us -> 0.01 us
  local copies, waits for them, and re-layouts: 25.5 us -> 13.4 us
    dot_general x4 -> x0, matrix products: 43.1 us -> none  [the longest x1 14.7 us: on_device(): lax.dot_general(up_weight, up_grad, contract_last, preferred_element_type...]
    all_to_all x1 -> x0, blocking collectives: 40.5 us -> none  [on_device(): lax.all_to_all(outgoing, 'expert', split_axis=0, concat_axis=0, tiled=True)]
    reduce_scatter x1 -> x0, waiting for transfers between devices: 35.2 us -> none  [on_device(): lax.psum_scatter(lax.optimization_barrier(partial_value.astype(jnp.bfloat...]
    ppermute x0 -> x30, starting transfers between devices: none -> 34.5 us  [the longest x18 21.2 us: exchange(): lax.ppermute(pieces[r], 'expert', [(i, i ^ r) for i in range(experts)])]
    pallas_call x0 -> x22, Pallas kernels: none -> 28.6 us  [call(): pl.pallas_call(body, out_shape=out_shape, in_specs=list(specs) + [VMEM] *...]
    ppermute x0 -> x30, waiting for transfers between devices: none -> 25.9 us  [the longest x18 23.5 us: exchange(): lax.ppermute(pieces[r], 'expert', [(i, i ^ r) for i in range(experts)])]
    all_gather x1 -> x0, waiting for transfers between devices: 23.3 us -> none  [on_device(): features = lax.all_gather(out_grad, 'cuts', axis=1, tiled=True)]
    mul x5 -> x0, local copies, waits for them, and re-layouts: 15.5 us -> none  [the longest x3 15.2 us: pack_rows(): gate_values[:, :, None] * out_rows[:, None, :].astype(jnp.float32)]
  transfers between devices with their start and end apart: 3 -> 30, of which waited for: 2 -> 12; matrix products, arithmetic and copies ran while one was open for 9% -> 0% of each run, Pallas kernels for 0% -> 22%
where the time goes in v2:
time: 104 us; the launch traced here: 103 us
  starting transfers between devices  34.5 us (33%)
  Pallas kernels  28.6 us (28%)
  waiting for transfers between devices  25.9 us (25%)
  local copies, waits for them, and re-layouts  13.4 us (13%)
  between operations  1.07 us (1%)
    pallas_call x22, Pallas kernels, call(): pl.pallas_call(body, out_shape=out_shape, in_specs=list(specs) + [VMEM] *...  28.6 us
    ppermute x18, waiting for transfers between devices, exchange(): lax.ppermute(pieces[r], 'expert', [(i, i ^ r) for i in range(experts)])  23.5 us
    ppermute x18, starting transfers between devices, exchange(): lax.ppermute(pieces[r], 'expert', [(i, i ^ r) for i in range(experts)])  21.2 us
    unnamed x35, local copies, waits for them, and re-layouts  13.4 us
    ppermute x6, starting transfers between devices, along(): return lax.ppermute(x, 'cuts', pairs)  12.1 us
    ppermute x6, waiting for transfers between devices, swap(): return lax.ppermute(x, 'cuts', [(i, i ^ 1) for i in range(cuts)])  2.41 us
  transfers between devices with their start and end apart: 30, of which 12 were waited for; matrix products, arithmetic and copies ran while one was open for 0% of the time, Pallas kernels for 22%

profile of v2, /device:TPU:0, one launch (start us, length us, event | category | flops | bytes accessed | tf_op | source)
XLA Modules:
  0.0 103.5 jit_solution(17248479085954100817)
XLA Ops:
  0.6 3.1 %collective-permute-start.5 = (bf16[128,768]{1,0:T(8,128)(2,1)}, bf16[128,768]{1,0:T(8,128)(2,1)S(1)}, u32[]{:S(2)}, u32[]{:S(2)}) collective-permute-start(bf16[128,768]{1,0:T(8,128)(2,1)} %refs_0_.2), channel_id=1, source_target_pairs={{0,2},{1,3},{2,4},{3,5},{4,6},{5,7},{6,0},{7,1},{8,10},{9,11},{10,... | collective-permute-start | bytes 589832 | tf_op jit(solution)/shard_map/ppermute | solution.py:402
  3.7 2.1 %collective-permute-start.6 = (bf16[128,768]{1,0:T(8,128)(2,1)}, bf16[128,768]{1,0:T(8,128)(2,1)S(1)}, u32[]{:S(2)}, u32[]{:S(2)}) collective-permute-start(bf16[128,768]{1,0:T(8,128)(2,1)} %refs_0_.2), channel_id=1, source_target_pairs={{0,6},{1,7},{2,0},{3,1},{4,2},{5,3},{6,4},{7,5},{8,14},{9,15},{10,... | collective-permute-start | bytes 589832 | tf_op jit(solution)/shard_map/ppermute | solution.py:402
  5.8 1.0 copy-done.4
  8.5 1.7 %collective-permute-start.1 = (bf16[1,64,768]{2,1,0:T(8,128)(2,1)S(1)}, bf16[1,64,768]{2,1,0:T(8,128)(2,1)S(1)}, u32[]{:S(2)}, u32[]{:S(2)}) collective-permute-start(bf16[1,64,768]{2,1,0:T(8,128)(2,1)S(1)} %get-tuple-element.76), channel_id=1, source_target_pairs={{0,8},{8,0},{16,24},{24,16},{1,9},{9,1},{17,25},{25,17},{2,10},{10... | collective-permute-start | bytes 294920 | tf_op jit(solution)/shard_map/ppermute | solution.py:409
  10.2 1.5 %collective-permute-start.2 = (bf16[1,64,768]{2,1,0:T(8,128)(2,1)S(1)}, bf16[1,64,768]{2,1,0:T(8,128)(2,1)S(1)}, u32[]{:S(2)}, u32[]{:S(2)}) collective-permute-start(bf16[1,64,768]{2,1,0:T(8,128)(2,1)S(1)} %get-tuple-element.77), channel_id=1, source_target_pairs={{0,16},{8,24},{16,0},{24,8},{1,17},{9,25},{17,1},{25,9},{2,18},{10... | collective-permute-start | bytes 294920 | tf_op jit(solution)/shard_map/ppermute | solution.py:409
  12.1 1.0 %copy-done.2 = bf16[1,4,64,1024]{3,2,1,0:T(8,128)(2,1)S(1)} copy-done((bf16[1,4,64,1024]{3,2,1,0:T(8,128)(2,1)S(1)}, bf16[1,4,64,1024]{3,2,1,0:T(8,128)(2,1)}, u32[]{:S(2)}) %copy-start.2) | copy-done | bytes 524312
  13.1 1.0 %copy-done.3 = bf16[1,4,64,1024]{3,2,1,0:T(8,128)(2,1)S(1)} copy-done((bf16[1,4,64,1024]{3,2,1,0:T(8,128)(2,1)S(1)}, bf16[1,4,64,1024]{3,2,1,0:T(8,128)(2,1)}, u32[]{:S(2)}) %copy-start.3) | copy-done | bytes 524312
  15.9 1.4 %collective-permute-done.3 = bf16[1,64,768]{2,1,0:T(8,128)(2,1)S(1)} collective-permute-done((bf16[1,64,768]{2,1,0:T(8,128)(2,1)S(1)}, bf16[1,64,768]{2,1,0:T(8,128)(2,1)S(1)}, u32[]{:S(2)}, u32[]{:S(2)}) %collective-permute-start.3) | collective-permute-done | bytes 98336 | tf_op jit(solution)/shard_map/ppermute | solution.py:409
  17.3 4.6 %copy-done = bf16[1,1024,6144]{2,1,0:T(8,128)(2,1)S(1)} copy-done((bf16[1,1024,6144]{2,1,0:T(8,128)(2,1)S(1)}, bf16[1,1024,6144]{2,1,0:T(8,128)(2,1)}, u32[]{:S(2)}) %copy-start) | copy-done | bytes 12582936
  21.9 1.2 %hidden_part.6 = (f32[1024,256]{1,0:T(8,128)S(1)}, f32[8,128]{1,0:T(8,128)S(1)}) custom-call(bf16[1,256,768]{2,1,0:T(8,128)(2,1)S(1)} %constant_dynamic-update-slice_fusion.refs_0_.refs_1_, bf16[1,1024,6144]{2,1,0:T(8,128)(2,1)S(1)} %copy-done, f32[8,128]{1,0:T(8,128)S(1)} %get-tuple-element.79.refs_2_), custom_call_target="tpu_custom_call" | custom-call | flops 402653184 | bytes 3670016 | tf_op jit(solution)/shard_map/hidden_part/pallas_call | solution.py:38
  25.6 2.3 %collective-permute-start.13 = (bf16[2,64,768]{2,1,0:T(8,128)(2,1)S(1)}, bf16[2,64,768]{2,1,0:T(8,128)(2,1)S(1)}, u32[]{:S(2)}, u32[]{:S(2)}) collective-permute-start(bf16[2,64,768]{2,1,0:T(8,128)(2,1)S(1)} %get-tuple-element.92), channel_id=1, source_target_pairs={{0,24},{8,16},{16,8},{24,0},{1,25},{9,17},{17,9},{25,1},{2,26},{10... | collective-permute-start | bytes 589832 | tf_op jit(solution)/shard_map/ppermute | solution.py:409
  27.9 1.3 %collective-permute-done.11 = bf16[2,64,768]{2,1,0:T(8,128)(2,1)S(1)} collective-permute-done((bf16[2,64,768]{2,1,0:T(8,128)(2,1)S(1)}, bf16[2,64,768]{2,1,0:T(8,128)(2,1)S(1)}, u32[]{:S(2)}, u32[]{:S(2)}) %collective-permute-start.11) | collective-permute-done | bytes 196640 | tf_op jit(solution)/shard_map/ppermute | solution.py:409
  29.2 7.2 %collective-permute-done.12 = bf16[2,64,768]{2,1,0:T(8,128)(2,1)S(1)} collective-permute-done((bf16[2,64,768]{2,1,0:T(8,128)(2,1)S(1)}, bf16[2,64,768]{2,1,0:T(8,128)(2,1)S(1)}, u32[]{:S(2)}, u32[]{:S(2)}) %collective-permute-start.12) | collective-permute-done | bytes 196640 | tf_op jit(solution)/shard_map/ppermute | solution.py:409
  36.5 1.2 %hidden_part.7 = (f32[1024,256]{1,0:T(8,128)S(1)}, f32[8,128]{1,0:T(8,128)S(1)}) custom-call(bf16[1,256,768]{2,1,0:T(8,128)(2,1)S(1)} %collective-permute-done.4.refs_0_.refs_2_, bf16[1,1024,6144]{2,1,0:T(8,128)(2,1)S(1)} %copy-done.1, f32[1024,256]{1,0:T(8,128)S(1)} %get-tuple-element.80.refs_2_, f32[8,128]{1,0:T(8,128)S(1)} %get-tuple-element.82.refs_3_), custom_call_target="tpu_custom_call" | custom-call | flops 402653184 | bytes 3670016 | tf_op jit(solution)/shard_map/hidden_part/pallas_call | solution.py:38
  37.8 2.0 %down_part.3 = (bf16[1,1024,6144]{2,1,0:T(8,128)(2,1)}, f32[8,128]{1,0:T(8,128)S(1)}) custom-call(bf16[1024,256]{1,0:T(8,128)(2,1)S(1)} %get-tuple-element.74.refs_0_, bf16[1,256,768]{2,1,0:T(8,128)(2,1)S(1)} %constant_dynamic-update-slice_fusion.refs_0_.refs_1_, bf16[1,256,768]{2,1,0:T(8,128)(2,1)S(1)} %collective-permute-done.4.refs_0_.refs_2_, ...), custom_call_target="tpu_custom_call" | custom-call | flops 805306368 | bytes 3145728 | tf_op jit(solution)/shard_map/down_part/pallas_call | solution.py:38
  40.1 1.6 %collective-permute-start.7 = (bf16[1,64,768]{2,1,0:T(8,128)(2,1)S(1)}, bf16[1,64,768]{2,1,0:T(8,128)(2,1)S(1)}, u32[]{:S(2)}, u32[]{:S(2)}) collective-permute-start(bf16[1,64,768]{2,1,0:T(8,128)(2,1)S(1)} %get-tuple-element.86), channel_id=1, source_target_pairs={{0,8},{8,0},{16,24},{24,16},{1,9},{9,1},{17,25},{25,17},{2,10},{10... | collective-permute-start | bytes 294920 | tf_op jit(solution)/shard_map/ppermute | solution.py:409
  42.4 1.3 %collective-permute-start.9 = (bf16[1,64,768]{2,1,0:T(8,128)(2,1)S(1)}, bf16[1,64,768]{2,1,0:T(8,128)(2,1)S(1)}, u32[]{:S(2)}, u32[]{:S(2)}) collective-permute-start(bf16[1,64,768]{2,1,0:T(8,128)(2,1)S(1)} %get-tuple-element.88), channel_id=1, source_target_pairs={{0,24},{8,16},{16,8},{24,0},{1,25},{9,17},{17,9},{25,1},{2,26},{10... | collective-permute-start | bytes 294920 | tf_op jit(solution)/shard_map/ppermute | solution.py:409
  43.6 1.7 %collective-permute-done.7 = bf16[1,64,768]{2,1,0:T(8,128)(2,1)S(1)} collective-permute-done((bf16[1,64,768]{2,1,0:T(8,128)(2,1)S(1)}, bf16[1,64,768]{2,1,0:T(8,128)(2,1)S(1)}, u32[]{:S(2)}, u32[]{:S(2)}) %collective-permute-start.7) | collective-permute-done | bytes 98336 | tf_op jit(solution)/shard_map/ppermute | solution.py:409
  45.4 3.3 %collective-permute-done.8 = bf16[1,64,768]{2,1,0:T(8,128)(2,1)S(1)} collective-permute-done((bf16[1,64,768]{2,1,0:T(8,128)(2,1)S(1)}, bf16[1,64,768]{2,1,0:T(8,128)(2,1)S(1)}, u32[]{:S(2)}, u32[]{:S(2)}) %collective-permute-start.8) | collective-permute-done | bytes 98336 | tf_op jit(solution)/shard_map/ppermute | solution.py:409
  48.8 1.7 %hidden_part.8 = (f32[1024,256]{1,0:T(8,128)S(1)}, f32[8,128]{1,0:T(8,128)S(1)}) custom-call(bf16[2,256,768]{2,1,0:T(8,128)(2,1)S(1)} %constant_dynamic-update-slice_fusion.8.refs_0_.refs_1_, bf16[1,1024,6144]{2,1,0:T(8,128)(2,1)S(1)} %copy-done.1, f32[1024,256]{1,0:T(8,128)S(1)} %get-tuple-element.93.refs_2_, f32[8,128]{1,0:T(8,128)S(1)} %get-tuple-element.94.refs_3_), custom_call_target="tpu_custom_call" | custom-call | flops 805306368 | bytes 5242880 | tf_op jit(solution)/shard_map/hidden_part/pallas_call | solution.py:38
  50.5 1.7 %hidden_part.9 = (f32[1024,256]{1,0:T(8,128)S(1)}, f32[8,128]{1,0:T(8,128)S(1)}) custom-call(bf16[2,256,768]{2,1,0:T(8,128)(2,1)S(1)} %collective-permute-done.14.refs_0_.refs_2_, bf16[1,1024,6144]{2,1,0:T(8,128)(2,1)S(1)} %copy-done.1, f32[1024,256]{1,0:T(8,128)S(1)} %get-tuple-element.95.refs_2_, f32[8,128]{1,0:T(8,128)S(1)} %get-tuple-element.96.refs_3_), custom_call_target="tpu_custom_call" | custom-call | flops 805306368 | bytes 5242880 | tf_op jit(solution)/shard_map/hidden_part/pallas_call | solution.py:38
  52.2 1.2 %hidden_part.10 = (f32[1024,256]{1,0:T(8,128)S(1)}, f32[8,128]{1,0:T(8,128)S(1)}) custom-call(bf16[1,256,768]{2,1,0:T(8,128)(2,1)S(1)} %constant_dynamic-update-slice_fusion.4.refs_0_.refs_1_, bf16[1,1024,6144]{2,1,0:T(8,128)(2,1)S(1)} %copy-done.1, f32[1024,256]{1,0:T(8,128)S(1)} %get-tuple-element.97.refs_2_, f32[8,128]{1,0:T(8,128)S(1)} %get-tuple-element.98.refs_3_), custom_call_target="tpu_custom_call" | custom-call | flops 402653184 | bytes 3670016 | tf_op jit(solution)/shard_map/hidden_part/pallas_call | solution.py:38
  53.5 1.6 %hidden_part.11 = (bf16[1024,256]{1,0:T(8,128)(2,1)S(1)}, bf16[1024,256]{1,0:T(8,128)(2,1)S(1)}, f32[8,128]{1,0:T(8,128)S(1)}) custom-call(bf16[1,256,768]{2,1,0:T(8,128)(2,1)S(1)} %collective-permute-done.10.refs_0_.refs_2_, bf16[1,1024,6144]{2,1,0:T(8,128)(2,1)S(1)} %copy-done.1, f32[1024,256]{1,0:T(8,128)S(1)} %get-tuple-element.99.refs_2_, ...), custom_call_target="tpu_custom_call" | custom-call | flops 402653184 | bytes 3670016 | tf_op jit(solution)/shard_map/hidden_part/pallas_call | solution.py:38
  55.7 1.2 %slice-done.4 = s8[4194304]{0:T(1024)(128)(4,1)S(1)} async-done(((s8[12582912]{0:T(1024)(128)(4,1)}), s8[4194304]{0:T(1024)(128)(4,1)S(1)}, s32[]{:S(2)}) %slice-start.4) | async-done | bytes 4194328
  56.9 1.3 %slice-done.2 = s8[4194304]{0:T(1024)(128)(4,1)S(1)} async-done(((s8[12582912]{0:T(1024)(128)(4,1)}), s8[4194304]{0:T(1024)(128)(4,1)S(1)}, s32[]{:S(2)}) %slice-start.2) | async-done | bytes 4194328
  58.2 1.2 %slice-done.5 = s8[4194304]{0:T(1024)(128)(4,1)S(1)} async-done(((s8[12582912]{0:T(1024)(128)(4,1)}), s8[4194304]{0:T(1024)(128)(4,1)S(1)}, s32[]{:S(2)}) %slice-start.5) | async-done | bytes 4194328
  59.4 1.1 %slot_part.6 = (bf16[1,256,768]{2,1,0:T(8,128)(2,1)S(1)}, f32[8,128]{1,0:T(8,128)S(1)}) custom-call(bf16[1024,256]{1,0:T(8,128)(2,1)S(1)} %get-tuple-element.103.refs_0_, bf16[1024,256]{1,0:T(8,128)(2,1)S(1)} %get-tuple-element.104.refs_1_, bf16[1,6144,1024]{2,1,0:T(8,128)(2,1)S(1)} %bitcast.3, bf16[1,6144,1024]{2,1,0:T(8,128)(2,1)S(1)} %bitcast.5, ...), custom_call_target="tpu_custom_call" | custom-call | flops 805306368 | bytes 4194304 | tf_op jit(solution)/shard_map/slot_part/pallas_call | solution.py:38
  60.5 1.9 %slot_part.7 = (bf16[2,256,768]{2,1,0:T(8,128)(2,1)S(1)}, f32[8,128]{1,0:T(8,128)S(1)}) custom-call(bf16[1024,256]{1,0:T(8,128)(2,1)S(1)} %get-tuple-element.103.refs_0_, bf16[1024,256]{1,0:T(8,128)(2,1)S(1)} %get-tuple-element.104.refs_1_, bf16[1,6144,1024]{2,1,0:T(8,128)(2,1)S(1)} %bitcast.3, bf16[1,6144,1024]{2,1,0:T(8,128)(2,1)S(1)} %bitcast.5, ...), custom_call_target="tpu_custom_call" | custom-call | flops 1610612736 | bytes 7340032 | tf_op jit(solution)/shard_map/slot_part/pallas_call | solution.py:38
  63.0 2.4 %collective-permute-done.15.refs_4_ = bf16[1,256,768]{2,1,0:T(8,128)(2,1)S(1)} collective-permute-done((bf16[1,256,768]{2,1,0:T(8,128)(2,1)S(1)}, bf16[1,256,768]{2,1,0:T(8,128)(2,1)S(1)}, u32[]{:S(2)}, u32[]{:S(2)}) %collective-permute-start.15) | collective-permute-done | bytes 393248 | tf_op jit(solution)/shard_map/ppermute | solution.py:405
  65.4 1.1 %slot_part.8 = (bf16[1,64,768]{2,1,0:T(8,128)(2,1)S(1)}, bf16[1,64,768]{2,1,0:T(8,128)(2,1)S(1)}, bf16[1,64,768]{2,1,0:T(8,128)(2,1)S(1)}, bf16[1,64,768]{2,1,0:T(8,128)(2,1)S(1)}, f32[8,128]{1,0:T(8,128)S(1)}) custom-call(bf16[1024,256]{1,0:T(8,128)(2,1)S(1)} %get-tuple-element.103.refs_0_, bf16[1024,256]{1,0:T(8,128)(2,1)S(1)} %get-tuple-element.104.refs_1_, ...), custom_call_target="tpu_custom_call" | custom-call | flops 805306368 | bytes 4194304 | tf_op jit(solution)/shard_map/slot_part/pallas_call | solution.py:38
  66.6 1.1 %slot_part.9 = (bf16[1,256,768]{2,1,0:T(8,128)(2,1)S(1)}, f32[8,128]{1,0:T(8,128)S(1)}) custom-call(bf16[1024,256]{1,0:T(8,128)(2,1)S(1)} %get-tuple-element.103.refs_0_, bf16[1024,256]{1,0:T(8,128)(2,1)S(1)} %get-tuple-element.104.refs_1_, bf16[1,6144,1024]{2,1,0:T(8,128)(2,1)S(1)} %bitcast.3, bf16[1,6144,1024]{2,1,0:T(8,128)(2,1)S(1)} %bitcast.5, ...), custom_call_target="tpu_custom_call" | custom-call | flops 805306368 | bytes 4194304 | tf_op jit(solution)/shard_map/slot_part/pallas_call | solution.py:38
  68.6 1.2 %collective-permute-start.19 = (bf16[1,64,768]{2,1,0:T(8,128)(2,1)S(1)}, bf16[1,64,768]{2,1,0:T(8,128)(2,1)S(1)}, u32[]{:S(2)}, u32[]{:S(2)}) collective-permute-start(bf16[1,64,768]{2,1,0:T(8,128)(2,1)S(1)} %get-tuple-element.114), channel_id=1, source_target_pairs={{0,16},{8,24},{16,0},{24,8},{1,17},{9,25},{17,1},{25,9},{2,18},{10... | collective-permute-start | bytes 294920 | tf_op jit(solution)/shard_map/ppermute | solution.py:409
  69.8 1.8 %collective-permute-start.20 = (bf16[1,64,768]{2,1,0:T(8,128)(2,1)S(1)}, bf16[1,64,768]{2,1,0:T(8,128)(2,1)S(1)}, u32[]{:S(2)}, u32[]{:S(2)}) collective-permute-start(bf16[1,64,768]{2,1,0:T(8,128)(2,1)S(1)} %get-tuple-element.115), channel_id=1, source_target_pairs={{0,24},{8,16},{16,8},{24,0},{1,25},{9,17},{17,9},{25,1},{2,26},{10... | collective-permute-start | bytes 294920 | tf_op jit(solution)/shard_map/ppermute | solution.py:409
  71.6 2.1 %collective-permute-done.18.refs_1_ = bf16[1,64,768]{2,1,0:T(8,128)(2,1)S(1)} collective-permute-done((bf16[1,64,768]{2,1,0:T(8,128)(2,1)S(1)}, bf16[1,64,768]{2,1,0:T(8,128)(2,1)S(1)}, u32[]{:S(2)}, u32[]{:S(2)}) %collective-permute-start.18) | collective-permute-done | bytes 98336 | tf_op jit(solution)/shard_map/ppermute | solution.py:409
  74.3 1.0 collective-permute-done.20.refs_3_
  75.6 2.2 %collective-permute-start.24 = (bf16[128,768]{1,0:T(8,128)(2,1)S(1)}, bf16[128,768]{1,0:T(8,128)(2,1)S(1)}, u32[]{:S(2)}, u32[]{:S(2)}) collective-permute-start(bf16[128,768]{1,0:T(8,128)(2,1)S(1)} %get-tuple-element.123), channel_id=1, source_target_pairs={{0,4},{1,5},{2,6},{3,7},{4,0},{5,1},{6,2},{7,3},{8,12},{9,13},{10,... | collective-permute-start | bytes 589832 | tf_op jit(solution)/shard_map/ppermute | solution.py:402
  77.8 2.0 %slot_part.10 = (bf16[2,64,768]{2,1,0:T(8,128)(2,1)S(1)}, bf16[2,64,768]{2,1,0:T(8,128)(2,1)S(1)}, bf16[2,64,768]{2,1,0:T(8,128)(2,1)S(1)}, bf16[2,64,768]{2,1,0:T(8,128)(2,1)S(1)}, f32[8,128]{1,0:T(8,128)S(1)}) custom-call(bf16[1024,256]{1,0:T(8,128)(2,1)S(1)} %get-tuple-element.103.refs_0_, bf16[1024,256]{1,0:T(8,128)(2,1)S(1)} %get-tuple-element.104.refs_1_, ...), custom_call_target="tpu_custom_call" | custom-call | flops 1610612736 | bytes 7340032 | tf_op jit(solution)/shard_map/slot_part/pallas_call | solution.py:38
  79.8 1.6 %collective-permute-start.25 = (bf16[2,64,768]{2,1,0:T(8,128)(2,1)S(1)}, bf16[2,64,768]{2,1,0:T(8,128)(2,1)S(1)}, u32[]{:S(2)}, u32[]{:S(2)}) collective-permute-start(bf16[2,64,768]{2,1,0:T(8,128)(2,1)S(1)} %get-tuple-element.125), channel_id=1, source_target_pairs={{0,8},{8,0},{16,24},{24,16},{1,9},{9,1},{17,25},{25,17},{2,10},{10... | collective-permute-start | bytes 589832 | tf_op jit(solution)/shard_map/ppermute | solution.py:409
  82.1 1.2 %collective-permute-start.27 = (bf16[2,64,768]{2,1,0:T(8,128)(2,1)S(1)}, bf16[2,64,768]{2,1,0:T(8,128)(2,1)S(1)}, u32[]{:S(2)}, u32[]{:S(2)}) collective-permute-start(bf16[2,64,768]{2,1,0:T(8,128)(2,1)S(1)} %get-tuple-element.127), channel_id=1, source_target_pairs={{0,24},{8,16},{16,8},{24,0},{1,25},{9,17},{17,9},{25,1},{2,26},{10... | collective-permute-start | bytes 589832 | tf_op jit(solution)/shard_map/ppermute | solution.py:409
  83.3 1.1 %slot_part.11 = (bf16[1,64,768]{2,1,0:T(8,128)(2,1)S(1)}, bf16[1,64,768]{2,1,0:T(8,128)(2,1)S(1)}, bf16[1,64,768]{2,1,0:T(8,128)(2,1)S(1)}, bf16[1,64,768]{2,1,0:T(8,128)(2,1)S(1)}, f32[8,128]{1,0:T(8,128)S(1)}) custom-call(bf16[1024,256]{1,0:T(8,128)(2,1)S(1)} %get-tuple-element.103.refs_0_, bf16[1024,256]{1,0:T(8,128)(2,1)S(1)} %get-tuple-element.104.refs_1_, ...), custom_call_target="tpu_custom_call" | custom-call | flops 805306368 | bytes 4194304 | tf_op jit(solution)/shard_map/slot_part/pallas_call | solution.py:38
  84.5 4.3 %down_part.4 = (bf16[1,1024,6144]{2,1,0:T(8,128)(2,1)}, f32[8,128]{1,0:T(8,128)S(1)}) custom-call(bf16[1024,256]{1,0:T(8,128)(2,1)S(1)} %get-tuple-element.74.refs_0_, bf16[2,256,768]{2,1,0:T(8,128)(2,1)S(1)} %constant_dynamic-update-slice_fusion.8.refs_0_.refs_1_, ...), custom_call_target="tpu_custom_call", output_to_operand_aliasing={{0}: (3, {})} | custom-call | flops 1610612736 | bytes 6291456 | tf_op jit(solution)/shard_map/down_part/pallas_call | solution.py:38
  88.8 2.2 %collective-permute-done.26.refs_2_ = bf16[2,64,768]{2,1,0:T(8,128)(2,1)S(1)} collective-permute-done((bf16[2,64,768]{2,1,0:T(8,128)(2,1)S(1)}, bf16[2,64,768]{2,1,0:T(8,128)(2,1)S(1)}, u32[]{:S(2)}, u32[]{:S(2)}) %collective-permute-start.26) | collective-permute-done | bytes 196640 | tf_op jit(solution)/shard_map/ppermute | solution.py:409
  91.3 3.8 %collective-permute-start.29 = (bf16[128,768]{1,0:T(8,128)(2,1)S(1)}, bf16[128,768]{1,0:T(8,128)(2,1)S(1)}, u32[]{:S(2)}, u32[]{:S(2)}) collective-permute-start(bf16[128,768]{1,0:T(8,128)(2,1)S(1)} %get-tuple-element.132), channel_id=1, source_target_pairs={{0,6},{1,7},{2,0},{3,1},{4,2},{5,3},{6,4},{7,5},{8,14},{9,15},{10,... | collective-permute-start | bytes 589832 | tf_op jit(solution)/shard_map/ppermute | solution.py:402
  95.7 1.4 %collective-permute-start.22 = (bf16[1,64,768]{2,1,0:T(8,128)(2,1)S(1)}, bf16[1,64,768]{2,1,0:T(8,128)(2,1)S(1)}, u32[]{:S(2)}, u32[]{:S(2)}) collective-permute-start(bf16[1,64,768]{2,1,0:T(8,128)(2,1)S(1)} %get-tuple-element.121), channel_id=1, source_target_pairs={{0,16},{8,24},{16,0},{24,8},{1,17},{9,25},{17,1},{25,9},{2,18},{10... | collective-permute-start | bytes 294920 | tf_op jit(solution)/shard_map/ppermute | solution.py:409
  97.0 1.6 %collective-permute-start.23 = (bf16[1,64,768]{2,1,0:T(8,128)(2,1)S(1)}, bf16[1,64,768]{2,1,0:T(8,128)(2,1)S(1)}, u32[]{:S(2)}, u32[]{:S(2)}) collective-permute-start(bf16[1,64,768]{2,1,0:T(8,128)(2,1)S(1)} %get-tuple-element.122), channel_id=1, source_target_pairs={{0,24},{8,16},{16,8},{24,0},{1,25},{9,17},{17,9},{25,1},{2,26},{10... | collective-permute-start | bytes 294920 | tf_op jit(solution)/shard_map/ppermute | solution.py:409
  98.6 2.0 %down_part.5 = (bf16[1,1024,6144]{2,1,0:T(8,128)(2,1)}, f32[8,128]{1,0:T(8,128)S(1)}) custom-call(bf16[1024,256]{1,0:T(8,128)(2,1)S(1)} %get-tuple-element.74.refs_0_, bf16[1,256,768]{2,1,0:T(8,128)(2,1)S(1)} %constant_dynamic-update-slice_fusion.4.refs_0_.refs_1_, ...), custom_call_target="tpu_custom_call", output_to_operand_aliasing={{0}: (3, {})} | custom-call | flops 805306368 | bytes 3145728 | tf_op jit(solution)/shard_map/down_part/pallas_call | solution.py:38
  100.7 1.9 %collective-permute-done.23.refs_3_ = bf16[1,64,768]{2,1,0:T(8,128)(2,1)S(1)} collective-permute-done((bf16[1,64,768]{2,1,0:T(8,128)(2,1)S(1)}, bf16[1,64,768]{2,1,0:T(8,128)(2,1)S(1)}, u32[]{:S(2)}, u32[]{:S(2)}) %collective-permute-start.23) | collective-permute-done | bytes 98336 | tf_op jit(solution)/shard_map/ppermute | solution.py:409
  102.5 0.9 combine.5
  (74 shorter events, 12.3 us)
Async XLA Ops:
  0.6 22.5 %collective-permute-start.5 = (bf16[128,768]{1,0:T(8,128)(2,1)}, bf16[128,768]{1,0:T(8,128)(2,1)S(1)}, u32[]{:S(2)}, u32[]{:S(2)}) collective-permute-start(bf16[128,768]{1,0:T(8,128)(2,1)} %refs_0_.2), channel_id=1, source_target_pairs={{0,2},{1,3},{2,4},{3,5},{4,6},{5,7},{6,0},{7,1},{8,10},{9,11},{10,... | collective-permute-start | bytes 589832 | tf_op jit(solution)/shard_map/ppermute | solution.py:402
  3.7 19.4 %collective-permute-start.6 = (bf16[128,768]{1,0:T(8,128)(2,1)}, bf16[128,768]{1,0:T(8,128)(2,1)S(1)}, u32[]{:S(2)}, u32[]{:S(2)}) collective-permute-start(bf16[128,768]{1,0:T(8,128)(2,1)} %refs_0_.2), channel_id=1, source_target_pairs={{0,6},{1,7},{2,0},{3,1},{4,2},{5,3},{6,4},{7,5},{8,14},{9,15},{10,... | collective-permute-start | bytes 589832 | tf_op jit(solution)/shard_map/ppermute | solution.py:402
  5.8 1.0 copy-start.4
  6.8 0.7 copy-start.5
  7.4 0.7 copy-start.6
  8.5 6.5 %collective-permute-start.1 = (bf16[1,64,768]{2,1,0:T(8,128)(2,1)S(1)}, bf16[1,64,768]{2,1,0:T(8,128)(2,1)S(1)}, u32[]{:S(2)}, u32[]{:S(2)}) collective-permute-start(bf16[1,64,768]{2,1,0:T(8,128)(2,1)S(1)} %get-tuple-element.76), channel_id=1, source_target_pairs={{0,8},{8,0},{16,24},{24,16},{1,9},{9,1},{17,25},{25,17},{2,10},{10... | collective-permute-start | bytes 294920 | tf_op jit(solution)/shard_map/ppermute | solution.py:409
  10.2 5.7 %collective-permute-start.2 = (bf16[1,64,768]{2,1,0:T(8,128)(2,1)S(1)}, bf16[1,64,768]{2,1,0:T(8,128)(2,1)S(1)}, u32[]{:S(2)}, u32[]{:S(2)}) collective-permute-start(bf16[1,64,768]{2,1,0:T(8,128)(2,1)S(1)} %get-tuple-element.77), channel_id=1, source_target_pairs={{0,16},{8,24},{16,0},{24,8},{1,17},{9,25},{17,1},{25,9},{2,18},{10... | collective-permute-start | bytes 294920 | tf_op jit(solution)/shard_map/ppermute | solution.py:409
  11.8 5.5 %collective-permute-start.3 = (bf16[1,64,768]{2,1,0:T(8,128)(2,1)S(1)}, bf16[1,64,768]{2,1,0:T(8,128)(2,1)S(1)}, u32[]{:S(2)}, u32[]{:S(2)}) collective-permute-start(bf16[1,64,768]{2,1,0:T(8,128)(2,1)S(1)} %get-tuple-element.78), channel_id=1, source_target_pairs={{0,24},{8,16},{16,8},{24,0},{1,25},{9,17},{17,9},{25,1},{2,26},{10... | collective-permute-start | bytes 294920 | tf_op jit(solution)/shard_map/ppermute | solution.py:409
  12.1 1.0 %copy-start.2 = (bf16[1,4,64,1024]{3,2,1,0:T(8,128)(2,1)S(1)}, bf16[1,4,64,1024]{3,2,1,0:T(8,128)(2,1)}, u32[]{:S(2)}) copy-start(bf16[1,4,64,1024]{3,2,1,0:T(8,128)(2,1)} %refs_0_.3) | copy-start | bytes 1572868
  13.1 1.0 %copy-start.3 = (bf16[1,4,64,1024]{3,2,1,0:T(8,128)(2,1)S(1)}, bf16[1,4,64,1024]{3,2,1,0:T(8,128)(2,1)}, u32[]{:S(2)}) copy-start(bf16[1,4,64,1024]{3,2,1,0:T(8,128)(2,1)} %refs_1_.7) | copy-start | bytes 1572868
  17.3 4.6 %copy-start = (bf16[1,1024,6144]{2,1,0:T(8,128)(2,1)S(1)}, bf16[1,1024,6144]{2,1,0:T(8,128)(2,1)}, u32[]{:S(2)}) copy-start(bf16[1,1024,6144]{2,1,0:T(8,128)(2,1)} %refs_1_.13) | copy-start | bytes 37748740
  21.9 14.7 %copy-start.1 = (bf16[1,1024,6144]{2,1,0:T(8,128)(2,1)S(1)}, bf16[1,1024,6144]{2,1,0:T(8,128)(2,1)}, u32[]{:S(2)}) copy-start(bf16[1,1024,6144]{2,1,0:T(8,128)(2,1)} %refs_1_.13) | copy-start | bytes 37748740
  23.5 5.7 %collective-permute-start.11 = (bf16[2,64,768]{2,1,0:T(8,128)(2,1)S(1)}, bf16[2,64,768]{2,1,0:T(8,128)(2,1)S(1)}, u32[]{:S(2)}, u32[]{:S(2)}) collective-permute-start(bf16[2,64,768]{2,1,0:T(8,128)(2,1)S(1)} %get-tuple-element.90), channel_id=1, source_target_pairs={{0,8},{8,0},{16,24},{24,16},{1,9},{9,1},{17,25},{25,17},{2,10},{10... | collective-permute-start | bytes 589832 | tf_op jit(solution)/shard_map/ppermute | solution.py:409
  24.1 15.8 %collective-permute-start = (bf16[128,768]{1,0:T(8,128)(2,1)S(1)}, bf16[128,768]{1,0:T(8,128)(2,1)S(1)}, u32[]{:S(2)}, u32[]{:S(2)}) collective-permute-start(bf16[128,768]{1,0:T(8,128)(2,1)S(1)} %get-tuple-element.70), channel_id=1, source_target_pairs={{0,4},{1,5},{2,6},{3,7},{4,0},{5,1},{6,2},{7,3},{8,12},{9,13},{10,... | collective-permute-start | bytes 589832 | tf_op jit(solution)/shard_map/ppermute | solution.py:402
  24.9 11.7 %collective-permute-start.4 = (bf16[1,256,768]{2,1,0:T(8,128)(2,1)S(1)}, bf16[1,256,768]{2,1,0:T(8,128)(2,1)S(1)}, u32[]{:S(2)}, u32[]{:S(2)}) collective-permute-start(bf16[1,256,768]{2,1,0:T(8,128)(2,1)S(1)} %constant_dynamic-update-slice_fusion.refs_0_.refs_1_), channel_id=1, source_target_pairs={{0,1},{1,0},{2,3},{3,2},{4,5},{5,4},{6,7},{7,6},{8,9},{9,8},{10,11... | collective-permute-start | bytes 1179656 | tf_op jit(solution)/shard_map/ppermute | solution.py:405
  24.9 11.5 %collective-permute-start.12 = (bf16[2,64,768]{2,1,0:T(8,128)(2,1)S(1)}, bf16[2,64,768]{2,1,0:T(8,128)(2,1)S(1)}, u32[]{:S(2)}, u32[]{:S(2)}) collective-permute-start(bf16[2,64,768]{2,1,0:T(8,128)(2,1)S(1)} %get-tuple-element.91), channel_id=1, source_target_pairs={{0,16},{8,24},{16,0},{24,8},{1,17},{9,25},{17,1},{25,9},{2,18},{10... | collective-permute-start | bytes 589832 | tf_op jit(solution)/shard_map/ppermute | solution.py:409
  25.6 10.8 %collective-permute-start.13 = (bf16[2,64,768]{2,1,0:T(8,128)(2,1)S(1)}, bf16[2,64,768]{2,1,0:T(8,128)(2,1)S(1)}, u32[]{:S(2)}, u32[]{:S(2)}) collective-permute-start(bf16[2,64,768]{2,1,0:T(8,128)(2,1)S(1)} %get-tuple-element.92), channel_id=1, source_target_pairs={{0,24},{8,16},{16,8},{24,0},{1,25},{9,17},{17,9},{25,1},{2,26},{10... | collective-permute-start | bytes 589832 | tf_op jit(solution)/shard_map/ppermute | solution.py:409
  36.4 14.0 %collective-permute-start.14 = (bf16[2,256,768]{2,1,0:T(8,128)(2,1)S(1)}, bf16[2,256,768]{2,1,0:T(8,128)(2,1)S(1)}, u32[]{:S(2)}, u32[]{:S(2)}) collective-permute-start(bf16[2,256,768]{2,1,0:T(8,128)(2,1)S(1)} %constant_dynamic-update-slice_fusion.8.refs_0_.refs_1_), channel_id=1, source_target_pairs={{0,1},{1,0},{2,3},{3,2},{4,5},{5,4},{6,7},{7,6},{8,9},{9,8},{10,11... | collective-permute-start | bytes 2359304 | tf_op jit(solution)/shard_map/ppermute | solution.py:405
  40.1 5.3 %collective-permute-start.7 = (bf16[1,64,768]{2,1,0:T(8,128)(2,1)S(1)}, bf16[1,64,768]{2,1,0:T(8,128)(2,1)S(1)}, u32[]{:S(2)}, u32[]{:S(2)}) collective-permute-start(bf16[1,64,768]{2,1,0:T(8,128)(2,1)S(1)} %get-tuple-element.86), channel_id=1, source_target_pairs={{0,8},{8,0},{16,24},{24,16},{1,9},{9,1},{17,25},{25,17},{2,10},{10... | collective-permute-start | bytes 294920 | tf_op jit(solution)/shard_map/ppermute | solution.py:409
  41.6 7.0 %collective-permute-start.8 = (bf16[1,64,768]{2,1,0:T(8,128)(2,1)S(1)}, bf16[1,64,768]{2,1,0:T(8,128)(2,1)S(1)}, u32[]{:S(2)}, u32[]{:S(2)}) collective-permute-start(bf16[1,64,768]{2,1,0:T(8,128)(2,1)S(1)} %get-tuple-element.87), channel_id=1, source_target_pairs={{0,16},{8,24},{16,0},{24,8},{1,17},{9,25},{17,1},{25,9},{2,18},{10... | collective-permute-start | bytes 294920 | tf_op jit(solution)/shard_map/ppermute | solution.py:409
  42.4 6.3 %collective-permute-start.9 = (bf16[1,64,768]{2,1,0:T(8,128)(2,1)S(1)}, bf16[1,64,768]{2,1,0:T(8,128)(2,1)S(1)}, u32[]{:S(2)}, u32[]{:S(2)}) collective-permute-start(bf16[1,64,768]{2,1,0:T(8,128)(2,1)S(1)} %get-tuple-element.88), channel_id=1, source_target_pairs={{0,24},{8,16},{16,8},{24,0},{1,25},{9,17},{17,9},{25,1},{2,26},{10... | collective-permute-start | bytes 294920 | tf_op jit(solution)/shard_map/ppermute | solution.py:409
  48.7 4.8 %collective-permute-start.10 = (bf16[1,256,768]{2,1,0:T(8,128)(2,1)S(1)}, bf16[1,256,768]{2,1,0:T(8,128)(2,1)S(1)}, u32[]{:S(2)}, u32[]{:S(2)}) collective-permute-start(bf16[1,256,768]{2,1,0:T(8,128)(2,1)S(1)} %constant_dynamic-update-slice_fusion.4.refs_0_.refs_1_), channel_id=1, source_target_pairs={{0,1},{1,0},{2,3},{3,2},{4,5},{5,4},{6,7},{7,6},{8,9},{9,8},{10,11... | collective-permute-start | bytes 1179656 | tf_op jit(solution)/shard_map/ppermute | solution.py:405
  50.5 4.6 %slice-start.3 = ((s8[12582912]{0:T(1024)(128)(4,1)}), s8[4194304]{0:T(1024)(128)(4,1)S(1)}, s32[]{:S(2)}) async-start(s8[12582912]{0:T(1024)(128)(4,1)} %bitcast.4), calls=%async_computation.3 | async-start | bytes 8388608
  52.2 2.9 %slice-start = ((s8[12582912]{0:T(1024)(128)(4,1)}), s8[4194304]{0:T(1024)(128)(4,1)S(1)}, s32[]{:S(2)}) async-start(s8[12582912]{0:T(1024)(128)(4,1)} %bitcast.2), calls=%async_computation | async-start | bytes 8388608
  52.2 3.5 %slice-start.1 = ((s8[12582912]{0:T(1024)(128)(4,1)}), s8[4194304]{0:T(1024)(128)(4,1)S(1)}, s32[]{:S(2)}) async-start(s8[12582912]{0:T(1024)(128)(4,1)} %bitcast.2), calls=%async_computation.1 | async-start | bytes 8388608
  52.2 4.7 %slice-start.4 = ((s8[12582912]{0:T(1024)(128)(4,1)}), s8[4194304]{0:T(1024)(128)(4,1)S(1)}, s32[]{:S(2)}) async-start(s8[12582912]{0:T(1024)(128)(4,1)} %bitcast.4), calls=%async_computation.4 | async-start | bytes 8388608
  53.5 4.7 %slice-start.2 = ((s8[12582912]{0:T(1024)(128)(4,1)}), s8[4194304]{0:T(1024)(128)(4,1)S(1)}, s32[]{:S(2)}) async-start(s8[12582912]{0:T(1024)(128)(4,1)} %bitcast.2), calls=%async_computation.2 | async-start | bytes 8388608
  53.5 5.9 %slice-start.5 = ((s8[12582912]{0:T(1024)(128)(4,1)}), s8[4194304]{0:T(1024)(128)(4,1)S(1)}, s32[]{:S(2)}) async-start(s8[12582912]{0:T(1024)(128)(4,1)} %bitcast.4), calls=%async_computation.5 | async-start | bytes 8388608
  62.4 15.4 %collective-permute-start.17 = (bf16[2,256,768]{2,1,0:T(8,128)(2,1)S(1)}, bf16[2,256,768]{2,1,0:T(8,128)(2,1)S(1)}, u32[]{:S(2)}, u32[]{:S(2)}) collective-permute-start(bf16[2,256,768]{2,1,0:T(8,128)(2,1)S(1)} %get-tuple-element.111), channel_id=1, source_target_pairs={{0,1},{1,0},{2,3},{3,2},{4,5},{5,4},{6,7},{7,6},{8,9},{9,8},{10,11... | collective-permute-start | bytes 2359304 | tf_op jit(solution)/shard_map/ppermute | solution.py:405
  62.9 2.5 %collective-permute-start.15 = (bf16[1,256,768]{2,1,0:T(8,128)(2,1)S(1)}, bf16[1,256,768]{2,1,0:T(8,128)(2,1)S(1)}, u32[]{:S(2)}, u32[]{:S(2)}) collective-permute-start(bf16[1,256,768]{2,1,0:T(8,128)(2,1)S(1)} %get-tuple-element.106), channel_id=1, source_target_pairs={{0,1},{1,0},{2,3},{3,2},{4,5},{5,4},{6,7},{7,6},{8,9},{9,8},{10,11... | collective-permute-start | bytes 1179656 | tf_op jit(solution)/shard_map/ppermute | solution.py:405
  67.7 15.7 %collective-permute-start.16 = (bf16[1,256,768]{2,1,0:T(8,128)(2,1)S(1)}, bf16[1,256,768]{2,1,0:T(8,128)(2,1)S(1)}, u32[]{:S(2)}, u32[]{:S(2)}) collective-permute-start(bf16[1,256,768]{2,1,0:T(8,128)(2,1)S(1)} %get-tuple-element.110), channel_id=1, source_target_pairs={{0,1},{1,0},{2,3},{3,2},{4,5},{5,4},{6,7},{7,6},{8,9},{9,8},{10,11... | collective-permute-start | bytes 1179656 | tf_op jit(solution)/shard_map/ppermute | solution.py:405
  68.1 5.6 %collective-permute-start.18 = (bf16[1,64,768]{2,1,0:T(8,128)(2,1)S(1)}, bf16[1,64,768]{2,1,0:T(8,128)(2,1)S(1)}, u32[]{:S(2)}, u32[]{:S(2)}) collective-permute-start(bf16[1,64,768]{2,1,0:T(8,128)(2,1)S(1)} %get-tuple-element.113), channel_id=1, source_target_pairs={{0,8},{8,0},{16,24},{24,16},{1,9},{9,1},{17,25},{25,17},{2,10},{10... | collective-permute-start | bytes 294920 | tf_op jit(solution)/shard_map/ppermute | solution.py:409
  68.6 5.7 %collective-permute-start.19 = (bf16[1,64,768]{2,1,0:T(8,128)(2,1)S(1)}, bf16[1,64,768]{2,1,0:T(8,128)(2,1)S(1)}, u32[]{:S(2)}, u32[]{:S(2)}) collective-permute-start(bf16[1,64,768]{2,1,0:T(8,128)(2,1)S(1)} %get-tuple-element.114), channel_id=1, source_target_pairs={{0,16},{8,24},{16,0},{24,8},{1,17},{9,25},{17,1},{25,9},{2,18},{10... | collective-permute-start | bytes 294920 | tf_op jit(solution)/shard_map/ppermute | solution.py:409
  69.8 5.5 %collective-permute-start.20 = (bf16[1,64,768]{2,1,0:T(8,128)(2,1)S(1)}, bf16[1,64,768]{2,1,0:T(8,128)(2,1)S(1)}, u32[]{:S(2)}, u32[]{:S(2)}) collective-permute-start(bf16[1,64,768]{2,1,0:T(8,128)(2,1)S(1)} %get-tuple-element.115), channel_id=1, source_target_pairs={{0,24},{8,16},{16,8},{24,0},{1,25},{9,17},{17,9},{25,1},{2,26},{10... | collective-permute-start | bytes 294920 | tf_op jit(solution)/shard_map/ppermute | solution.py:409
  75.6 21.4 %collective-permute-start.24 = (bf16[128,768]{1,0:T(8,128)(2,1)S(1)}, bf16[128,768]{1,0:T(8,128)(2,1)S(1)}, u32[]{:S(2)}, u32[]{:S(2)}) collective-permute-start(bf16[128,768]{1,0:T(8,128)(2,1)S(1)} %get-tuple-element.123), channel_id=1, source_target_pairs={{0,4},{1,5},{2,6},{3,7},{4,0},{5,1},{6,2},{7,3},{8,12},{9,13},{10,... | collective-permute-start | bytes 589832 | tf_op jit(solution)/shard_map/ppermute | solution.py:402
  79.8 9.0 %collective-permute-start.25 = (bf16[2,64,768]{2,1,0:T(8,128)(2,1)S(1)}, bf16[2,64,768]{2,1,0:T(8,128)(2,1)S(1)}, u32[]{:S(2)}, u32[]{:S(2)}) collective-permute-start(bf16[2,64,768]{2,1,0:T(8,128)(2,1)S(1)} %get-tuple-element.125), channel_id=1, source_target_pairs={{0,8},{8,0},{16,24},{24,16},{1,9},{9,1},{17,25},{25,17},{2,10},{10... | collective-permute-start | bytes 589832 | tf_op jit(solution)/shard_map/ppermute | solution.py:409
  81.3 9.6 %collective-permute-start.26 = (bf16[2,64,768]{2,1,0:T(8,128)(2,1)S(1)}, bf16[2,64,768]{2,1,0:T(8,128)(2,1)S(1)}, u32[]{:S(2)}, u32[]{:S(2)}) collective-permute-start(bf16[2,64,768]{2,1,0:T(8,128)(2,1)S(1)} %get-tuple-element.126), channel_id=1, source_target_pairs={{0,16},{8,24},{16,0},{24,8},{1,17},{9,25},{17,1},{25,9},{2,18},{10... | collective-permute-start | bytes 589832 | tf_op jit(solution)/shard_map/ppermute | solution.py:409
  82.1 8.8 %collective-permute-start.27 = (bf16[2,64,768]{2,1,0:T(8,128)(2,1)S(1)}, bf16[2,64,768]{2,1,0:T(8,128)(2,1)S(1)}, u32[]{:S(2)}, u32[]{:S(2)}) collective-permute-start(bf16[2,64,768]{2,1,0:T(8,128)(2,1)S(1)} %get-tuple-element.127), channel_id=1, source_target_pairs={{0,24},{8,16},{16,8},{24,0},{1,25},{9,17},{17,9},{25,1},{2,26},{10... | collective-permute-start | bytes 589832 | tf_op jit(solution)/shard_map/ppermute | solution.py:409
  91.2 11.3 %collective-permute-start.28 = (bf16[128,768]{1,0:T(8,128)(2,1)S(1)}, bf16[128,768]{1,0:T(8,128)(2,1)S(1)}, u32[]{:S(2)}, u32[]{:S(2)}) collective-permute-start(bf16[128,768]{1,0:T(8,128)(2,1)S(1)} %get-tuple-element.131), channel_id=1, source_target_pairs={{0,2},{1,3},{2,4},{3,5},{4,6},{5,7},{6,0},{7,1},{8,10},{9,11},{10,... | collective-permute-start | bytes 589832 | tf_op jit(solution)/shard_map/ppermute | solution.py:402
  91.3 11.2 %collective-permute-start.29 = (bf16[128,768]{1,0:T(8,128)(2,1)S(1)}, bf16[128,768]{1,0:T(8,128)(2,1)S(1)}, u32[]{:S(2)}, u32[]{:S(2)}) collective-permute-start(bf16[128,768]{1,0:T(8,128)(2,1)S(1)} %get-tuple-element.132), channel_id=1, source_target_pairs={{0,6},{1,7},{2,0},{3,1},{4,2},{5,3},{6,4},{7,5},{8,14},{9,15},{10,... | collective-permute-start | bytes 589832 | tf_op jit(solution)/shard_map/ppermute | solution.py:402
  95.1 5.5 %collective-permute-start.21 = (bf16[1,64,768]{2,1,0:T(8,128)(2,1)S(1)}, bf16[1,64,768]{2,1,0:T(8,128)(2,1)S(1)}, u32[]{:S(2)}, u32[]{:S(2)}) collective-permute-start(bf16[1,64,768]{2,1,0:T(8,128)(2,1)S(1)} %get-tuple-element.120), channel_id=1, source_target_pairs={{0,8},{8,0},{16,24},{24,16},{1,9},{9,1},{17,25},{25,17},{2,10},{10... | collective-permute-start | bytes 294920 | tf_op jit(solution)/shard_map/ppermute | solution.py:409
  95.7 5.0 %collective-permute-start.22 = (bf16[1,64,768]{2,1,0:T(8,128)(2,1)S(1)}, bf16[1,64,768]{2,1,0:T(8,128)(2,1)S(1)}, u32[]{:S(2)}, u32[]{:S(2)}) collective-permute-start(bf16[1,64,768]{2,1,0:T(8,128)(2,1)S(1)} %get-tuple-element.121), channel_id=1, source_target_pairs={{0,16},{8,24},{16,0},{24,8},{1,17},{9,25},{17,1},{25,9},{2,18},{10... | collective-permute-start | bytes 294920 | tf_op jit(solution)/shard_map/ppermute | solution.py:409
  97.0 5.5 %collective-permute-start.23 = (bf16[1,64,768]{2,1,0:T(8,128)(2,1)S(1)}, bf16[1,64,768]{2,1,0:T(8,128)(2,1)S(1)}, u32[]{:S(2)}, u32[]{:S(2)}) collective-permute-start(bf16[1,64,768]{2,1,0:T(8,128)(2,1)S(1)} %get-tuple-element.122), channel_id=1, source_target_pairs={{0,24},{8,16},{16,8},{24,0},{1,25},{9,17},{17,9},{25,1},{2,26},{10... | collective-permute-start | bytes 294920 | tf_op jit(solution)/shard_map/ppermute | solution.py:409

commit v3 on v2

--- a/solution.py
+++ b/solution.py
@@ -14,6 +14,9 @@
 TN = (((0,), (0,)), ((), ()))
 NN = (((1,), (0,)), ((), ()))
 MIB = 1 << 20
+ACT_FLOPS = 1.2e10
+SMALL = 1e3
+DOWN_WEIGHT = 0.0
 
 
 def dot(a, b, dims):
@@ -24,7 +27,11 @@
     return jax.ShapeDtypeStruct(shape, dtype)
 
 
-def call(kernel, name, operands, out_shape, after=(), flops=0, moved=0, mib=8, out_specs=None, **more):
+def in_hbm(x):
+    return pltpu.with_memory_space_constraint(x, pltpu.HBM)
+
+
+def call(kernel, name, operands, out_shape, after=(), flops=0, moved=0, mib=4, out_specs=None, **more):
     count, extra, results = len(operands), len(after), len(out_shape)
 
     def body(*refs):
@@ -49,31 +56,32 @@
     )(*operands, *after)
 
 
-def fill(raw, sel, gate, outs, b, capacity):
-    rows = (dot(sel, raw, NN) * gate).astype(BF16)
-    for r, out in enumerate(outs):
-        out[b] = rows[r * capacity : (r + 1) * capacity]
-
-
-def first_pack(raw, ids, probs, experts, capacity):
-    tokens, columns = raw.shape
+def route(raw, ids, probs, experts, capacity):
+    tokens = ids.shape[1]
     lines = max(8, experts)
     rows = experts * capacity
 
-    def kernel(raw_ref, ids_ref, probs_ref, sel_ref, gate_ref, copy_ref, *outs):
-        copy_ref[...] = raw_ref[...]
-        me = lax.axis_index("expert")
-        expert = lax.broadcasted_iota(jnp.int32, (lines, tokens), 0) ^ me
+    def kernel(raw_hbm, ids_hbm, probs_hbm, sel_ref, gate_ref, own_ref, ids_ref, probs_ref, sems):
+        copies = [
+            pltpu.make_async_copy(ids_hbm, ids_ref, sems.at[0]),
+            pltpu.make_async_copy(probs_hbm, probs_ref, sems.at[1]),
+            pltpu.make_async_copy(raw_hbm, own_ref, sems.at[2]),
+        ]
+        for copy in copies:
+            copy.start()
+        before = lax.broadcasted_iota(jnp.int32, (tokens, tokens), 0)
+        here = lax.broadcasted_iota(jnp.int32, (tokens, tokens), 1)
+        earlier = (before < here).astype(F32).astype(BF16)
+        slot = lax.broadcasted_iota(jnp.int32, (capacity, tokens), 0).astype(F32)
+        expert = lax.broadcasted_iota(jnp.int32, (lines, tokens), 0) ^ lax.axis_index("expert")
+        for copy in copies:
+            copy.wait()
         first = (ids_ref[0:1, :] == expert).astype(F32)
         second = (ids_ref[1:2, :] == expert).astype(F32)
         hit = first + second
-        before = lax.broadcasted_iota(jnp.int32, (tokens, tokens), 0)
-        here = lax.broadcasted_iota(jnp.int32, (tokens, tokens), 1)
-        earlier = (before < here).astype(F32).astype(BF16)
         place = dot(hit.astype(BF16), earlier, NN)
         place = jnp.where(hit > 0.0, place, -1.0)
         gate = first * probs_ref[0:1, :] + second * probs_ref[1:2, :]
-        slot = lax.broadcasted_iota(jnp.int32, (capacity, tokens), 0).astype(F32)
         for r in range(experts):
             match = place[r : r + 1, :] == slot
             span = pl.ds(r * capacity, capacity)
@@ -81,53 +89,85 @@
             gate_ref[span, :] = jnp.sum(
                 jnp.where(match, gate[r : r + 1, :], 0.0), axis=1, keepdims=True
             )
-        fill(raw_ref[...], sel_ref[...], gate_ref[...], outs, 0, capacity)
-
-    return call(
-        kernel,
-        "first_pack",
-        [raw, ids, probs],
-        [shaped((rows, tokens), BF16), shaped((rows, 1), F32), shaped(raw.shape, BF16)]
-        + [shaped((1, capacity, columns), BF16)] * experts,
-        flops=2 * rows * tokens * columns,
-        moved=1e6,
-    )
-
-
-def pack(raws, sel, gate, experts, capacity, after):
+
+    return call(
+        kernel,
+        "route",
+        [in_hbm(raw), in_hbm(ids), in_hbm(probs)],
+        [shaped((rows, tokens), BF16), shaped((rows, 1), F32), shaped(raw.shape, BF16)],
+        flops=SMALL,
+        moved=SMALL,
+        in_specs=[ANY] * 3,
+        scratch_shapes=[
+            pltpu.VMEM(ids.shape, jnp.int32),
+            pltpu.VMEM(probs.shape, F32),
+            pltpu.SemaphoreType.DMA((3,)),
+        ],
+    )
+
+
+def pack(raws, sel, gate, experts, capacity, after, again=False):
     blocks = len(raws)
     columns = raws[0].shape[1]
 
     def kernel(*refs):
         sel_ref, gate_ref = refs[blocks : blocks + 2]
+        outs = refs[blocks + 2 :]
         for b in range(blocks):
-            fill(refs[b][...], sel_ref[...], gate_ref[...], refs[blocks + 2 :], b, capacity)
+            rows = (dot(sel_ref[...], refs[b][...], NN) * gate_ref[...]).astype(BF16)
+            for r, out in enumerate(outs[:experts]):
+                out[b] = rows[r * capacity : (r + 1) * capacity]
+        if again:
+            outs[experts][...] = refs[0][...]
 
     return call(
         kernel,
         "pack",
         [*raws, sel, gate],
-        [shaped((blocks, capacity, columns), BF16)] * experts,
+        [shaped((blocks, capacity, columns), BF16)] * experts
+        + [shaped(raws[0].shape, BF16)] * again,
         after,
         flops=2 * blocks * sel.shape[0] * sel.shape[1] * columns,
         moved=6e5 * blocks,
     )
 
 
+def join(pieces, after):
+    experts = len(pieces)
+    blocks, capacity, columns = pieces[0].shape
+
+    def kernel(*refs):
+        for r in range(experts):
+            refs[experts][:, pl.ds(r * capacity, capacity), :] = refs[r][...]
+
+    return call(
+        kernel, "join", pieces, [shaped((blocks, experts * capacity, columns), BF16)], after
+    )
+
+
 def activations(gate_pre, up_pre, after):
     _, groups, capacity, units = gate_pre.shape
     rows = groups * capacity
-
-    def kernel(gate_ref, up_ref, up_factor, gate_factor, act):
+    tile = 256
+
+    def kernel(gate_hbm, up_hbm, up_factor, gate_factor, act, gate_ref, up_ref, sems):
         me = lax.axis_index("expert")
-        tile = 256
+        copies = []
+        for r in range(groups):
+            span = pl.ds(r * capacity, capacity)
+            for i, (source, target) in enumerate(((gate_hbm, gate_ref), (up_hbm, up_ref))):
+                copies.append(
+                    pltpu.make_async_copy(source.at[0, me ^ r], target.at[span, :], sems.at[i, r])
+                )
+        for copy in copies:
+            copy.start()
+        for copy in copies:
+            copy.wait()
 
         def step(i, unused):
             span = pl.ds(pl.multiple_of(i * tile, tile), tile)
-            a = jnp.concatenate([gate_ref[0, me ^ r, :, span] for r in range(groups)], axis=0)
-            b = jnp.concatenate([up_ref[0, me ^ r, :, span] for r in range(groups)], axis=0)
-            a = a.astype(F32).T
-            b = b.astype(F32).T
+            a = gate_ref[:, span].astype(F32).T
+            b = up_ref[:, span].astype(F32).T
             sig = 1.0 / (1.0 + jnp.exp(-a))
             swish = a * sig
             up_factor[span, :] = swish
@@ -140,11 +180,17 @@
     return call(
         kernel,
         "activations",
-        [gate_pre, up_pre],
+        [in_hbm(gate_pre), in_hbm(up_pre)],
         [shaped((units, rows), F32), shaped((units, rows), F32), shaped((units, rows), BF16)],
         after,
-        flops=3e7,
-        moved=14 * rows * units,
+        flops=ACT_FLOPS,
+        moved=SMALL,
+        in_specs=[ANY, ANY],
+        scratch_shapes=[
+            pltpu.VMEM((rows, units), BF16),
+            pltpu.VMEM((rows, units), BF16),
+            pltpu.SemaphoreType.DMA((2, groups)),
+        ],
     )
 
 
@@ -155,48 +201,43 @@
     return z * 2 + (1 - core if sibling else core)
 
 
-def hidden_part(x, w_down, shifts, line, sibling, total, factors, after):
-    blocks, rows, columns = x.shape
+def hidden_part(terms, w_down, line, total, factors, after):
+    _, rows, columns = terms[0][0].shape
     units = w_down.shape[1]
-    tile = 256
+    count = len(terms)
     has_total = total is not None
 
-    def kernel(x_ref, w_ref, *refs):
+    def kernel(*refs):
+        w_ref, refs, x_refs = refs[count], refs[count + 1 :], refs[:count]
         outs = refs[has_total + len(factors) :]
         factor_refs = refs[has_total : has_total + len(factors)]
-        starts = [
-            pl.multiple_of(block_of(-s, line, sibling) * columns, 128) for s in shifts
-        ]
-
-        def step(i, unused):
-            span = pl.ds(pl.multiple_of(i * tile, tile), tile)
-            value = refs[0][span, :] if has_total else 0.0
-            for b, start in enumerate(starts):
-                value = value + dot(w_ref[0, span, pl.ds(start, columns)], x_ref[b], NT)
-            if factors:
-                for out, factor in zip(outs, factor_refs):
-                    out[span, :] = (value * factor[span, :]).astype(BF16)
-            else:
-                outs[0][span, :] = value
-            return unused
-
-        lax.fori_loop(0, units // tile, step, 0)
+        value = refs[0][...] if has_total else 0.0
+        for x_ref, (_, shifts, sibling) in zip(x_refs, terms):
+            for b, shift in enumerate(shifts):
+                start = pl.multiple_of(block_of(-shift, line, sibling) * columns, 128)
+                value = value + dot(w_ref[0, :, pl.ds(start, columns)], x_ref[b], NT)
+        if factors:
+            for out, factor in zip(outs, factor_refs):
+                out[...] = (value * factor[...]).astype(BF16)
+        else:
+            outs[0][...] = value
 
     return call(
         kernel,
         "hidden_part",
-        [x, w_down] + ([total] if has_total else []) + list(factors),
+        [term[0] for term in terms] + [w_down] + ([total] if has_total else []) + list(factors),
         [shaped((units, rows), BF16)] * 2 if factors else [shaped((units, rows), F32)],
         after,
-        flops=2 * blocks * rows * columns * units,
-        moved=2 * blocks * columns * units + 8 * rows * units,
-    )
-
-
-def down_part(act, mine, theirs, shifts, line, before, out_shape, after):
+        moved=SMALL,
+        flops=SMALL,
+    )
+
+
+def down_part(act, mine, theirs, shifts, line, before, out_shape, after, weight=1.0):
     blocks, rows, columns = mine.shape
     units = act.shape[0]
-    split = 4
+    split = 2
+    slots = 3
     part = units // split
     steps = [(half, b) for half in range(2) for b in range(blocks)]
 
@@ -205,11 +246,11 @@
         copies = []
         for i, (half, b) in enumerate(steps):
             start = pl.multiple_of(block_of(-shifts[b], line, bool(half)) * columns, 128)
-            now = i % 2
+            now = i % slots
             x = (theirs_ref if half else mine_ref)[b]
             for j in range(split):
-                if i >= 2:
-                    copies[(i - 2) * split + j].wait()
+                if i >= slots:
+                    copies[(i - slots) * split + j].wait()
                 span = pl.ds(j * part, part)
                 held[now, span, :] = dot(act_ref[span, :], x, NN).astype(BF16)
                 copy = pltpu.make_async_copy(
@@ -219,7 +260,7 @@
                 )
                 copy.start()
                 copies.append(copy)
-        for copy in copies[-2 * split :]:
+        for copy in copies[-slots * split :]:
             copy.wait()
 
     operands = [act, mine, theirs]
@@ -231,14 +272,15 @@
         operands,
         [shaped(out_shape, BF16)],
         after,
-        flops=4 * blocks * rows * columns * units,
-        moved=4 * blocks * columns * units,
+        flops=weight * 4 * blocks * rows * columns * units,
+        moved=weight * 4 * blocks * columns * units,
+        mib=6,
         in_specs=[VMEM] * 3 + [ANY] * (len(operands) - 3),
         out_specs=[ANY],
         input_output_aliases={} if before is None else {3: 0},
         scratch_shapes=[
-            pltpu.VMEM((2, units, columns), BF16),
-            pltpu.SemaphoreType.DMA((2, split)),
+            pltpu.VMEM((slots, units, columns), BF16),
+            pltpu.SemaphoreType.DMA((slots, split)),
         ],
     )
 
@@ -281,31 +323,31 @@
     )
 
 
-def combine(pieces, sel, others, after):
+def combine(pieces, sel, others, dtypes, after):
     experts = len(pieces)
     blocks, _, columns = pieces[0].shape
     tokens = sel.shape[1]
-    count = len(others)
+    flat = [x for group in others for x in group]
 
     def kernel(*refs):
         piece_refs, sel_ref = refs[:experts], refs[experts]
-        other_refs = refs[experts + 1 : experts + 1 + count]
-        out_refs = refs[experts + 1 + count :]
+        other_refs = list(refs[experts + 1 : experts + 1 + len(flat)])
+        out_refs = refs[experts + 1 + len(flat) :]
         for b in range(blocks):
             rows = jnp.concatenate([piece[b] for piece in piece_refs], axis=0)
             value = dot(sel_ref[...], rows, TN)
-            for other in other_refs:
-                value = value + other[...].astype(F32)
-            out_refs[b][...] = value.astype(BF16)
+            for _ in others[b]:
+                value = value + other_refs.pop(0)[...].astype(F32)
+            out_refs[b][...] = value.astype(dtypes[b])
 
     return call(
         kernel,
         "combine",
-        [*pieces, sel, *others],
-        [shaped((tokens, columns), BF16)] * blocks,
+        [*pieces, sel, *flat],
+        [shaped((tokens, columns), dtype) for dtype in dtypes],
         after,
         flops=2 * blocks * sel.shape[0] * tokens * columns,
-        moved=6e5 * blocks + 2e5 * count,
+        moved=6e5 * blocks,
     )
 
 
@@ -405,61 +447,52 @@
         return lax.ppermute(x, "cuts", [(i, i ^ 1) for i in range(cuts)])
 
     def exchange(pieces):
-        moved = [
-            lax.ppermute(pieces[r], "expert", [(i, i ^ r) for i in range(experts)])
-            for r in range(1, experts)
-        ]
-        return [pieces[0]] + moved
-
-    near = [1, line - 1]
-    far = [2]
-    raws = [along(out_grad, shift) for shift in near]
-    sel, gate, again, *pieces, t = first_pack(
-        out_grad, expert_ids.T, gate_probs.T, experts, capacity
-    )
-    pieces0 = exchange(pieces)
-    raw2 = along(again, 2)
+        moved = {
+            r: lax.ppermute(pieces[r], "expert", [(i, i ^ r) for i in range(experts)])
+            for r in range(experts - 1, 0, -1)
+        }
+        return [pieces[0]] + [moved[r] for r in range(1, experts)]
+
+    raw1 = along(out_grad, 1)
+    raw2 = along(raw1, 1)
+    raw3 = along(out_grad, 3)
+    one, two = [0, 1], [3, 2]
+    sel, gate, own, t = route(out_grad, expert_ids.T, gate_probs.T, experts, capacity)
+    *pieces, t = pack([own, raw1], sel, gate, experts, capacity, [t])
+    pieces = exchange(pieces)
+    *pieces2, t = pack([raw3, raw2], sel, gate, experts, capacity, [t])
+    pieces2 = exchange(pieces2)
     up_factor, gate_factor, act, t = activations(gate_pre, up_pre, [t])
-    mine0 = jnp.concatenate(pieces0, axis=1)
-    theirs0 = swap(mine0)
-    total, t = hidden_part(mine0, w_down, [0], line, False, None, (), [t])
-    *pieces, t = pack(raws, sel, gate, experts, capacity, [t])
-    pieces1 = exchange(pieces)
-    total, t = hidden_part(theirs0, w_down, [0], line, True, total, (), [t])
-    down, t = down_part(act, mine0, theirs0, [0], line, None, w_down.shape, [t])
-    *pieces, t = pack([raw2], sel, gate, experts, capacity, [t])
-    pieces2 = exchange(pieces)
-    mine1 = jnp.concatenate(pieces1, axis=1)
+    mine1, t = join(pieces, [t])
     theirs1 = swap(mine1)
-    total, t = hidden_part(mine1, w_down, near, line, False, total, (), [t])
-    total, t = hidden_part(theirs1, w_down, near, line, True, total, (), [t])
-    mine2 = jnp.concatenate(pieces2, axis=1)
+    mine2, t = join(pieces2, [t])
     theirs2 = swap(mine2)
-    total, t = hidden_part(mine2, w_down, far, line, False, total, (), [t])
+    total, t = hidden_part(
+        [(mine1, one, False), (theirs1, one, True), (mine2, two, False)],
+        w_down, line, None, (), [t],
+    )
     gate_grad, up_grad, t = hidden_part(
-        theirs2, w_down, far, line, True, total, (gate_factor, up_factor), [t]
-    )
-
+        [(theirs2, two, True)], w_down, line, total, (gate_factor, up_factor), [t, w_gate]
+    )
+
+    first, last = [2, 3], [1, 0]
     back = functools.partial(slot_part, gate_grad, up_grad, w_gate, w_up)
-    part2, t = back(far, line, True, None, experts, [t])
-    other2 = swap(part2)
-    part1, t = back(near, line, True, None, experts, [t])
-    other1 = swap(part1)
-    *send2, t = back(far, line, False, other2, experts, [t])
-    got2 = exchange(send2)
-    part0, t = back([0], line, True, None, experts, [t])
-    other0 = swap(part0)
-    far_out, t = combine(got2, sel, [], [t])
-    landed = [along(far_out, 2)]
-    *send1, t = back(near, line, False, other1, experts, [t])
-    got1 = exchange(send1)
-    *send0, t = back([0], line, False, other0, experts, [t])
-    got0 = exchange(send0)
-    down, t = down_part(act, mine1, theirs1, near, line, down, w_down.shape, [t])
-    *near_out, t = combine(got1, sel, [], [t])
-    landed += [along(part, shift) for part, shift in zip(near_out, near)]
-    down, t = down_part(act, mine2, theirs2, far, line, down, w_down.shape, [t])
-    result, t = combine(got0, sel, landed, [t])
+    part, t = back(first, line, True, None, experts, [t])
+    other1 = swap(part)
+    part, t = back(last, line, True, None, experts, [t])
+    other2 = swap(part)
+    *pieces, t = back(first, line, False, other1, experts, [t])
+    got1 = exchange(pieces)
+    *pieces, t = back(last, line, False, other2, experts, [t])
+    got2 = exchange(pieces)
+    part2, part3, t = combine(got1, sel, [[], []], [BF16, BF16], [t])
+    landed2 = along(part2, 1)
+    landed3 = along(part3, 3)
+    down, t = down_part(act, mine1, theirs1, one, line, None, w_down.shape, [t])
+    part1, part0, t = combine(got2, sel, [[landed2], [landed3]], [BF16, F32], [t])
+    landed1 = along(part1, 1)
+    down, t = down_part(act, mine2, theirs2, two, line, down, w_down.shape, [t], DOWN_WEIGHT)
+    result = (part0 + landed1.astype(F32)).astype(BF16)
     return result, down
 
 

time: 104 us -> 78 us (0.75)
  local copies, waits for them, and re-layouts: 13.4 us -> 1.33 us
  starting transfers between devices: 34.5 us -> 24.2 us
  Pallas kernels: 28.6 us -> 23.6 us
  waiting for transfers between devices: 25.9 us -> 27 us
    ppermute x6, waiting for transfers between devices: 0.02 us -> 17.1 us  [along(): return lax.ppermute(x, 'cuts', pairs)]
    ppermute x18 -> x12, waiting for transfers between devices: 23.5 us -> 9.95 us  [exchange(): lax.ppermute(pieces[r], 'expert', [(i, i ^ r) for i in range(experts)])]
    unnamed x35 -> x18, local copies, waits for them, and re-layouts: 13.4 us -> 1.33 us
    ppermute x18 -> x12, starting transfers between devices: 21.2 us -> 13.8 us  [exchange(): lax.ppermute(pieces[r], 'expert', [(i, i ^ r) for i in range(experts)])]
    pallas_call x22 -> x16, Pallas kernels: 28.6 us -> 23.6 us  [call(): pl.pallas_call(body, out_shape=out_shape, in_specs=list(specs) + [VMEM] *...]
    ppermute x6 -> x4, waiting for transfers between devices: 2.41 us -> 0.01 us  [swap(): return lax.ppermute(x, 'cuts', [(i, i ^ 1) for i in range(cuts)])]
    ppermute x6, starting transfers between devices: 12.1 us -> 9.66 us  [along(): return lax.ppermute(x, 'cuts', pairs)]
  transfers between devices with their start and end apart: 30 -> 22, of which waited for: 12 -> 10; matrix products, arithmetic and copies ran while one was open for 0% -> 0% of each run, Pallas kernels for 22% -> 26%
where the time goes in v3:
time: 78 us; the launch traced here: 77.8 us
  waiting for transfers between devices  27 us (35%)
  starting transfers between devices  24.2 us (31%)
  Pallas kernels  23.6 us (30%)
  local copies, waits for them, and re-layouts  1.33 us (2%)
  between operations  0.94 us (1%)
    pallas_call x16, Pallas kernels, call(): pl.pallas_call(body, out_shape=out_shape, in_specs=list(specs) + [VMEM] *...  23.6 us
    ppermute x6, waiting for transfers between devices, along(): return lax.ppermute(x, 'cuts', pairs)  17.1 us
    ppermute x12, starting transfers between devices, exchange(): lax.ppermute(pieces[r], 'expert', [(i, i ^ r) for i in range(experts)])  13.8 us
    ppermute x12, waiting for transfers between devices, exchange(): lax.ppermute(pieces[r], 'expert', [(i, i ^ r) for i in range(experts)])  9.95 us
    ppermute x6, starting transfers between devices, along(): return lax.ppermute(x, 'cuts', pairs)  9.66 us
  transfers between devices with their start and end apart: 22, of which 10 were waited for; matrix products, arithmetic and copies ran while one was open for 0% of the time, Pallas kernels for 26%

profile of v3, /device:TPU:0, one launch (start us, length us, event | category | flops | bytes accessed | tf_op | source)
XLA Modules:
  0.0 77.8 jit_solution(860319802886829433)
XLA Ops:
  0.6 3.1 %collective-permute-start.1 = (bf16[128,768]{1,0:T(8,128)(2,1)}, bf16[128,768]{1,0:T(8,128)(2,1)S(1)}, u32[]{:S(2)}, u32[]{:S(2)}) collective-permute-start(bf16[128,768]{1,0:T(8,128)(2,1)} %refs_0_.2), channel_id=1, source_target_pairs={{0,2},{1,3},{2,4},{3,5},{4,6},{5,7},{6,0},{7,1},{8,10},{9,11},{10,... | collective-permute-start | bytes 589832 | tf_op jit(solution)/shard_map/ppermute | solution.py:444
  3.7 2.1 %collective-permute-start = (bf16[128,768]{1,0:T(8,128)(2,1)}, bf16[128,768]{1,0:T(8,128)(2,1)S(1)}, u32[]{:S(2)}, u32[]{:S(2)}) collective-permute-start(bf16[128,768]{1,0:T(8,128)(2,1)} %refs_0_.2), channel_id=1, source_target_pairs={{0,6},{1,7},{2,0},{3,1},{4,2},{5,3},{6,4},{7,5},{8,14},{9,15},{10,... | collective-permute-start | bytes 589832 | tf_op jit(solution)/shard_map/ppermute | solution.py:444
  5.8 1.2 %route.1 = (bf16[256,128]{1,0:T(8,128)(2,1)S(1)}, f32[256,1]{1,0:T(8,128)S(1)}, bf16[128,768]{1,0:T(8,128)(2,1)S(1)}, f32[8,128]{1,0:T(8,128)S(1)}) custom-call(bf16[128,768]{1,0:T(8,128)(2,1)} %refs_0_.2, s32[2,128]{1,0:T(2,128)} %bitcast.8, f32[2,128]{1,0:T(2,128)} %bitcast.9), custom_call_target="tpu_custom_call" | custom-call | flops 1000 | bytes 1000 | tf_op jit(solution)/shard_map/route/pallas_call | solution.py:45
  7.0 4.7 %collective-permute-done.1.refs_1_ = bf16[128,768]{1,0:T(8,128)(2,1)S(1)} collective-permute-done((bf16[128,768]{1,0:T(8,128)(2,1)}, bf16[128,768]{1,0:T(8,128)(2,1)S(1)}, u32[]{:S(2)}, u32[]{:S(2)}) %collective-permute-start.1) | collective-permute-done | bytes 196640 | tf_op jit(solution)/shard_map/ppermute | solution.py:444
  11.7 0.4 pack.2
  12.1 1.8 %collective-permute-start.6 = (bf16[2,64,768]{2,1,0:T(8,128)(2,1)S(1)}, bf16[2,64,768]{2,1,0:T(8,128)(2,1)S(1)}, u32[]{:S(2)}, u32[]{:S(2)}) collective-permute-start(bf16[2,64,768]{2,1,0:T(8,128)(2,1)S(1)} %get-tuple-element.62), channel_id=1, source_target_pairs={{0,8},{8,0},{16,24},{24,16},{1,9},{9,1},{17,25},{25,17},{2,10},{10... | collective-permute-start | bytes 589832 | tf_op jit(solution)/shard_map/ppermute | solution.py:451
  13.9 1.5 %collective-permute-start.7 = (bf16[2,64,768]{2,1,0:T(8,128)(2,1)S(1)}, bf16[2,64,768]{2,1,0:T(8,128)(2,1)S(1)}, u32[]{:S(2)}, u32[]{:S(2)}) collective-permute-start(bf16[2,64,768]{2,1,0:T(8,128)(2,1)S(1)} %get-tuple-element.63), channel_id=1, source_target_pairs={{0,16},{8,24},{16,0},{24,8},{1,17},{9,25},{17,1},{25,9},{2,18},{10... | collective-permute-start | bytes 589832 | tf_op jit(solution)/shard_map/ppermute | solution.py:451
  15.4 0.2 collective-permute-start.8
  15.6 3.8 %collective-permute-done.2.refs_1_ = bf16[128,768]{1,0:T(8,128)(2,1)S(1)} collective-permute-done((bf16[128,768]{1,0:T(8,128)(2,1)S(1)}, bf16[128,768]{1,0:T(8,128)(2,1)S(1)}, u32[]{:S(2)}, u32[]{:S(2)}) %collective-permute-start.2) | collective-permute-done | bytes 196640 | tf_op jit(solution)/shard_map/ppermute | solution.py:444
  19.5 0.4 pack.3
  19.8 1.6 %collective-permute-start.3 = (bf16[2,64,768]{2,1,0:T(8,128)(2,1)S(1)}, bf16[2,64,768]{2,1,0:T(8,128)(2,1)S(1)}, u32[]{:S(2)}, u32[]{:S(2)}) collective-permute-start(bf16[2,64,768]{2,1,0:T(8,128)(2,1)S(1)} %get-tuple-element.58), channel_id=1, source_target_pairs={{0,8},{8,0},{16,24},{24,16},{1,9},{9,1},{17,25},{25,17},{2,10},{10... | collective-permute-start | bytes 589832 | tf_op jit(solution)/shard_map/ppermute | solution.py:451
  21.4 1.5 %collective-permute-start.4 = (bf16[2,64,768]{2,1,0:T(8,128)(2,1)S(1)}, bf16[2,64,768]{2,1,0:T(8,128)(2,1)S(1)}, u32[]{:S(2)}, u32[]{:S(2)}) collective-permute-start(bf16[2,64,768]{2,1,0:T(8,128)(2,1)S(1)} %get-tuple-element.59), channel_id=1, source_target_pairs={{0,16},{8,24},{16,0},{24,8},{1,17},{9,25},{17,1},{25,9},{2,18},{10... | collective-permute-start | bytes 589832 | tf_op jit(solution)/shard_map/ppermute | solution.py:451
  22.9 0.5 collective-permute-start.5
  23.4 2.4 %activations.1 = (f32[1024,256]{1,0:T(8,128)S(1)}, f32[1024,256]{1,0:T(8,128)S(1)}, bf16[1024,256]{1,0:T(8,128)(2,1)S(1)}, f32[8,128]{1,0:T(8,128)S(1)}) custom-call(bf16[1,4,64,1024]{3,2,1,0:T(8,128)(2,1)} %refs_0_.3, bf16[1,4,64,1024]{3,2,1,0:T(8,128)(2,1)} %refs_1_.2, f32[8,128]{1,0:T(8,128)S(1)} %get-tuple-element.65.refs_2_), custom_call_target="tpu_custom_call" | custom-call | flops 12000000000 | bytes 1000 | tf_op jit(solution)/shard_map/activations/pallas_call | solution.py:45
  25.8 0.1 join.2
  25.9 0.1 collective-permute-start.10
  25.9 1.8 %collective-permute-done.3.refs_1_ = bf16[2,64,768]{2,1,0:T(8,128)(2,1)S(1)} collective-permute-done((bf16[2,64,768]{2,1,0:T(8,128)(2,1)S(1)}, bf16[2,64,768]{2,1,0:T(8,128)(2,1)S(1)}, u32[]{:S(2)}, u32[]{:S(2)}) %collective-permute-start.3) | collective-permute-done | bytes 196640 | tf_op jit(solution)/shard_map/ppermute | solution.py:451
  27.8 3.6 %collective-permute-done.4.refs_2_ = bf16[2,64,768]{2,1,0:T(8,128)(2,1)S(1)} collective-permute-done((bf16[2,64,768]{2,1,0:T(8,128)(2,1)S(1)}, bf16[2,64,768]{2,1,0:T(8,128)(2,1)S(1)}, u32[]{:S(2)}, u32[]{:S(2)}) %collective-permute-start.4) | collective-permute-done | bytes 196640 | tf_op jit(solution)/shard_map/ppermute | solution.py:451
  31.4 0.1 collective-permute-start.9
  31.6 2.6 %hidden_part.2 = (f32[1024,256]{1,0:T(8,128)S(1)}, f32[8,128]{1,0:T(8,128)S(1)}) custom-call(bf16[2,256,768]{2,1,0:T(8,128)(2,1)S(1)} %get-tuple-element.69.refs_0_.refs_1_, bf16[2,256,768]{2,1,0:T(8,128)(2,1)S(1)} %collective-permute-done.10.refs_1_.refs_2_, bf16[2,256,768]{2,1,0:T(8,128)(2,1)S(1)} %get-tuple-element.68.refs_2_.refs_1_, ...), custom_call_target="tpu_custom_call" | custom-call | flops 1000 | bytes 1000 | tf_op jit(solution)/shard_map/hidden_part/pallas_call | solution.py:45
  34.3 1.0 %hidden_part.3 = (bf16[1024,256]{1,0:T(8,128)(2,1)S(1)}, bf16[1024,256]{1,0:T(8,128)(2,1)S(1)}, f32[8,128]{1,0:T(8,128)S(1)}) custom-call(bf16[2,256,768]{2,1,0:T(8,128)(2,1)S(1)} %collective-permute-done.9.refs_0_.refs_2_, bf16[1,1024,6144]{2,1,0:T(8,128)(2,1)S(1)} %bitcast.7, f32[1024,256]{1,0:T(8,128)S(1)} %get-tuple-element.71.refs_2_, ...), custom_call_target="tpu_custom_call" | custom-call | flops 1000 | bytes 1000 | tf_op jit(solution)/shard_map/hidden_part/pallas_call | solution.py:45
  35.3 1.3 %slice-done.5 = s8[4194304]{0:T(1024)(128)(4,1)S(1)} async-done(((s8[12582912]{0:T(1024)(128)(4,1)}), s8[4194304]{0:T(1024)(128)(4,1)S(1)}, s32[]{:S(2)}) %slice-start.5) | async-done | bytes 4194328
  36.6 1.9 %slot_part.4 = (bf16[2,256,768]{2,1,0:T(8,128)(2,1)S(1)}, f32[8,128]{1,0:T(8,128)S(1)}) custom-call(bf16[1024,256]{1,0:T(8,128)(2,1)S(1)} %get-tuple-element.75.refs_0_, bf16[1024,256]{1,0:T(8,128)(2,1)S(1)} %get-tuple-element.76.refs_1_, bf16[1,6144,1024]{2,1,0:T(8,128)(2,1)S(1)} %bitcast.3, bf16[1,6144,1024]{2,1,0:T(8,128)(2,1)S(1)} %bitcast.5, ...), custom_call_target="tpu_custom_call" | custom-call | flops 1610612736 | bytes 7340032 | tf_op jit(solution)/shard_map/slot_part/pallas_call | solution.py:45
  38.5 0.5 collective-permute-start.12
  39.1 1.9 %slot_part.5 = (bf16[2,256,768]{2,1,0:T(8,128)(2,1)S(1)}, f32[8,128]{1,0:T(8,128)S(1)}) custom-call(bf16[1024,256]{1,0:T(8,128)(2,1)S(1)} %get-tuple-element.75.refs_0_, bf16[1024,256]{1,0:T(8,128)(2,1)S(1)} %get-tuple-element.76.refs_1_, bf16[1,6144,1024]{2,1,0:T(8,128)(2,1)S(1)} %bitcast.3, bf16[1,6144,1024]{2,1,0:T(8,128)(2,1)S(1)} %bitcast.5, ...), custom_call_target="tpu_custom_call" | custom-call | flops 1610612736 | bytes 7340032 | tf_op jit(solution)/shard_map/slot_part/pallas_call | solution.py:45
  41.0 0.1 collective-permute-start.11
  41.1 2.0 %slot_part.6 = (bf16[2,64,768]{2,1,0:T(8,128)(2,1)S(1)}, bf16[2,64,768]{2,1,0:T(8,128)(2,1)S(1)}, bf16[2,64,768]{2,1,0:T(8,128)(2,1)S(1)}, bf16[2,64,768]{2,1,0:T(8,128)(2,1)S(1)}, f32[8,128]{1,0:T(8,128)S(1)}) custom-call(bf16[1024,256]{1,0:T(8,128)(2,1)S(1)} %get-tuple-element.75.refs_0_, bf16[1024,256]{1,0:T(8,128)(2,1)S(1)} %get-tuple-element.76.refs_1_, ...), custom_call_target="tpu_custom_call" | custom-call | flops 1610612736 | bytes 7340032 | tf_op jit(solution)/shard_map/slot_part/pallas_call | solution.py:45
  43.1 1.0 %collective-permute-start.16 = (bf16[2,64,768]{2,1,0:T(8,128)(2,1)S(1)}, bf16[2,64,768]{2,1,0:T(8,128)(2,1)S(1)}, u32[]{:S(2)}, u32[]{:S(2)}) collective-permute-start(bf16[2,64,768]{2,1,0:T(8,128)(2,1)S(1)} %get-tuple-element.88), channel_id=1, source_target_pairs={{0,8},{8,0},{16,24},{24,16},{1,9},{9,1},{17,25},{25,17},{2,10},{10... | collective-permute-start | bytes 589832 | tf_op jit(solution)/shard_map/ppermute | solution.py:451
  44.0 0.8 %collective-permute-start.17 = (bf16[2,64,768]{2,1,0:T(8,128)(2,1)S(1)}, bf16[2,64,768]{2,1,0:T(8,128)(2,1)S(1)}, u32[]{:S(2)}, u32[]{:S(2)}) collective-permute-start(bf16[2,64,768]{2,1,0:T(8,128)(2,1)S(1)} %get-tuple-element.89), channel_id=1, source_target_pairs={{0,16},{8,24},{16,0},{24,8},{1,17},{9,25},{17,1},{25,9},{2,18},{10... | collective-permute-start | bytes 589832 | tf_op jit(solution)/shard_map/ppermute | solution.py:451
  44.9 1.7 %collective-permute-start.18 = (bf16[2,64,768]{2,1,0:T(8,128)(2,1)S(1)}, bf16[2,64,768]{2,1,0:T(8,128)(2,1)S(1)}, u32[]{:S(2)}, u32[]{:S(2)}) collective-permute-start(bf16[2,64,768]{2,1,0:T(8,128)(2,1)S(1)} %get-tuple-element.90), channel_id=1, source_target_pairs={{0,24},{8,16},{16,8},{24,0},{1,25},{9,17},{17,9},{25,1},{2,26},{10... | collective-permute-start | bytes 589832 | tf_op jit(solution)/shard_map/ppermute | solution.py:451
  46.6 2.0 %slot_part.7 = (bf16[2,64,768]{2,1,0:T(8,128)(2,1)S(1)}, bf16[2,64,768]{2,1,0:T(8,128)(2,1)S(1)}, bf16[2,64,768]{2,1,0:T(8,128)(2,1)S(1)}, bf16[2,64,768]{2,1,0:T(8,128)(2,1)S(1)}, f32[8,128]{1,0:T(8,128)S(1)}) custom-call(bf16[1024,256]{1,0:T(8,128)(2,1)S(1)} %get-tuple-element.75.refs_0_, bf16[1024,256]{1,0:T(8,128)(2,1)S(1)} %get-tuple-element.76.refs_1_, ...), custom_call_target="tpu_custom_call" | custom-call | flops 1610612736 | bytes 7340032 | tf_op jit(solution)/shard_map/slot_part/pallas_call | solution.py:45
  48.6 1.0 %collective-permute-start.13 = (bf16[2,64,768]{2,1,0:T(8,128)(2,1)S(1)}, bf16[2,64,768]{2,1,0:T(8,128)(2,1)S(1)}, u32[]{:S(2)}, u32[]{:S(2)}) collective-permute-start(bf16[2,64,768]{2,1,0:T(8,128)(2,1)S(1)} %get-tuple-element.84), channel_id=1, source_target_pairs={{0,8},{8,0},{16,24},{24,16},{1,9},{9,1},{17,25},{25,17},{2,10},{10... | collective-permute-start | bytes 589832 | tf_op jit(solution)/shard_map/ppermute | solution.py:451
  49.6 0.8 %collective-permute-start.14 = (bf16[2,64,768]{2,1,0:T(8,128)(2,1)S(1)}, bf16[2,64,768]{2,1,0:T(8,128)(2,1)S(1)}, u32[]{:S(2)}, u32[]{:S(2)}) collective-permute-start(bf16[2,64,768]{2,1,0:T(8,128)(2,1)S(1)} %get-tuple-element.85), channel_id=1, source_target_pairs={{0,16},{8,24},{16,0},{24,8},{1,17},{9,25},{17,1},{25,9},{2,18},{10... | collective-permute-start | bytes 589832 | tf_op jit(solution)/shard_map/ppermute | solution.py:451
  50.4 0.4 collective-permute-done.16.refs_1_
  50.8 1.3 %collective-permute-start.15 = (bf16[2,64,768]{2,1,0:T(8,128)(2,1)S(1)}, bf16[2,64,768]{2,1,0:T(8,128)(2,1)S(1)}, u32[]{:S(2)}, u32[]{:S(2)}) collective-permute-start(bf16[2,64,768]{2,1,0:T(8,128)(2,1)S(1)} %get-tuple-element.86), channel_id=1, source_target_pairs={{0,24},{8,16},{16,8},{24,0},{1,25},{9,17},{17,9},{25,1},{2,26},{10... | collective-permute-start | bytes 589832 | tf_op jit(solution)/shard_map/ppermute | solution.py:451
  52.2 3.6 %collective-permute-done.18.refs_3_ = bf16[2,64,768]{2,1,0:T(8,128)(2,1)S(1)} collective-permute-done((bf16[2,64,768]{2,1,0:T(8,128)(2,1)S(1)}, bf16[2,64,768]{2,1,0:T(8,128)(2,1)S(1)}, u32[]{:S(2)}, u32[]{:S(2)}) %collective-permute-start.18) | collective-permute-done | bytes 196640 | tf_op jit(solution)/shard_map/ppermute | solution.py:451
  55.7 0.3 combine.2
  56.0 2.4 %collective-permute-start.19 = (bf16[128,768]{1,0:T(8,128)(2,1)S(1)}, bf16[128,768]{1,0:T(8,128)(2,1)S(1)}, u32[]{:S(2)}, u32[]{:S(2)}) collective-permute-start(bf16[128,768]{1,0:T(8,128)(2,1)S(1)} %get-tuple-element.92), channel_id=1, source_target_pairs={{0,2},{1,3},{2,4},{3,5},{4,6},{5,7},{6,0},{7,1},{8,10},{9,11},{10,... | collective-permute-start | bytes 589832 | tf_op jit(solution)/shard_map/ppermute | solution.py:444
  58.4 1.5 %collective-permute-start.20 = (bf16[128,768]{1,0:T(8,128)(2,1)S(1)}, bf16[128,768]{1,0:T(8,128)(2,1)S(1)}, u32[]{:S(2)}, u32[]{:S(2)}) collective-permute-start(bf16[128,768]{1,0:T(8,128)(2,1)S(1)} %get-tuple-element.93), channel_id=1, source_target_pairs={{0,6},{1,7},{2,0},{3,1},{4,2},{5,3},{6,4},{7,5},{8,14},{9,15},{10,... | collective-permute-start | bytes 589832 | tf_op jit(solution)/shard_map/ppermute | solution.py:444
  59.9 3.3 %down_part.2 = (bf16[1,1024,6144]{2,1,0:T(8,128)(2,1)}, f32[8,128]{1,0:T(8,128)S(1)}) custom-call(bf16[1024,256]{1,0:T(8,128)(2,1)S(1)} %get-tuple-element.94.refs_0_, bf16[2,256,768]{2,1,0:T(8,128)(2,1)S(1)} %get-tuple-element.69.refs_0_.refs_1_, bf16[2,256,768]{2,1,0:T(8,128)(2,1)S(1)} %collective-permute-done.10.refs_1_.refs_2_, ...), custom_call_target="tpu_custom_call" | custom-call | flops 1610612736 | bytes 6291456 | tf_op jit(solution)/shard_map/down_part/pallas_call | solution.py:45
  63.2 0.5 collective-permute-done.15.refs_3_
  63.7 2.0 %collective-permute-done.19.refs_5_ = bf16[128,768]{1,0:T(8,128)(2,1)S(1)} collective-permute-done((bf16[128,768]{1,0:T(8,128)(2,1)S(1)}, bf16[128,768]{1,0:T(8,128)(2,1)S(1)}, u32[]{:S(2)}, u32[]{:S(2)}) %collective-permute-start.19) | collective-permute-done | bytes 196640 | tf_op jit(solution)/shard_map/ppermute | solution.py:444
  65.7 2.5 %collective-permute-done.20.refs_6_ = bf16[128,768]{1,0:T(8,128)(2,1)S(1)} collective-permute-done((bf16[128,768]{1,0:T(8,128)(2,1)S(1)}, bf16[128,768]{1,0:T(8,128)(2,1)S(1)}, u32[]{:S(2)}, u32[]{:S(2)}) %collective-permute-start.20) | collective-permute-done | bytes 196640 | tf_op jit(solution)/shard_map/ppermute | solution.py:444
  68.2 0.3 combine.3
  68.5 0.6 collective-permute-start.21
  69.1 3.9 %down_part.3 = (bf16[1,1024,6144]{2,1,0:T(8,128)(2,1)}, f32[8,128]{1,0:T(8,128)}) custom-call(bf16[1024,256]{1,0:T(8,128)(2,1)S(1)} %get-tuple-element.94.refs_0_, bf16[2,256,768]{2,1,0:T(8,128)(2,1)S(1)} %get-tuple-element.68.refs_2_.refs_1_, bf16[2,256,768]{2,1,0:T(8,128)(2,1)S(1)} %collective-permute-done.9.refs_0_.refs_2_, ...), custom_call_target="tpu_custom_call", output_to_operand_aliasing={{0}: (3, {})} | custom-call | tf_op jit(solution)/shard_map/down_part/pallas_call | solution.py:45
  73.0 4.1 %collective-permute-done.21 = bf16[128,768]{1,0:T(8,128)(2,1)S(1)} collective-permute-done((bf16[128,768]{1,0:T(8,128)(2,1)S(1)}, bf16[128,768]{1,0:T(8,128)(2,1)S(1)}, u32[]{:S(2)}, u32[]{:S(2)}) %collective-permute-start.21) | collective-permute-done | bytes 196640 | tf_op jit(solution)/shard_map/ppermute | solution.py:444
  77.1 0.7 add_convert_fusion
  (34 shorter events, 0.1 us)
Async XLA Ops:
  0.6 11.1 %collective-permute-start.1 = (bf16[128,768]{1,0:T(8,128)(2,1)}, bf16[128,768]{1,0:T(8,128)(2,1)S(1)}, u32[]{:S(2)}, u32[]{:S(2)}) collective-permute-start(bf16[128,768]{1,0:T(8,128)(2,1)} %refs_0_.2), channel_id=1, source_target_pairs={{0,2},{1,3},{2,4},{3,5},{4,6},{5,7},{6,0},{7,1},{8,10},{9,11},{10,... | collective-permute-start | bytes 589832 | tf_op jit(solution)/shard_map/ppermute | solution.py:444
  3.7 11.9 %collective-permute-start = (bf16[128,768]{1,0:T(8,128)(2,1)}, bf16[128,768]{1,0:T(8,128)(2,1)S(1)}, u32[]{:S(2)}, u32[]{:S(2)}) collective-permute-start(bf16[128,768]{1,0:T(8,128)(2,1)} %refs_0_.2), channel_id=1, source_target_pairs={{0,6},{1,7},{2,0},{3,1},{4,2},{5,3},{6,4},{7,5},{8,14},{9,15},{10,... | collective-permute-start | bytes 589832 | tf_op jit(solution)/shard_map/ppermute | solution.py:444
  11.7 7.8 %collective-permute-start.2 = (bf16[128,768]{1,0:T(8,128)(2,1)S(1)}, bf16[128,768]{1,0:T(8,128)(2,1)S(1)}, u32[]{:S(2)}, u32[]{:S(2)}) collective-permute-start(bf16[128,768]{1,0:T(8,128)(2,1)S(1)} %collective-permute-done.1.refs_1_), channel_id=1, source_target_pairs={{0,2},{1,3},{2,4},{3,5},{4,6},{5,7},{6,0},{7,1},{8,10},{9,11},{10,... | collective-permute-start | bytes 589832 | tf_op jit(solution)/shard_map/ppermute | solution.py:444
  12.1 10.8 %collective-permute-start.6 = (bf16[2,64,768]{2,1,0:T(8,128)(2,1)S(1)}, bf16[2,64,768]{2,1,0:T(8,128)(2,1)S(1)}, u32[]{:S(2)}, u32[]{:S(2)}) collective-permute-start(bf16[2,64,768]{2,1,0:T(8,128)(2,1)S(1)} %get-tuple-element.62), channel_id=1, source_target_pairs={{0,8},{8,0},{16,24},{24,16},{1,9},{9,1},{17,25},{25,17},{2,10},{10... | collective-permute-start | bytes 589832 | tf_op jit(solution)/shard_map/ppermute | solution.py:451
  13.9 11.9 %collective-permute-start.7 = (bf16[2,64,768]{2,1,0:T(8,128)(2,1)S(1)}, bf16[2,64,768]{2,1,0:T(8,128)(2,1)S(1)}, u32[]{:S(2)}, u32[]{:S(2)}) collective-permute-start(bf16[2,64,768]{2,1,0:T(8,128)(2,1)S(1)} %get-tuple-element.63), channel_id=1, source_target_pairs={{0,16},{8,24},{16,0},{24,8},{1,17},{9,25},{17,1},{25,9},{2,18},{10... | collective-permute-start | bytes 589832 | tf_op jit(solution)/shard_map/ppermute | solution.py:451
  15.4 10.4 %collective-permute-start.8 = (bf16[2,64,768]{2,1,0:T(8,128)(2,1)S(1)}, bf16[2,64,768]{2,1,0:T(8,128)(2,1)S(1)}, u32[]{:S(2)}, u32[]{:S(2)}) collective-permute-start(bf16[2,64,768]{2,1,0:T(8,128)(2,1)S(1)} %get-tuple-element.64), channel_id=1, source_target_pairs={{0,24},{8,16},{16,8},{24,0},{1,25},{9,17},{17,9},{25,1},{2,26},{10... | collective-permute-start | bytes 589832 | tf_op jit(solution)/shard_map/ppermute | solution.py:451
  19.5 12.0 %slice-start.6 = ((s8[12582912]{0:T(1024)(128)(4,1)}), s8[4194304]{0:T(1024)(128)(4,1)S(1)}, s32[]{:S(2)}) async-start(s8[12582912]{0:T(1024)(128)(4,1)} %bitcast.6), calls=%async_computation.6 | async-start | bytes 8388608
  19.8 7.9 %collective-permute-start.3 = (bf16[2,64,768]{2,1,0:T(8,128)(2,1)S(1)}, bf16[2,64,768]{2,1,0:T(8,128)(2,1)S(1)}, u32[]{:S(2)}, u32[]{:S(2)}) collective-permute-start(bf16[2,64,768]{2,1,0:T(8,128)(2,1)S(1)} %get-tuple-element.58), channel_id=1, source_target_pairs={{0,8},{8,0},{16,24},{24,16},{1,9},{9,1},{17,25},{25,17},{2,10},{10... | collective-permute-start | bytes 589832 | tf_op jit(solution)/shard_map/ppermute | solution.py:451
  21.4 9.9 %collective-permute-start.4 = (bf16[2,64,768]{2,1,0:T(8,128)(2,1)S(1)}, bf16[2,64,768]{2,1,0:T(8,128)(2,1)S(1)}, u32[]{:S(2)}, u32[]{:S(2)}) collective-permute-start(bf16[2,64,768]{2,1,0:T(8,128)(2,1)S(1)} %get-tuple-element.59), channel_id=1, source_target_pairs={{0,16},{8,24},{16,0},{24,8},{1,17},{9,25},{17,1},{25,9},{2,18},{10... | collective-permute-start | bytes 589832 | tf_op jit(solution)/shard_map/ppermute | solution.py:451
  22.9 8.4 %collective-permute-start.5 = (bf16[2,64,768]{2,1,0:T(8,128)(2,1)S(1)}, bf16[2,64,768]{2,1,0:T(8,128)(2,1)S(1)}, u32[]{:S(2)}, u32[]{:S(2)}) collective-permute-start(bf16[2,64,768]{2,1,0:T(8,128)(2,1)S(1)} %get-tuple-element.60), channel_id=1, source_target_pairs={{0,24},{8,16},{16,8},{24,0},{1,25},{9,17},{17,9},{25,1},{2,26},{10... | collective-permute-start | bytes 589832 | tf_op jit(solution)/shard_map/ppermute | solution.py:451
  23.4 10.8 %slice-start = ((s8[12582912]{0:T(1024)(128)(4,1)}), s8[4194304]{0:T(1024)(128)(4,1)S(1)}, s32[]{:S(2)}) async-start(s8[12582912]{0:T(1024)(128)(4,1)} %bitcast.2), calls=%async_computation | async-start | bytes 8388608
  23.4 8.1 %slice-start.7 = ((s8[12582912]{0:T(1024)(128)(4,1)}), s8[4194304]{0:T(1024)(128)(4,1)S(1)}, s32[]{:S(2)}) async-start(s8[12582912]{0:T(1024)(128)(4,1)} %bitcast.6), calls=%async_computation.7 | async-start | bytes 8388608
  23.4 8.1 %slice-start.8 = ((s8[12582912]{0:T(1024)(128)(4,1)}), s8[4194304]{0:T(1024)(128)(4,1)S(1)}, s32[]{:S(2)}) async-start(s8[12582912]{0:T(1024)(128)(4,1)} %bitcast.6), calls=%async_computation.8 | async-start | bytes 8388608
  23.4 10.8 %slice-start.1 = ((s8[12582912]{0:T(1024)(128)(4,1)}), s8[4194304]{0:T(1024)(128)(4,1)S(1)}, s32[]{:S(2)}) async-start(s8[12582912]{0:T(1024)(128)(4,1)} %bitcast.2), calls=%async_computation.1 | async-start | bytes 8388608
  23.4 10.8 %slice-start.2 = ((s8[12582912]{0:T(1024)(128)(4,1)}), s8[4194304]{0:T(1024)(128)(4,1)S(1)}, s32[]{:S(2)}) async-start(s8[12582912]{0:T(1024)(128)(4,1)} %bitcast.2), calls=%async_computation.2 | async-start | bytes 8388608
  25.9 5.6 %collective-permute-start.10 = (bf16[2,256,768]{2,1,0:T(8,128)(2,1)S(1)}, bf16[2,256,768]{2,1,0:T(8,128)(2,1)S(1)}, u32[]{:S(2)}, u32[]{:S(2)}) collective-permute-start(bf16[2,256,768]{2,1,0:T(8,128)(2,1)S(1)} %get-tuple-element.69.refs_0_.refs_1_), channel_id=1, source_target_pairs={{0,1},{1,0},{2,3},{3,2},{4,5},{5,4},{6,7},{7,6},{8,9},{9,8},{10,11... | collective-permute-start | bytes 2359304 | tf_op jit(solution)/shard_map/ppermute | solution.py:447
  31.4 2.8 %collective-permute-start.9 = (bf16[2,256,768]{2,1,0:T(8,128)(2,1)S(1)}, bf16[2,256,768]{2,1,0:T(8,128)(2,1)S(1)}, u32[]{:S(2)}, u32[]{:S(2)}) collective-permute-start(bf16[2,256,768]{2,1,0:T(8,128)(2,1)S(1)} %get-tuple-element.68.refs_2_.refs_1_), channel_id=1, source_target_pairs={{0,1},{1,0},{2,3},{3,2},{4,5},{5,4},{6,7},{7,6},{8,9},{9,8},{10,11... | collective-permute-start | bytes 2359304 | tf_op jit(solution)/shard_map/ppermute | solution.py:447
  31.5 3.8 %slice-start.3 = ((s8[12582912]{0:T(1024)(128)(4,1)}), s8[4194304]{0:T(1024)(128)(4,1)S(1)}, s32[]{:S(2)}) async-start(s8[12582912]{0:T(1024)(128)(4,1)} %bitcast.4), calls=%async_computation.3 | async-start | bytes 8388608
  31.5 3.8 %slice-start.4 = ((s8[12582912]{0:T(1024)(128)(4,1)}), s8[4194304]{0:T(1024)(128)(4,1)S(1)}, s32[]{:S(2)}) async-start(s8[12582912]{0:T(1024)(128)(4,1)} %bitcast.4), calls=%async_computation.4 | async-start | bytes 8388608
  34.2 2.4 %slice-start.5 = ((s8[12582912]{0:T(1024)(128)(4,1)}), s8[4194304]{0:T(1024)(128)(4,1)S(1)}, s32[]{:S(2)}) async-start(s8[12582912]{0:T(1024)(128)(4,1)} %bitcast.4), calls=%async_computation.5 | async-start | bytes 8388608
  38.5 2.6 %collective-permute-start.12 = (bf16[2,256,768]{2,1,0:T(8,128)(2,1)S(1)}, bf16[2,256,768]{2,1,0:T(8,128)(2,1)S(1)}, u32[]{:S(2)}, u32[]{:S(2)}) collective-permute-start(bf16[2,256,768]{2,1,0:T(8,128)(2,1)S(1)} %get-tuple-element.80), channel_id=1, source_target_pairs={{0,1},{1,0},{2,3},{3,2},{4,5},{5,4},{6,7},{7,6},{8,9},{9,8},{10,11... | collective-permute-start | bytes 2359304 | tf_op jit(solution)/shard_map/ppermute | solution.py:447
  41.0 5.6 %collective-permute-start.11 = (bf16[2,256,768]{2,1,0:T(8,128)(2,1)S(1)}, bf16[2,256,768]{2,1,0:T(8,128)(2,1)S(1)}, u32[]{:S(2)}, u32[]{:S(2)}) collective-permute-start(bf16[2,256,768]{2,1,0:T(8,128)(2,1)S(1)} %get-tuple-element.79), channel_id=1, source_target_pairs={{0,1},{1,0},{2,3},{3,2},{4,5},{5,4},{6,7},{7,6},{8,9},{9,8},{10,11... | collective-permute-start | bytes 2359304 | tf_op jit(solution)/shard_map/ppermute | solution.py:447
  43.1 7.8 %collective-permute-start.16 = (bf16[2,64,768]{2,1,0:T(8,128)(2,1)S(1)}, bf16[2,64,768]{2,1,0:T(8,128)(2,1)S(1)}, u32[]{:S(2)}, u32[]{:S(2)}) collective-permute-start(bf16[2,64,768]{2,1,0:T(8,128)(2,1)S(1)} %get-tuple-element.88), channel_id=1, source_target_pairs={{0,8},{8,0},{16,24},{24,16},{1,9},{9,1},{17,25},{25,17},{2,10},{10... | collective-permute-start | bytes 589832 | tf_op jit(solution)/shard_map/ppermute | solution.py:451
  44.0 8.1 %collective-permute-start.17 = (bf16[2,64,768]{2,1,0:T(8,128)(2,1)S(1)}, bf16[2,64,768]{2,1,0:T(8,128)(2,1)S(1)}, u32[]{:S(2)}, u32[]{:S(2)}) collective-permute-start(bf16[2,64,768]{2,1,0:T(8,128)(2,1)S(1)} %get-tuple-element.89), channel_id=1, source_target_pairs={{0,16},{8,24},{16,0},{24,8},{1,17},{9,25},{17,1},{25,9},{2,18},{10... | collective-permute-start | bytes 589832 | tf_op jit(solution)/shard_map/ppermute | solution.py:451
  44.9 10.8 %collective-permute-start.18 = (bf16[2,64,768]{2,1,0:T(8,128)(2,1)S(1)}, bf16[2,64,768]{2,1,0:T(8,128)(2,1)S(1)}, u32[]{:S(2)}, u32[]{:S(2)}) collective-permute-start(bf16[2,64,768]{2,1,0:T(8,128)(2,1)S(1)} %get-tuple-element.90), channel_id=1, source_target_pairs={{0,24},{8,16},{16,8},{24,0},{1,25},{9,17},{17,9},{25,1},{2,26},{10... | collective-permute-start | bytes 589832 | tf_op jit(solution)/shard_map/ppermute | solution.py:451
  48.6 14.6 %collective-permute-start.13 = (bf16[2,64,768]{2,1,0:T(8,128)(2,1)S(1)}, bf16[2,64,768]{2,1,0:T(8,128)(2,1)S(1)}, u32[]{:S(2)}, u32[]{:S(2)}) collective-permute-start(bf16[2,64,768]{2,1,0:T(8,128)(2,1)S(1)} %get-tuple-element.84), channel_id=1, source_target_pairs={{0,8},{8,0},{16,24},{24,16},{1,9},{9,1},{17,25},{25,17},{2,10},{10... | collective-permute-start | bytes 589832 | tf_op jit(solution)/shard_map/ppermute | solution.py:451
  49.6 13.6 %collective-permute-start.14 = (bf16[2,64,768]{2,1,0:T(8,128)(2,1)S(1)}, bf16[2,64,768]{2,1,0:T(8,128)(2,1)S(1)}, u32[]{:S(2)}, u32[]{:S(2)}) collective-permute-start(bf16[2,64,768]{2,1,0:T(8,128)(2,1)S(1)} %get-tuple-element.85), channel_id=1, source_target_pairs={{0,16},{8,24},{16,0},{24,8},{1,17},{9,25},{17,1},{25,9},{2,18},{10... | collective-permute-start | bytes 589832 | tf_op jit(solution)/shard_map/ppermute | solution.py:451
  50.8 12.9 %collective-permute-start.15 = (bf16[2,64,768]{2,1,0:T(8,128)(2,1)S(1)}, bf16[2,64,768]{2,1,0:T(8,128)(2,1)S(1)}, u32[]{:S(2)}, u32[]{:S(2)}) collective-permute-start(bf16[2,64,768]{2,1,0:T(8,128)(2,1)S(1)} %get-tuple-element.86), channel_id=1, source_target_pairs={{0,24},{8,16},{16,8},{24,0},{1,25},{9,17},{17,9},{25,1},{2,26},{10... | collective-permute-start | bytes 589832 | tf_op jit(solution)/shard_map/ppermute | solution.py:451
  56.0 9.7 %collective-permute-start.19 = (bf16[128,768]{1,0:T(8,128)(2,1)S(1)}, bf16[128,768]{1,0:T(8,128)(2,1)S(1)}, u32[]{:S(2)}, u32[]{:S(2)}) collective-permute-start(bf16[128,768]{1,0:T(8,128)(2,1)S(1)} %get-tuple-element.92), channel_id=1, source_target_pairs={{0,2},{1,3},{2,4},{3,5},{4,6},{5,7},{6,0},{7,1},{8,10},{9,11},{10,... | collective-permute-start | bytes 589832 | tf_op jit(solution)/shard_map/ppermute | solution.py:444
  58.4 9.7 %collective-permute-start.20 = (bf16[128,768]{1,0:T(8,128)(2,1)S(1)}, bf16[128,768]{1,0:T(8,128)(2,1)S(1)}, u32[]{:S(2)}, u32[]{:S(2)}) collective-permute-start(bf16[128,768]{1,0:T(8,128)(2,1)S(1)} %get-tuple-element.93), channel_id=1, source_target_pairs={{0,6},{1,7},{2,0},{3,1},{4,2},{5,3},{6,4},{7,5},{8,14},{9,15},{10,... | collective-permute-start | bytes 589832 | tf_op jit(solution)/shard_map/ppermute | solution.py:444
  68.5 8.6 %collective-permute-start.21 = (bf16[128,768]{1,0:T(8,128)(2,1)S(1)}, bf16[128,768]{1,0:T(8,128)(2,1)S(1)}, u32[]{:S(2)}, u32[]{:S(2)}) collective-permute-start(bf16[128,768]{1,0:T(8,128)(2,1)S(1)} %get-tuple-element.98), channel_id=1, source_target_pairs={{0,2},{1,3},{2,4},{3,5},{4,6},{5,7},{6,0},{7,1},{8,10},{9,11},{10,... | collective-permute-start | bytes 589832 | tf_op jit(solution)/shard_map/ppermute | solution.py:444

commit v4 on v3

--- a/solution.py
+++ b/solution.py
@@ -194,11 +194,19 @@
     )
 
 
+def ring(line):
+    return [*range(0, line, 2), *range(line - 1 - line % 2, 0, -2)]
+
+
 def block_of(shift, line, sibling):
     cut = lax.axis_index("cuts")
-    z = lax.rem(lax.div(cut, 2) + (shift + line), line)
     core = lax.rem(cut, 2)
-    return z * 2 + (1 - core if sibling else core)
+    z = lax.div(cut, 2)
+    order = ring(line)
+    ahead = jnp.int32(0)
+    for i, place in enumerate(order):
+        ahead = jnp.where(z == place, order[(i + shift) % line], ahead)
+    return ahead * 2 + (1 - core if sibling else core)
 
 
 def hidden_part(terms, w_down, line, total, factors, after):
@@ -285,41 +293,52 @@
     )
 
 
-def slot_part(gate_grad, up_grad, w_gate, w_up, shifts, line, sibling, arrived, experts, after):
+def slot_part(gate_grad, up_grad, w_gate, w_up, shifts, line, sibling, after):
     units, rows = gate_grad.shape
     blocks = len(shifts)
     columns = w_gate.shape[1] // (2 * line)
     tile = 256
-    capacity = rows // experts
-    split = arrived is not None
-
-    def kernel(gate_ref, up_ref, wg_ref, wu_ref, *refs):
+    dtype = BF16 if sibling else F32
+
+    def kernel(gate_ref, up_ref, wg_ref, wu_ref, out_ref):
         for b, shift in enumerate(shifts):
             base = block_of(shift, line, sibling) * columns
             for i in range(columns // tile):
                 span = pl.ds(pl.multiple_of(base + i * tile, tile), tile)
                 value = dot(wg_ref[0, span, :], gate_ref[...], NN)
-                value = (value + dot(wu_ref[0, span, :], up_ref[...], NN)).T
-                out = pl.ds(i * tile, tile)
-                if not split:
-                    refs[0][b, :, out] = value.astype(BF16)
-                    continue
-                value = (value + refs[0][b, :, out].astype(F32)).astype(BF16)
-                for r in range(experts):
-                    refs[1 + r][b, :, out] = value[r * capacity : (r + 1) * capacity]
-
-    if split:
-        out_shape = [shaped((blocks, capacity, columns), BF16)] * experts
-    else:
-        out_shape = [shaped((blocks, rows, columns), BF16)]
+                value = value + dot(wu_ref[0, span, :], up_ref[...], NN)
+                out_ref[b, :, pl.ds(i * tile, tile)] = value.T.astype(dtype)
+
     return call(
         kernel,
         "slot_part",
-        [gate_grad, up_grad, w_gate, w_up] + ([arrived] if split else []),
-        out_shape,
+        [gate_grad, up_grad, w_gate, w_up],
+        [shaped((blocks, rows, columns), dtype)],
         after,
         flops=4 * blocks * rows * columns * units,
         moved=4 * blocks * columns * units + 4 * rows * units,
+    )
+
+
+def add_halves(own, arrived, experts, after):
+    blocks, rows, columns = own.shape
+    capacity = rows // experts
+
+    def kernel(own_ref, other_ref, *outs):
+        for b in range(blocks):
+            for r in range(experts):
+                span = pl.ds(r * capacity, capacity)
+                value = own_ref[b, span, :] + other_ref[b, span, :].astype(F32)
+                outs[r][b] = value.astype(BF16)
+
+    return call(
+        kernel,
+        "add_halves",
+        [own, arrived],
+        [shaped((blocks, capacity, columns), BF16)] * experts,
+        after,
+        moved=SMALL,
+        flops=SMALL,
     )
 
 
@@ -440,7 +459,12 @@
         )
 
     def along(x, shift):
-        pairs = [(i, (i + 2 * shift) % cuts) for i in range(cuts)]
+        order = ring(line)
+        pairs = [
+            (2 * order[i] + core, 2 * order[(i + shift) % line] + core)
+            for i in range(line)
+            for core in range(2)
+        ]
         return lax.ppermute(x, "cuts", pairs)
 
     def swap(x):
@@ -477,22 +501,23 @@
 
     first, last = [2, 3], [1, 0]
     back = functools.partial(slot_part, gate_grad, up_grad, w_gate, w_up)
-    part, t = back(first, line, True, None, experts, [t])
-    other1 = swap(part)
-    part, t = back(last, line, True, None, experts, [t])
-    other2 = swap(part)
-    *pieces, t = back(first, line, False, other1, experts, [t])
-    got1 = exchange(pieces)
-    *pieces, t = back(last, line, False, other2, experts, [t])
-    got2 = exchange(pieces)
+    def exchanged(shifts, t):
+        part, t = back(shifts, line, True, [t])
+        arrived = swap(part)
+        part, t = back(shifts, line, False, [t])
+        *pieces, t = add_halves(part, arrived, experts, [t])
+        return exchange(pieces), t
+
+    got1, t = exchanged(first, t)
+    got2, t = exchanged(last, t)
     part2, part3, t = combine(got1, sel, [[], []], [BF16, BF16], [t])
     landed2 = along(part2, 1)
     landed3 = along(part3, 3)
     down, t = down_part(act, mine1, theirs1, one, line, None, w_down.shape, [t])
-    part1, part0, t = combine(got2, sel, [[landed2], [landed3]], [BF16, F32], [t])
+    part1, part0, t = combine(got2, sel, [[landed2], []], [BF16, F32], [t])
     landed1 = along(part1, 1)
     down, t = down_part(act, mine2, theirs2, two, line, down, w_down.shape, [t], DOWN_WEIGHT)
-    result = (part0 + landed1.astype(F32)).astype(BF16)
+    result = (part0 + landed3.astype(F32) + landed1.astype(F32)).astype(BF16)
     return result, down
 
 

time: 78 us -> 72.9 us (0.935)
  waiting for transfers between devices: 27 us -> 19.5 us
  starting transfers between devices: 24.2 us -> 26.3 us
    ppermute x6, waiting for transfers between devices: 17.1 us -> 6.83 us  [along(): return lax.ppermute(x, 'cuts', pairs)]
    ppermute x12, waiting for transfers between devices: 9.95 us -> 12.6 us  [exchange(): lax.ppermute(pieces[r], 'expert', [(i, i ^ r) for i in range(experts)])]
    ppermute x6, starting transfers between devices: 9.66 us -> 11.2 us  [along(): return lax.ppermute(x, 'cuts', pairs)]
    pallas_call x16 -> x18, Pallas kernels: 23.6 us -> 24 us  [call(): pl.pallas_call(body, out_shape=out_shape, in_specs=list(specs) + [VMEM] *...]
  transfers between devices with their start and end apart: 22 -> 22, of which waited for: 10 -> 9; matrix products, arithmetic and copies ran while one was open for 0% -> 0% of each run, Pallas kernels for 26% -> 26%
where the time goes in v4:
time: 72.9 us; the launch traced here: 72.7 us
  starting transfers between devices  26.3 us (36%)
  Pallas kernels  24 us (33%)
  waiting for transfers between devices  19.5 us (27%)
  local copies, waits for them, and re-layouts  1.29 us (2%)
  between operations  0.97 us (1%)
  other arithmetic  0.74 us (1%)
    pallas_call x18, Pallas kernels, call(): pl.pallas_call(body, out_shape=out_shape, in_specs=list(specs) + [VMEM] *...  24 us
    ppermute x12, starting transfers between devices, exchange(): lax.ppermute(pieces[r], 'expert', [(i, i ^ r) for i in range(experts)])  14 us
    ppermute x12, waiting for transfers between devices, exchange(): lax.ppermute(pieces[r], 'expert', [(i, i ^ r) for i in range(experts)])  12.6 us
    ppermute x6, starting transfers between devices, along(): return lax.ppermute(x, 'cuts', pairs)  11.2 us
    ppermute x6, waiting for transfers between devices, along(): return lax.ppermute(x, 'cuts', pairs)  6.83 us
  transfers between devices with their start and end apart: 22, of which 9 were waited for; matrix products, arithmetic and copies ran while one was open for 0% of the time, Pallas kernels for 26%

profile of v4, /device:TPU:0, one launch (start us, length us, event | category | flops | bytes accessed | tf_op | source)
XLA Modules:
  0.0 72.7 jit_solution(1538522820969121360)
XLA Ops:
  0.6 4.1 %collective-permute-start.1 = (bf16[128,768]{1,0:T(8,128)(2,1)}, bf16[128,768]{1,0:T(8,128)(2,1)S(1)}, u32[]{:S(2)}, u32[]{:S(2)}) collective-permute-start(bf16[128,768]{1,0:T(8,128)(2,1)} %refs_0_.2), channel_id=1, source_target_pairs={{0,4},{1,5},{4,6},{5,7},{6,2},{7,3},{2,0},{3,1},{8,12},{9,13},{12,... | collective-permute-start | bytes 589832 | tf_op jit(solution)/shard_map/ppermute | solution.py:468
  4.7 1.3 %route.1 = (bf16[256,128]{1,0:T(8,128)(2,1)S(1)}, f32[256,1]{1,0:T(8,128)S(1)}, bf16[128,768]{1,0:T(8,128)(2,1)S(1)}, f32[8,128]{1,0:T(8,128)S(1)}) custom-call(bf16[128,768]{1,0:T(8,128)(2,1)} %refs_0_.2, s32[2,128]{1,0:T(2,128)} %bitcast.8, f32[2,128]{1,0:T(2,128)} %bitcast.9), custom_call_target="tpu_custom_call" | custom-call | flops 1000 | bytes 1000 | tf_op jit(solution)/shard_map/route/pallas_call | solution.py:45
  6.0 4.4 %collective-permute-done.1.refs_1_ = bf16[128,768]{1,0:T(8,128)(2,1)S(1)} collective-permute-done((bf16[128,768]{1,0:T(8,128)(2,1)}, bf16[128,768]{1,0:T(8,128)(2,1)S(1)}, u32[]{:S(2)}, u32[]{:S(2)}) %collective-permute-start.1) | collective-permute-done | bytes 196640 | tf_op jit(solution)/shard_map/ppermute | solution.py:468
  10.4 3.3 %collective-permute-start.2 = (bf16[128,768]{1,0:T(8,128)(2,1)S(1)}, bf16[128,768]{1,0:T(8,128)(2,1)S(1)}, u32[]{:S(2)}, u32[]{:S(2)}) collective-permute-start(bf16[128,768]{1,0:T(8,128)(2,1)S(1)} %collective-permute-done.1.refs_1_), channel_id=1, source_target_pairs={{0,4},{1,5},{4,6},{5,7},{6,2},{7,3},{2,0},{3,1},{8,12},{9,13},{12,... | collective-permute-start | bytes 589832 | tf_op jit(solution)/shard_map/ppermute | solution.py:468
  13.7 0.4 pack.2
  14.0 1.6 %collective-permute-start.6 = (bf16[2,64,768]{2,1,0:T(8,128)(2,1)S(1)}, bf16[2,64,768]{2,1,0:T(8,128)(2,1)S(1)}, u32[]{:S(2)}, u32[]{:S(2)}) collective-permute-start(bf16[2,64,768]{2,1,0:T(8,128)(2,1)S(1)} %get-tuple-element.66), channel_id=1, source_target_pairs={{0,8},{8,0},{16,24},{24,16},{1,9},{9,1},{17,25},{25,17},{2,10},{10... | collective-permute-start | bytes 589832 | tf_op jit(solution)/shard_map/ppermute | solution.py:475
  15.6 1.5 %collective-permute-start.7 = (bf16[2,64,768]{2,1,0:T(8,128)(2,1)S(1)}, bf16[2,64,768]{2,1,0:T(8,128)(2,1)S(1)}, u32[]{:S(2)}, u32[]{:S(2)}) collective-permute-start(bf16[2,64,768]{2,1,0:T(8,128)(2,1)S(1)} %get-tuple-element.67), channel_id=1, source_target_pairs={{0,16},{8,24},{16,0},{24,8},{1,17},{9,25},{17,1},{25,9},{2,18},{10... | collective-permute-start | bytes 589832 | tf_op jit(solution)/shard_map/ppermute | solution.py:475
  17.1 0.5 collective-permute-start.8
  17.6 1.4 %collective-permute-done.2.refs_1_ = bf16[128,768]{1,0:T(8,128)(2,1)S(1)} collective-permute-done((bf16[128,768]{1,0:T(8,128)(2,1)S(1)}, bf16[128,768]{1,0:T(8,128)(2,1)S(1)}, u32[]{:S(2)}, u32[]{:S(2)}) %collective-permute-start.2) | collective-permute-done | bytes 196640 | tf_op jit(solution)/shard_map/ppermute | solution.py:468
  18.9 0.4 pack.3
  19.3 1.6 %collective-permute-start.3 = (bf16[2,64,768]{2,1,0:T(8,128)(2,1)S(1)}, bf16[2,64,768]{2,1,0:T(8,128)(2,1)S(1)}, u32[]{:S(2)}, u32[]{:S(2)}) collective-permute-start(bf16[2,64,768]{2,1,0:T(8,128)(2,1)S(1)} %get-tuple-element.62), channel_id=1, source_target_pairs={{0,8},{8,0},{16,24},{24,16},{1,9},{9,1},{17,25},{25,17},{2,10},{10... | collective-permute-start | bytes 589832 | tf_op jit(solution)/shard_map/ppermute | solution.py:475
  20.9 1.5 %collective-permute-start.4 = (bf16[2,64,768]{2,1,0:T(8,128)(2,1)S(1)}, bf16[2,64,768]{2,1,0:T(8,128)(2,1)S(1)}, u32[]{:S(2)}, u32[]{:S(2)}) collective-permute-start(bf16[2,64,768]{2,1,0:T(8,128)(2,1)S(1)} %get-tuple-element.63), channel_id=1, source_target_pairs={{0,16},{8,24},{16,0},{24,8},{1,17},{9,25},{17,1},{25,9},{2,18},{10... | collective-permute-start | bytes 589832 | tf_op jit(solution)/shard_map/ppermute | solution.py:475
  22.4 0.6 collective-permute-start.5
  23.0 2.4 %activations.1 = (f32[1024,256]{1,0:T(8,128)S(1)}, f32[1024,256]{1,0:T(8,128)S(1)}, bf16[1024,256]{1,0:T(8,128)(2,1)S(1)}, f32[8,128]{1,0:T(8,128)S(1)}) custom-call(bf16[1,4,64,1024]{3,2,1,0:T(8,128)(2,1)} %refs_0_.3, bf16[1,4,64,1024]{3,2,1,0:T(8,128)(2,1)} %refs_1_.2, f32[8,128]{1,0:T(8,128)S(1)} %get-tuple-element.69.refs_2_), custom_call_target="tpu_custom_call" | custom-call | flops 12000000000 | bytes 1000 | tf_op jit(solution)/shard_map/activations/pallas_call | solution.py:45
  25.5 0.1 collective-permute-start.10
  25.5 3.1 %collective-permute-done.3.refs_1_ = bf16[2,64,768]{2,1,0:T(8,128)(2,1)S(1)} collective-permute-done((bf16[2,64,768]{2,1,0:T(8,128)(2,1)S(1)}, bf16[2,64,768]{2,1,0:T(8,128)(2,1)S(1)}, u32[]{:S(2)}, u32[]{:S(2)}) %collective-permute-start.3) | collective-permute-done | bytes 196640 | tf_op jit(solution)/shard_map/ppermute | solution.py:475
  28.6 4.0 %collective-permute-done.4.refs_2_ = bf16[2,64,768]{2,1,0:T(8,128)(2,1)S(1)} collective-permute-done((bf16[2,64,768]{2,1,0:T(8,128)(2,1)S(1)}, bf16[2,64,768]{2,1,0:T(8,128)(2,1)S(1)}, u32[]{:S(2)}, u32[]{:S(2)}) %collective-permute-start.4) | collective-permute-done | bytes 196640 | tf_op jit(solution)/shard_map/ppermute | solution.py:475
  32.6 0.1 collective-permute-start.9
  32.8 2.6 %hidden_part.2 = (f32[1024,256]{1,0:T(8,128)S(1)}, f32[8,128]{1,0:T(8,128)S(1)}) custom-call(bf16[2,256,768]{2,1,0:T(8,128)(2,1)S(1)} %get-tuple-element.73.refs_0_.refs_1_, bf16[2,256,768]{2,1,0:T(8,128)(2,1)S(1)} %collective-permute-done.10.refs_1_.refs_2_, bf16[2,256,768]{2,1,0:T(8,128)(2,1)S(1)} %get-tuple-element.72.refs_2_.refs_1_, ...), custom_call_target="tpu_custom_call" | custom-call | flops 1000 | bytes 1000 | tf_op jit(solution)/shard_map/hidden_part/pallas_call | solution.py:45
  35.5 1.1 %hidden_part.3 = (bf16[1024,256]{1,0:T(8,128)(2,1)S(1)}, bf16[1024,256]{1,0:T(8,128)(2,1)S(1)}, f32[8,128]{1,0:T(8,128)S(1)}) custom-call(bf16[2,256,768]{2,1,0:T(8,128)(2,1)S(1)} %collective-permute-done.9.refs_0_.refs_2_, bf16[1,1024,6144]{2,1,0:T(8,128)(2,1)S(1)} %bitcast.7, f32[1024,256]{1,0:T(8,128)S(1)} %get-tuple-element.75.refs_2_, ...), custom_call_target="tpu_custom_call" | custom-call | flops 1000 | bytes 1000 | tf_op jit(solution)/shard_map/hidden_part/pallas_call | solution.py:45
  36.6 1.3 %slice-done.5 = s8[4194304]{0:T(1024)(128)(4,1)S(1)} async-done(((s8[12582912]{0:T(1024)(128)(4,1)}), s8[4194304]{0:T(1024)(128)(4,1)S(1)}, s32[]{:S(2)}) %slice-start.5) | async-done | bytes 4194328
  37.9 1.9 %slot_part.4 = (bf16[2,256,768]{2,1,0:T(8,128)(2,1)S(1)}, f32[8,128]{1,0:T(8,128)S(1)}) custom-call(bf16[1024,256]{1,0:T(8,128)(2,1)S(1)} %get-tuple-element.79.refs_0_, bf16[1024,256]{1,0:T(8,128)(2,1)S(1)} %get-tuple-element.80.refs_1_, bf16[1,6144,1024]{2,1,0:T(8,128)(2,1)S(1)} %bitcast.3, bf16[1,6144,1024]{2,1,0:T(8,128)(2,1)S(1)} %bitcast.5, ...), custom_call_target="tpu_custom_call" | custom-call | flops 1610612736 | bytes 7340032 | tf_op jit(solution)/shard_map/slot_part/pallas_call | solution.py:45
  39.8 0.5 collective-permute-start.11
  40.3 1.9 %slot_part.5 = (f32[2,256,768]{2,1,0:T(8,128)S(1)}, f32[8,128]{1,0:T(8,128)S(1)}) custom-call(bf16[1024,256]{1,0:T(8,128)(2,1)S(1)} %get-tuple-element.79.refs_0_, bf16[1024,256]{1,0:T(8,128)(2,1)S(1)} %get-tuple-element.80.refs_1_, bf16[1,6144,1024]{2,1,0:T(8,128)(2,1)S(1)} %bitcast.3, bf16[1,6144,1024]{2,1,0:T(8,128)(2,1)S(1)} %bitcast.5, ...), custom_call_target="tpu_custom_call" | custom-call | flops 1610612736 | bytes 7340032 | tf_op jit(solution)/shard_map/slot_part/pallas_call | solution.py:45
  42.3 0.2 add_halves.2
  42.5 1.9 %slot_part.6 = (bf16[2,256,768]{2,1,0:T(8,128)(2,1)S(1)}, f32[8,128]{1,0:T(8,128)S(1)}) custom-call(bf16[1024,256]{1,0:T(8,128)(2,1)S(1)} %get-tuple-element.79.refs_0_, bf16[1024,256]{1,0:T(8,128)(2,1)S(1)} %get-tuple-element.80.refs_1_, bf16[1,6144,1024]{2,1,0:T(8,128)(2,1)S(1)} %bitcast.3, bf16[1,6144,1024]{2,1,0:T(8,128)(2,1)S(1)} %bitcast.5, ...), custom_call_target="tpu_custom_call" | custom-call | flops 1610612736 | bytes 7340032 | tf_op jit(solution)/shard_map/slot_part/pallas_call | solution.py:45
  44.4 0.4 collective-permute-start.12
  44.8 0.9 %collective-permute-start.16 = (bf16[2,64,768]{2,1,0:T(8,128)(2,1)S(1)}, bf16[2,64,768]{2,1,0:T(8,128)(2,1)S(1)}, u32[]{:S(2)}, u32[]{:S(2)}) collective-permute-start(bf16[2,64,768]{2,1,0:T(8,128)(2,1)S(1)} %get-tuple-element.96), channel_id=1, source_target_pairs={{0,8},{8,0},{16,24},{24,16},{1,9},{9,1},{17,25},{25,17},{2,10},{10... | collective-permute-start | bytes 589832 | tf_op jit(solution)/shard_map/ppermute | solution.py:475
  45.7 0.8 %collective-permute-start.17 = (bf16[2,64,768]{2,1,0:T(8,128)(2,1)S(1)}, bf16[2,64,768]{2,1,0:T(8,128)(2,1)S(1)}, u32[]{:S(2)}, u32[]{:S(2)}) collective-permute-start(bf16[2,64,768]{2,1,0:T(8,128)(2,1)S(1)} %get-tuple-element.97), channel_id=1, source_target_pairs={{0,16},{8,24},{16,0},{24,8},{1,17},{9,25},{17,1},{25,9},{2,18},{10... | collective-permute-start | bytes 589832 | tf_op jit(solution)/shard_map/ppermute | solution.py:475
  46.5 1.7 %collective-permute-start.18 = (bf16[2,64,768]{2,1,0:T(8,128)(2,1)S(1)}, bf16[2,64,768]{2,1,0:T(8,128)(2,1)S(1)}, u32[]{:S(2)}, u32[]{:S(2)}) collective-permute-start(bf16[2,64,768]{2,1,0:T(8,128)(2,1)S(1)} %get-tuple-element.98), channel_id=1, source_target_pairs={{0,24},{8,16},{16,8},{24,0},{1,25},{9,17},{17,9},{25,1},{2,26},{10... | collective-permute-start | bytes 589832 | tf_op jit(solution)/shard_map/ppermute | solution.py:475
  48.3 1.9 %slot_part.7 = (f32[2,256,768]{2,1,0:T(8,128)S(1)}, f32[8,128]{1,0:T(8,128)S(1)}) custom-call(bf16[1024,256]{1,0:T(8,128)(2,1)S(1)} %get-tuple-element.79.refs_0_, bf16[1024,256]{1,0:T(8,128)(2,1)S(1)} %get-tuple-element.80.refs_1_, bf16[1,6144,1024]{2,1,0:T(8,128)(2,1)S(1)} %bitcast.3, bf16[1,6144,1024]{2,1,0:T(8,128)(2,1)S(1)} %bitcast.5, ...), custom_call_target="tpu_custom_call" | custom-call | flops 1610612736 | bytes 7340032 | tf_op jit(solution)/shard_map/slot_part/pallas_call | solution.py:45
  50.2 0.2 add_halves.3
  50.4 1.0 %collective-permute-start.13 = (bf16[2,64,768]{2,1,0:T(8,128)(2,1)S(1)}, bf16[2,64,768]{2,1,0:T(8,128)(2,1)S(1)}, u32[]{:S(2)}, u32[]{:S(2)}) collective-permute-start(bf16[2,64,768]{2,1,0:T(8,128)(2,1)S(1)} %get-tuple-element.92), channel_id=1, source_target_pairs={{0,8},{8,0},{16,24},{24,16},{1,9},{9,1},{17,25},{25,17},{2,10},{10... | collective-permute-start | bytes 589832 | tf_op jit(solution)/shard_map/ppermute | solution.py:475
  51.4 0.8 %collective-permute-start.14 = (bf16[2,64,768]{2,1,0:T(8,128)(2,1)S(1)}, bf16[2,64,768]{2,1,0:T(8,128)(2,1)S(1)}, u32[]{:S(2)}, u32[]{:S(2)}) collective-permute-start(bf16[2,64,768]{2,1,0:T(8,128)(2,1)S(1)} %get-tuple-element.93), channel_id=1, source_target_pairs={{0,16},{8,24},{16,0},{24,8},{1,17},{9,25},{17,1},{25,9},{2,18},{10... | collective-permute-start | bytes 589832 | tf_op jit(solution)/shard_map/ppermute | solution.py:475
  52.2 0.3 collective-permute-done.16.refs_1_
  52.5 1.4 %collective-permute-start.15 = (bf16[2,64,768]{2,1,0:T(8,128)(2,1)S(1)}, bf16[2,64,768]{2,1,0:T(8,128)(2,1)S(1)}, u32[]{:S(2)}, u32[]{:S(2)}) collective-permute-start(bf16[2,64,768]{2,1,0:T(8,128)(2,1)S(1)} %get-tuple-element.94), channel_id=1, source_target_pairs={{0,24},{8,16},{16,8},{24,0},{1,25},{9,17},{17,9},{25,1},{2,26},{10... | collective-permute-start | bytes 589832 | tf_op jit(solution)/shard_map/ppermute | solution.py:475
  54.0 3.5 %collective-permute-done.18.refs_3_ = bf16[2,64,768]{2,1,0:T(8,128)(2,1)S(1)} collective-permute-done((bf16[2,64,768]{2,1,0:T(8,128)(2,1)S(1)}, bf16[2,64,768]{2,1,0:T(8,128)(2,1)S(1)}, u32[]{:S(2)}, u32[]{:S(2)}) %collective-permute-start.18) | collective-permute-done | bytes 196640 | tf_op jit(solution)/shard_map/ppermute | solution.py:475
  57.4 0.3 combine.2
  57.7 1.0 %collective-permute-start.19 = (bf16[128,768]{1,0:T(8,128)(2,1)S(1)}, bf16[128,768]{1,0:T(8,128)(2,1)S(1)}, u32[]{:S(2)}, u32[]{:S(2)}) collective-permute-start(bf16[128,768]{1,0:T(8,128)(2,1)S(1)} %get-tuple-element.100), channel_id=1, source_target_pairs={{0,4},{1,5},{4,6},{5,7},{6,2},{7,3},{2,0},{3,1},{8,12},{9,13},{12,... | collective-permute-start | bytes 589832 | tf_op jit(solution)/shard_map/ppermute | solution.py:468
  58.7 1.3 %collective-permute-start.20 = (bf16[128,768]{1,0:T(8,128)(2,1)S(1)}, bf16[128,768]{1,0:T(8,128)(2,1)S(1)}, u32[]{:S(2)}, u32[]{:S(2)}) collective-permute-start(bf16[128,768]{1,0:T(8,128)(2,1)S(1)} %get-tuple-element.105), channel_id=1, source_target_pairs={{0,2},{1,3},{4,0},{5,1},{6,4},{7,5},{2,6},{3,7},{8,10},{9,11},{12,... | collective-permute-start | bytes 589832 | tf_op jit(solution)/shard_map/ppermute | solution.py:468
  60.0 3.3 %down_part.2 = (bf16[1,1024,6144]{2,1,0:T(8,128)(2,1)}, f32[8,128]{1,0:T(8,128)S(1)}) custom-call(bf16[1024,256]{1,0:T(8,128)(2,1)S(1)} %get-tuple-element.101.refs_0_, bf16[2,256,768]{2,1,0:T(8,128)(2,1)S(1)} %get-tuple-element.73.refs_0_.refs_1_, bf16[2,256,768]{2,1,0:T(8,128)(2,1)S(1)} %collective-permute-done.10.refs_1_.refs_2_, ...), custom_call_target="tpu_custom_call" | custom-call | flops 1610612736 | bytes 6291456 | tf_op jit(solution)/shard_map/down_part/pallas_call | solution.py:45
  63.3 1.8 %collective-permute-done.15.refs_3_ = bf16[2,64,768]{2,1,0:T(8,128)(2,1)S(1)} collective-permute-done((bf16[2,64,768]{2,1,0:T(8,128)(2,1)S(1)}, bf16[2,64,768]{2,1,0:T(8,128)(2,1)S(1)}, u32[]{:S(2)}, u32[]{:S(2)}) %collective-permute-start.15) | collective-permute-done | bytes 196640 | tf_op jit(solution)/shard_map/ppermute | solution.py:475
  65.1 0.5 collective-permute-done.19.refs_5_
  65.7 0.3 combine.3
  66.0 1.6 %collective-permute-start.21 = (bf16[128,768]{1,0:T(8,128)(2,1)S(1)}, bf16[128,768]{1,0:T(8,128)(2,1)S(1)}, u32[]{:S(2)}, u32[]{:S(2)}) collective-permute-start(bf16[128,768]{1,0:T(8,128)(2,1)S(1)} %get-tuple-element.106), channel_id=1, source_target_pairs={{0,4},{1,5},{4,6},{5,7},{6,2},{7,3},{2,0},{3,1},{8,12},{9,13},{12,... | collective-permute-start | bytes 589832 | tf_op jit(solution)/shard_map/ppermute | solution.py:468
  67.5 3.9 %down_part.3 = (bf16[1,1024,6144]{2,1,0:T(8,128)(2,1)}, f32[8,128]{1,0:T(8,128)}) custom-call(bf16[1024,256]{1,0:T(8,128)(2,1)S(1)} %get-tuple-element.101.refs_0_, bf16[2,256,768]{2,1,0:T(8,128)(2,1)S(1)} %get-tuple-element.72.refs_2_.refs_1_, bf16[2,256,768]{2,1,0:T(8,128)(2,1)S(1)} %collective-permute-done.9.refs_0_.refs_2_, ...), custom_call_target="tpu_custom_call", output_to_operand_aliasing={{0}: (3, {})} | custom-call | tf_op jit(solution)/shard_map/down_part/pallas_call | solution.py:45
  71.4 0.5 collective-permute-done.21
  72.0 0.7 %add_convert_fusion = bf16[128,768]{1,0:T(8,128)(2,1)} fusion(bf16[128,768]{1,0:T(8,128)(2,1)S(1)} %collective-permute-done.21, f32[128,768]{1,0:T(8,128)S(1)} %get-tuple-element.104, bf16[128,768]{1,0:T(8,128)(2,1)S(1)} %collective-permute-done.20), kind=kLoop, calls=%fused_computation | loop fusion | flops 491520 | bytes 983040 | tf_op jit(solution)/shard_map/convert_element_type | solution.py:520
  (36 shorter events, 0.2 us)
Async XLA Ops:
  0.6 9.8 %collective-permute-start.1 = (bf16[128,768]{1,0:T(8,128)(2,1)}, bf16[128,768]{1,0:T(8,128)(2,1)S(1)}, u32[]{:S(2)}, u32[]{:S(2)}) collective-permute-start(bf16[128,768]{1,0:T(8,128)(2,1)} %refs_0_.2), channel_id=1, source_target_pairs={{0,4},{1,5},{4,6},{5,7},{6,2},{7,3},{2,0},{3,1},{8,12},{9,13},{12,... | collective-permute-start | bytes 589832 | tf_op jit(solution)/shard_map/ppermute | solution.py:468
  4.7 12.9 %collective-permute-start = (bf16[128,768]{1,0:T(8,128)(2,1)}, bf16[128,768]{1,0:T(8,128)(2,1)S(1)}, u32[]{:S(2)}, u32[]{:S(2)}) collective-permute-start(bf16[128,768]{1,0:T(8,128)(2,1)} %refs_0_.2), channel_id=1, source_target_pairs={{0,2},{1,3},{4,0},{5,1},{6,4},{7,5},{2,6},{3,7},{8,10},{9,11},{12,... | collective-permute-start | bytes 589832 | tf_op jit(solution)/shard_map/ppermute | solution.py:468
  10.4 8.5 %collective-permute-start.2 = (bf16[128,768]{1,0:T(8,128)(2,1)S(1)}, bf16[128,768]{1,0:T(8,128)(2,1)S(1)}, u32[]{:S(2)}, u32[]{:S(2)}) collective-permute-start(bf16[128,768]{1,0:T(8,128)(2,1)S(1)} %collective-permute-done.1.refs_1_), channel_id=1, source_target_pairs={{0,4},{1,5},{4,6},{5,7},{6,2},{7,3},{2,0},{3,1},{8,12},{9,13},{12,... | collective-permute-start | bytes 589832 | tf_op jit(solution)/shard_map/ppermute | solution.py:468
  14.0 8.4 %collective-permute-start.6 = (bf16[2,64,768]{2,1,0:T(8,128)(2,1)S(1)}, bf16[2,64,768]{2,1,0:T(8,128)(2,1)S(1)}, u32[]{:S(2)}, u32[]{:S(2)}) collective-permute-start(bf16[2,64,768]{2,1,0:T(8,128)(2,1)S(1)} %get-tuple-element.66), channel_id=1, source_target_pairs={{0,8},{8,0},{16,24},{24,16},{1,9},{9,1},{17,25},{25,17},{2,10},{10... | collective-permute-start | bytes 589832 | tf_op jit(solution)/shard_map/ppermute | solution.py:475
  15.6 9.8 %collective-permute-start.7 = (bf16[2,64,768]{2,1,0:T(8,128)(2,1)S(1)}, bf16[2,64,768]{2,1,0:T(8,128)(2,1)S(1)}, u32[]{:S(2)}, u32[]{:S(2)}) collective-permute-start(bf16[2,64,768]{2,1,0:T(8,128)(2,1)S(1)} %get-tuple-element.67), channel_id=1, source_target_pairs={{0,16},{8,24},{16,0},{24,8},{1,17},{9,25},{17,1},{25,9},{2,18},{10... | collective-permute-start | bytes 589832 | tf_op jit(solution)/shard_map/ppermute | solution.py:475
  17.1 8.3 %collective-permute-start.8 = (bf16[2,64,768]{2,1,0:T(8,128)(2,1)S(1)}, bf16[2,64,768]{2,1,0:T(8,128)(2,1)S(1)}, u32[]{:S(2)}, u32[]{:S(2)}) collective-permute-start(bf16[2,64,768]{2,1,0:T(8,128)(2,1)S(1)} %get-tuple-element.68), channel_id=1, source_target_pairs={{0,24},{8,16},{16,8},{24,0},{1,25},{9,17},{17,9},{25,1},{2,26},{10... | collective-permute-start | bytes 589832 | tf_op jit(solution)/shard_map/ppermute | solution.py:475
  18.9 13.8 %slice-start.6 = ((s8[12582912]{0:T(1024)(128)(4,1)}), s8[4194304]{0:T(1024)(128)(4,1)S(1)}, s32[]{:S(2)}) async-start(s8[12582912]{0:T(1024)(128)(4,1)} %bitcast.6), calls=%async_computation.6 | async-start | bytes 8388608
  19.3 9.3 %collective-permute-start.3 = (bf16[2,64,768]{2,1,0:T(8,128)(2,1)S(1)}, bf16[2,64,768]{2,1,0:T(8,128)(2,1)S(1)}, u32[]{:S(2)}, u32[]{:S(2)}) collective-permute-start(bf16[2,64,768]{2,1,0:T(8,128)(2,1)S(1)} %get-tuple-element.62), channel_id=1, source_target_pairs={{0,8},{8,0},{16,24},{24,16},{1,9},{9,1},{17,25},{25,17},{2,10},{10... | collective-permute-start | bytes 589832 | tf_op jit(solution)/shard_map/ppermute | solution.py:475
  20.9 11.7 %collective-permute-start.4 = (bf16[2,64,768]{2,1,0:T(8,128)(2,1)S(1)}, bf16[2,64,768]{2,1,0:T(8,128)(2,1)S(1)}, u32[]{:S(2)}, u32[]{:S(2)}) collective-permute-start(bf16[2,64,768]{2,1,0:T(8,128)(2,1)S(1)} %get-tuple-element.63), channel_id=1, source_target_pairs={{0,16},{8,24},{16,0},{24,8},{1,17},{9,25},{17,1},{25,9},{2,18},{10... | collective-permute-start | bytes 589832 | tf_op jit(solution)/shard_map/ppermute | solution.py:475
  22.4 10.2 %collective-permute-start.5 = (bf16[2,64,768]{2,1,0:T(8,128)(2,1)S(1)}, bf16[2,64,768]{2,1,0:T(8,128)(2,1)S(1)}, u32[]{:S(2)}, u32[]{:S(2)}) collective-permute-start(bf16[2,64,768]{2,1,0:T(8,128)(2,1)S(1)} %get-tuple-element.64), channel_id=1, source_target_pairs={{0,24},{8,16},{16,8},{24,0},{1,25},{9,17},{17,9},{25,1},{2,26},{10... | collective-permute-start | bytes 589832 | tf_op jit(solution)/shard_map/ppermute | solution.py:475
  23.0 12.5 %slice-start = ((s8[12582912]{0:T(1024)(128)(4,1)}), s8[4194304]{0:T(1024)(128)(4,1)S(1)}, s32[]{:S(2)}) async-start(s8[12582912]{0:T(1024)(128)(4,1)} %bitcast.2), calls=%async_computation | async-start | bytes 8388608
  23.0 9.8 %slice-start.7 = ((s8[12582912]{0:T(1024)(128)(4,1)}), s8[4194304]{0:T(1024)(128)(4,1)S(1)}, s32[]{:S(2)}) async-start(s8[12582912]{0:T(1024)(128)(4,1)} %bitcast.6), calls=%async_computation.7 | async-start | bytes 8388608
  23.0 9.8 %slice-start.8 = ((s8[12582912]{0:T(1024)(128)(4,1)}), s8[4194304]{0:T(1024)(128)(4,1)S(1)}, s32[]{:S(2)}) async-start(s8[12582912]{0:T(1024)(128)(4,1)} %bitcast.6), calls=%async_computation.8 | async-start | bytes 8388608
  23.0 12.5 %slice-start.1 = ((s8[12582912]{0:T(1024)(128)(4,1)}), s8[4194304]{0:T(1024)(128)(4,1)S(1)}, s32[]{:S(2)}) async-start(s8[12582912]{0:T(1024)(128)(4,1)} %bitcast.2), calls=%async_computation.1 | async-start | bytes 8388608
  23.0 12.5 %slice-start.2 = ((s8[12582912]{0:T(1024)(128)(4,1)}), s8[4194304]{0:T(1024)(128)(4,1)S(1)}, s32[]{:S(2)}) async-start(s8[12582912]{0:T(1024)(128)(4,1)} %bitcast.2), calls=%async_computation.2 | async-start | bytes 8388608
  25.5 7.3 %collective-permute-start.10 = (bf16[2,256,768]{2,1,0:T(8,128)(2,1)S(1)}, bf16[2,256,768]{2,1,0:T(8,128)(2,1)S(1)}, u32[]{:S(2)}, u32[]{:S(2)}) collective-permute-start(bf16[2,256,768]{2,1,0:T(8,128)(2,1)S(1)} %get-tuple-element.73.refs_0_.refs_1_), channel_id=1, source_target_pairs={{0,1},{1,0},{2,3},{3,2},{4,5},{5,4},{6,7},{7,6},{8,9},{9,8},{10,11... | collective-permute-start | bytes 2359304 | tf_op jit(solution)/shard_map/ppermute | solution.py:471
  32.6 2.8 %collective-permute-start.9 = (bf16[2,256,768]{2,1,0:T(8,128)(2,1)S(1)}, bf16[2,256,768]{2,1,0:T(8,128)(2,1)S(1)}, u32[]{:S(2)}, u32[]{:S(2)}) collective-permute-start(bf16[2,256,768]{2,1,0:T(8,128)(2,1)S(1)} %get-tuple-element.72.refs_2_.refs_1_), channel_id=1, source_target_pairs={{0,1},{1,0},{2,3},{3,2},{4,5},{5,4},{6,7},{7,6},{8,9},{9,8},{10,11... | collective-permute-start | bytes 2359304 | tf_op jit(solution)/shard_map/ppermute | solution.py:471
  32.8 3.8 %slice-start.3 = ((s8[12582912]{0:T(1024)(128)(4,1)}), s8[4194304]{0:T(1024)(128)(4,1)S(1)}, s32[]{:S(2)}) async-start(s8[12582912]{0:T(1024)(128)(4,1)} %bitcast.4), calls=%async_computation.3 | async-start | bytes 8388608
  32.8 3.8 %slice-start.4 = ((s8[12582912]{0:T(1024)(128)(4,1)}), s8[4194304]{0:T(1024)(128)(4,1)S(1)}, s32[]{:S(2)}) async-start(s8[12582912]{0:T(1024)(128)(4,1)} %bitcast.4), calls=%async_computation.4 | async-start | bytes 8388608
  35.5 2.4 %slice-start.5 = ((s8[12582912]{0:T(1024)(128)(4,1)}), s8[4194304]{0:T(1024)(128)(4,1)S(1)}, s32[]{:S(2)}) async-start(s8[12582912]{0:T(1024)(128)(4,1)} %bitcast.4), calls=%async_computation.5 | async-start | bytes 8388608
  39.8 2.5 %collective-permute-start.11 = (bf16[2,256,768]{2,1,0:T(8,128)(2,1)S(1)}, bf16[2,256,768]{2,1,0:T(8,128)(2,1)S(1)}, u32[]{:S(2)}, u32[]{:S(2)}) collective-permute-start(bf16[2,256,768]{2,1,0:T(8,128)(2,1)S(1)} %get-tuple-element.84), channel_id=1, source_target_pairs={{0,1},{1,0},{2,3},{3,2},{4,5},{5,4},{6,7},{7,6},{8,9},{9,8},{10,11... | collective-permute-start | bytes 2359304 | tf_op jit(solution)/shard_map/ppermute | solution.py:471
  44.4 5.8 %collective-permute-start.12 = (bf16[2,256,768]{2,1,0:T(8,128)(2,1)S(1)}, bf16[2,256,768]{2,1,0:T(8,128)(2,1)S(1)}, u32[]{:S(2)}, u32[]{:S(2)}) collective-permute-start(bf16[2,256,768]{2,1,0:T(8,128)(2,1)S(1)} %get-tuple-element.89), channel_id=1, source_target_pairs={{0,1},{1,0},{2,3},{3,2},{4,5},{5,4},{6,7},{7,6},{8,9},{9,8},{10,11... | collective-permute-start | bytes 2359304 | tf_op jit(solution)/shard_map/ppermute | solution.py:471
  44.8 7.7 %collective-permute-start.16 = (bf16[2,64,768]{2,1,0:T(8,128)(2,1)S(1)}, bf16[2,64,768]{2,1,0:T(8,128)(2,1)S(1)}, u32[]{:S(2)}, u32[]{:S(2)}) collective-permute-start(bf16[2,64,768]{2,1,0:T(8,128)(2,1)S(1)} %get-tuple-element.96), channel_id=1, source_target_pairs={{0,8},{8,0},{16,24},{24,16},{1,9},{9,1},{17,25},{25,17},{2,10},{10... | collective-permute-start | bytes 589832 | tf_op jit(solution)/shard_map/ppermute | solution.py:475
  45.7 8.3 %collective-permute-start.17 = (bf16[2,64,768]{2,1,0:T(8,128)(2,1)S(1)}, bf16[2,64,768]{2,1,0:T(8,128)(2,1)S(1)}, u32[]{:S(2)}, u32[]{:S(2)}) collective-permute-start(bf16[2,64,768]{2,1,0:T(8,128)(2,1)S(1)} %get-tuple-element.97), channel_id=1, source_target_pairs={{0,16},{8,24},{16,0},{24,8},{1,17},{9,25},{17,1},{25,9},{2,18},{10... | collective-permute-start | bytes 589832 | tf_op jit(solution)/shard_map/ppermute | solution.py:475
  46.5 10.9 %collective-permute-start.18 = (bf16[2,64,768]{2,1,0:T(8,128)(2,1)S(1)}, bf16[2,64,768]{2,1,0:T(8,128)(2,1)S(1)}, u32[]{:S(2)}, u32[]{:S(2)}) collective-permute-start(bf16[2,64,768]{2,1,0:T(8,128)(2,1)S(1)} %get-tuple-element.98), channel_id=1, source_target_pairs={{0,24},{8,16},{16,8},{24,0},{1,25},{9,17},{17,9},{25,1},{2,26},{10... | collective-permute-start | bytes 589832 | tf_op jit(solution)/shard_map/ppermute | solution.py:475
  50.4 12.9 %collective-permute-start.13 = (bf16[2,64,768]{2,1,0:T(8,128)(2,1)S(1)}, bf16[2,64,768]{2,1,0:T(8,128)(2,1)S(1)}, u32[]{:S(2)}, u32[]{:S(2)}) collective-permute-start(bf16[2,64,768]{2,1,0:T(8,128)(2,1)S(1)} %get-tuple-element.92), channel_id=1, source_target_pairs={{0,8},{8,0},{16,24},{24,16},{1,9},{9,1},{17,25},{25,17},{2,10},{10... | collective-permute-start | bytes 589832 | tf_op jit(solution)/shard_map/ppermute | solution.py:475
  51.4 11.9 %collective-permute-start.14 = (bf16[2,64,768]{2,1,0:T(8,128)(2,1)S(1)}, bf16[2,64,768]{2,1,0:T(8,128)(2,1)S(1)}, u32[]{:S(2)}, u32[]{:S(2)}) collective-permute-start(bf16[2,64,768]{2,1,0:T(8,128)(2,1)S(1)} %get-tuple-element.93), channel_id=1, source_target_pairs={{0,16},{8,24},{16,0},{24,8},{1,17},{9,25},{17,1},{25,9},{2,18},{10... | collective-permute-start | bytes 589832 | tf_op jit(solution)/shard_map/ppermute | solution.py:475
  52.5 12.6 %collective-permute-start.15 = (bf16[2,64,768]{2,1,0:T(8,128)(2,1)S(1)}, bf16[2,64,768]{2,1,0:T(8,128)(2,1)S(1)}, u32[]{:S(2)}, u32[]{:S(2)}) collective-permute-start(bf16[2,64,768]{2,1,0:T(8,128)(2,1)S(1)} %get-tuple-element.94), channel_id=1, source_target_pairs={{0,24},{8,16},{16,8},{24,0},{1,25},{9,17},{17,9},{25,1},{2,26},{10... | collective-permute-start | bytes 589832 | tf_op jit(solution)/shard_map/ppermute | solution.py:475
  57.7 7.9 %collective-permute-start.19 = (bf16[128,768]{1,0:T(8,128)(2,1)S(1)}, bf16[128,768]{1,0:T(8,128)(2,1)S(1)}, u32[]{:S(2)}, u32[]{:S(2)}) collective-permute-start(bf16[128,768]{1,0:T(8,128)(2,1)S(1)} %get-tuple-element.100), channel_id=1, source_target_pairs={{0,4},{1,5},{4,6},{5,7},{6,2},{7,3},{2,0},{3,1},{8,12},{9,13},{12,... | collective-permute-start | bytes 589832 | tf_op jit(solution)/shard_map/ppermute | solution.py:468
  58.7 12.7 %collective-permute-start.20 = (bf16[128,768]{1,0:T(8,128)(2,1)S(1)}, bf16[128,768]{1,0:T(8,128)(2,1)S(1)}, u32[]{:S(2)}, u32[]{:S(2)}) collective-permute-start(bf16[128,768]{1,0:T(8,128)(2,1)S(1)} %get-tuple-element.105), channel_id=1, source_target_pairs={{0,2},{1,3},{4,0},{5,1},{6,4},{7,5},{2,6},{3,7},{8,10},{9,11},{12,... | collective-permute-start | bytes 589832 | tf_op jit(solution)/shard_map/ppermute | solution.py:468
  66.0 6.0 %collective-permute-start.21 = (bf16[128,768]{1,0:T(8,128)(2,1)S(1)}, bf16[128,768]{1,0:T(8,128)(2,1)S(1)}, u32[]{:S(2)}, u32[]{:S(2)}) collective-permute-start(bf16[128,768]{1,0:T(8,128)(2,1)S(1)} %get-tuple-element.106), channel_id=1, source_target_pairs={{0,4},{1,5},{4,6},{5,7},{6,2},{7,3},{2,0},{3,1},{8,12},{9,13},{12,... | collective-permute-start | bytes 589832 | tf_op jit(solution)/shard_map/ppermute | solution.py:468

commit v5 on v4

--- a/solution.py
+++ b/solution.py
@@ -56,6 +56,10 @@
     )(*operands, *after)
 
 
+def codes(experts):
+    return [0, *sorted(range(1, experts), key=lambda code: (-bin(code).count("1"), code))]
+
+
 def route(raw, ids, probs, experts, capacity):
     tokens = ids.shape[1]
     lines = max(8, experts)
@@ -73,7 +77,10 @@
         here = lax.broadcasted_iota(jnp.int32, (tokens, tokens), 1)
         earlier = (before < here).astype(F32).astype(BF16)
         slot = lax.broadcasted_iota(jnp.int32, (capacity, tokens), 0).astype(F32)
-        expert = lax.broadcasted_iota(jnp.int32, (lines, tokens), 0) ^ lax.axis_index("expert")
+        line = lax.broadcasted_iota(jnp.int32, (lines, tokens), 0)
+        expert = jnp.full((lines, tokens), experts, jnp.int32)
+        for r, code in enumerate(codes(experts)):
+            expert = jnp.where(line == r, lax.axis_index("expert") ^ code, expert)
         for copy in copies:
             copy.wait()
         first = (ids_ref[0:1, :] == expert).astype(F32)
@@ -157,7 +164,7 @@
             span = pl.ds(r * capacity, capacity)
             for i, (source, target) in enumerate(((gate_hbm, gate_ref), (up_hbm, up_ref))):
                 copies.append(
-                    pltpu.make_async_copy(source.at[0, me ^ r], target.at[span, :], sems.at[i, r])
+                    pltpu.make_async_copy(source.at[0, me ^ codes(groups)[r]], target.at[span, :], sems.at[i, r])
                 )
         for copy in copies:
             copy.start()
@@ -346,6 +353,8 @@
     experts = len(pieces)
     blocks, _, columns = pieces[0].shape
     tokens = sel.shape[1]
+    taken = sorted(range(experts), key=lambda r: codes(experts)[r])
+    place = [taken.index(r) for r in range(experts)]
     flat = [x for group in others for x in group]
 
     def kernel(*refs):
@@ -353,7 +362,7 @@
         other_refs = list(refs[experts + 1 : experts + 1 + len(flat)])
         out_refs = refs[experts + 1 + len(flat) :]
         for b in range(blocks):
-            rows = jnp.concatenate([piece[b] for piece in piece_refs], axis=0)
+            rows = jnp.concatenate([piece_refs[i][b] for i in place], axis=0)
             value = dot(sel_ref[...], rows, TN)
             for _ in others[b]:
                 value = value + other_refs.pop(0)[...].astype(F32)
@@ -362,7 +371,7 @@
     return call(
         kernel,
         "combine",
-        [*pieces, sel, *flat],
+        [*(pieces[r] for r in taken), sel, *flat],
         [shaped((tokens, columns), dtype) for dtype in dtypes],
         after,
         flops=2 * blocks * sel.shape[0] * tokens * columns,
@@ -471,11 +480,10 @@
         return lax.ppermute(x, "cuts", [(i, i ^ 1) for i in range(cuts)])
 
     def exchange(pieces):
-        moved = {
-            r: lax.ppermute(pieces[r], "expert", [(i, i ^ r) for i in range(experts)])
-            for r in range(experts - 1, 0, -1)
-        }
-        return [pieces[0]] + [moved[r] for r in range(1, experts)]
+        return [
+            lax.ppermute(piece, "expert", [(i, i ^ code) for i in range(experts)]) if code else piece
+            for piece, code in zip(pieces, codes(experts))
+        ]
 
     raw1 = along(out_grad, 1)
     raw2 = along(raw1, 1)

time: 72.9 us -> 73.1 us (level)
  starting transfers between devices: 26.3 us -> 27.5 us
  waiting for transfers between devices: 19.5 us -> 18.5 us
    ppermute x12, starting transfers between devices: 14 us -> 15.2 us  [exchange(): lax.ppermute(piece, 'expert', [(i, i ^ code) for i in range(experts)])]
    ppermute x12, waiting for transfers between devices: 12.6 us -> 11.5 us  [exchange(): lax.ppermute(piece, 'expert', [(i, i ^ code) for i in range(experts)])]
  transfers between devices with their start and end apart: 22 -> 22, of which waited for: 9 -> 10; matrix products, arithmetic and copies ran while one was open for 0% -> 0% of each run, Pallas kernels for 26% -> 26%
where the time goes in v5:
time: 73.1 us; the launch traced here: 72.9 us
  starting transfers between devices  27.5 us (38%)
  Pallas kernels  24 us (33%)
  waiting for transfers between devices  18.5 us (25%)
  local copies, waits for them, and re-layouts  1.29 us (2%)
  between operations  0.95 us (1%)
  other arithmetic  0.74 us (1%)
    pallas_call x18, Pallas kernels, call(): pl.pallas_call(body, out_shape=out_shape, in_specs=list(specs) + [VMEM] *...  24 us
    ppermute x12, starting transfers between devices, exchange(): lax.ppermute(piece, 'expert', [(i, i ^ code) for i in range(experts)])  15.2 us
    ppermute x12, waiting for transfers between devices, exchange(): lax.ppermute(piece, 'expert', [(i, i ^ code) for i in range(experts)])  11.5 us
    ppermute x6, starting transfers between devices, along(): return lax.ppermute(x, 'cuts', pairs)  11.2 us
    ppermute x6, waiting for transfers between devices, along(): return lax.ppermute(x, 'cuts', pairs)  7 us
  transfers between devices with their start and end apart: 22, of which 10 were waited for; matrix products, arithmetic and copies ran while one was open for 0% of the time, Pallas kernels for 26%

profile of v5, /device:TPU:0, one launch (start us, length us, event | category | flops | bytes accessed | tf_op | source)
XLA Modules:
  0.0 72.9 jit_solution(5372639207344377789)
XLA Ops:
  0.6 4.1 %collective-permute-start.1 = (bf16[128,768]{1,0:T(8,128)(2,1)}, bf16[128,768]{1,0:T(8,128)(2,1)S(1)}, u32[]{:S(2)}, u32[]{:S(2)}) collective-permute-start(bf16[128,768]{1,0:T(8,128)(2,1)} %refs_0_.2), channel_id=1, source_target_pairs={{0,4},{1,5},{4,6},{5,7},{6,2},{7,3},{2,0},{3,1},{8,12},{9,13},{12,... | collective-permute-start | bytes 589832 | tf_op jit(solution)/shard_map/ppermute | solution.py:477
  4.7 1.3 %route.1 = (bf16[256,128]{1,0:T(8,128)(2,1)S(1)}, f32[256,1]{1,0:T(8,128)S(1)}, bf16[128,768]{1,0:T(8,128)(2,1)S(1)}, f32[8,128]{1,0:T(8,128)S(1)}) custom-call(bf16[128,768]{1,0:T(8,128)(2,1)} %refs_0_.2, s32[2,128]{1,0:T(2,128)} %bitcast.8, f32[2,128]{1,0:T(2,128)} %bitcast.9), custom_call_target="tpu_custom_call" | custom-call | flops 1000 | bytes 1000 | tf_op jit(solution)/shard_map/route/pallas_call | solution.py:45
  6.0 4.4 %collective-permute-done.1.refs_1_ = bf16[128,768]{1,0:T(8,128)(2,1)S(1)} collective-permute-done((bf16[128,768]{1,0:T(8,128)(2,1)}, bf16[128,768]{1,0:T(8,128)(2,1)S(1)}, u32[]{:S(2)}, u32[]{:S(2)}) %collective-permute-start.1) | collective-permute-done | bytes 196640 | tf_op jit(solution)/shard_map/ppermute | solution.py:477
  10.4 3.3 %collective-permute-start.2 = (bf16[128,768]{1,0:T(8,128)(2,1)S(1)}, bf16[128,768]{1,0:T(8,128)(2,1)S(1)}, u32[]{:S(2)}, u32[]{:S(2)}) collective-permute-start(bf16[128,768]{1,0:T(8,128)(2,1)S(1)} %collective-permute-done.1.refs_1_), channel_id=1, source_target_pairs={{0,4},{1,5},{4,6},{5,7},{6,2},{7,3},{2,0},{3,1},{8,12},{9,13},{12,... | collective-permute-start | bytes 589832 | tf_op jit(solution)/shard_map/ppermute | solution.py:477
  13.7 0.4 pack.2
  14.0 2.5 %collective-permute-start.6 = (bf16[2,64,768]{2,1,0:T(8,128)(2,1)S(1)}, bf16[2,64,768]{2,1,0:T(8,128)(2,1)S(1)}, u32[]{:S(2)}, u32[]{:S(2)}) collective-permute-start(bf16[2,64,768]{2,1,0:T(8,128)(2,1)S(1)} %get-tuple-element.66), channel_id=1, source_target_pairs={{0,24},{8,16},{16,8},{24,0},{1,25},{9,17},{17,9},{25,1},{2,26},{10... | collective-permute-start | bytes 589832 | tf_op jit(solution)/shard_map/ppermute | solution.py:484
  16.5 0.5 collective-permute-start.7
  17.1 0.5 collective-permute-start.8
  17.6 1.4 %collective-permute-done.2.refs_1_ = bf16[128,768]{1,0:T(8,128)(2,1)S(1)} collective-permute-done((bf16[128,768]{1,0:T(8,128)(2,1)S(1)}, bf16[128,768]{1,0:T(8,128)(2,1)S(1)}, u32[]{:S(2)}, u32[]{:S(2)}) %collective-permute-start.2) | collective-permute-done | bytes 196640 | tf_op jit(solution)/shard_map/ppermute | solution.py:477
  18.9 0.4 pack.3
  19.3 2.5 %collective-permute-start.3 = (bf16[2,64,768]{2,1,0:T(8,128)(2,1)S(1)}, bf16[2,64,768]{2,1,0:T(8,128)(2,1)S(1)}, u32[]{:S(2)}, u32[]{:S(2)}) collective-permute-start(bf16[2,64,768]{2,1,0:T(8,128)(2,1)S(1)} %get-tuple-element.62), channel_id=1, source_target_pairs={{0,24},{8,16},{16,8},{24,0},{1,25},{9,17},{17,9},{25,1},{2,26},{10... | collective-permute-start | bytes 589832 | tf_op jit(solution)/shard_map/ppermute | solution.py:484
  21.8 0.5 collective-permute-start.4
  22.4 0.7 collective-permute-start.5
  23.1 2.4 %activations.1 = (f32[1024,256]{1,0:T(8,128)S(1)}, f32[1024,256]{1,0:T(8,128)S(1)}, bf16[1024,256]{1,0:T(8,128)(2,1)S(1)}, f32[8,128]{1,0:T(8,128)S(1)}) custom-call(bf16[1,4,64,1024]{3,2,1,0:T(8,128)(2,1)} %refs_0_.3, bf16[1,4,64,1024]{3,2,1,0:T(8,128)(2,1)} %refs_1_.2, f32[8,128]{1,0:T(8,128)S(1)} %get-tuple-element.69.refs_2_), custom_call_target="tpu_custom_call" | custom-call | flops 12000000000 | bytes 1000 | tf_op jit(solution)/shard_map/activations/pallas_call | solution.py:45
  25.5 1.7 %collective-permute-done.8.refs_3_ = bf16[2,64,768]{2,1,0:T(8,128)(2,1)S(1)} collective-permute-done((bf16[2,64,768]{2,1,0:T(8,128)(2,1)S(1)}, bf16[2,64,768]{2,1,0:T(8,128)(2,1)S(1)}, u32[]{:S(2)}, u32[]{:S(2)}) %collective-permute-start.8) | collective-permute-done | bytes 196640 | tf_op jit(solution)/shard_map/ppermute | solution.py:484
  27.3 0.1 collective-permute-start.10
  27.3 1.5 %collective-permute-done.3.refs_1_ = bf16[2,64,768]{2,1,0:T(8,128)(2,1)S(1)} collective-permute-done((bf16[2,64,768]{2,1,0:T(8,128)(2,1)S(1)}, bf16[2,64,768]{2,1,0:T(8,128)(2,1)S(1)}, u32[]{:S(2)}, u32[]{:S(2)}) %collective-permute-start.3) | collective-permute-done | bytes 196640 | tf_op jit(solution)/shard_map/ppermute | solution.py:484
  28.9 3.2 %collective-permute-done.4.refs_2_ = bf16[2,64,768]{2,1,0:T(8,128)(2,1)S(1)} collective-permute-done((bf16[2,64,768]{2,1,0:T(8,128)(2,1)S(1)}, bf16[2,64,768]{2,1,0:T(8,128)(2,1)S(1)}, u32[]{:S(2)}, u32[]{:S(2)}) %collective-permute-start.4) | collective-permute-done | bytes 196640 | tf_op jit(solution)/shard_map/ppermute | solution.py:484
  32.3 2.6 %hidden_part.2 = (f32[1024,256]{1,0:T(8,128)S(1)}, f32[8,128]{1,0:T(8,128)S(1)}) custom-call(bf16[2,256,768]{2,1,0:T(8,128)(2,1)S(1)} %get-tuple-element.73.refs_0_.refs_1_, bf16[2,256,768]{2,1,0:T(8,128)(2,1)S(1)} %collective-permute-done.10.refs_1_.refs_2_, bf16[2,256,768]{2,1,0:T(8,128)(2,1)S(1)} %get-tuple-element.72.refs_2_.refs_1_, ...), custom_call_target="tpu_custom_call" | custom-call | flops 1000 | bytes 1000 | tf_op jit(solution)/shard_map/hidden_part/pallas_call | solution.py:45
  35.0 1.1 %hidden_part.3 = (bf16[1024,256]{1,0:T(8,128)(2,1)S(1)}, bf16[1024,256]{1,0:T(8,128)(2,1)S(1)}, f32[8,128]{1,0:T(8,128)S(1)}) custom-call(bf16[2,256,768]{2,1,0:T(8,128)(2,1)S(1)} %collective-permute-done.9.refs_0_.refs_2_, bf16[1,1024,6144]{2,1,0:T(8,128)(2,1)S(1)} %bitcast.7, f32[1024,256]{1,0:T(8,128)S(1)} %get-tuple-element.75.refs_2_, ...), custom_call_target="tpu_custom_call" | custom-call | flops 1000 | bytes 1000 | tf_op jit(solution)/shard_map/hidden_part/pallas_call | solution.py:45
  36.2 1.3 %slice-done.5 = s8[4194304]{0:T(1024)(128)(4,1)S(1)} async-done(((s8[12582912]{0:T(1024)(128)(4,1)}), s8[4194304]{0:T(1024)(128)(4,1)S(1)}, s32[]{:S(2)}) %slice-start.5) | async-done | bytes 4194328
  37.4 1.9 %slot_part.4 = (bf16[2,256,768]{2,1,0:T(8,128)(2,1)S(1)}, f32[8,128]{1,0:T(8,128)S(1)}) custom-call(bf16[1024,256]{1,0:T(8,128)(2,1)S(1)} %get-tuple-element.79.refs_0_, bf16[1024,256]{1,0:T(8,128)(2,1)S(1)} %get-tuple-element.80.refs_1_, bf16[1,6144,1024]{2,1,0:T(8,128)(2,1)S(1)} %bitcast.3, bf16[1,6144,1024]{2,1,0:T(8,128)(2,1)S(1)} %bitcast.5, ...), custom_call_target="tpu_custom_call" | custom-call | flops 1610612736 | bytes 7340032 | tf_op jit(solution)/shard_map/slot_part/pallas_call | solution.py:45
  39.3 0.5 collective-permute-start.11
  39.9 1.9 %slot_part.5 = (f32[2,256,768]{2,1,0:T(8,128)S(1)}, f32[8,128]{1,0:T(8,128)S(1)}) custom-call(bf16[1024,256]{1,0:T(8,128)(2,1)S(1)} %get-tuple-element.79.refs_0_, bf16[1024,256]{1,0:T(8,128)(2,1)S(1)} %get-tuple-element.80.refs_1_, bf16[1,6144,1024]{2,1,0:T(8,128)(2,1)S(1)} %bitcast.3, bf16[1,6144,1024]{2,1,0:T(8,128)(2,1)S(1)} %bitcast.5, ...), custom_call_target="tpu_custom_call" | custom-call | flops 1610612736 | bytes 7340032 | tf_op jit(solution)/shard_map/slot_part/pallas_call | solution.py:45
  41.8 0.2 add_halves.2
  42.0 1.9 %slot_part.6 = (bf16[2,256,768]{2,1,0:T(8,128)(2,1)S(1)}, f32[8,128]{1,0:T(8,128)S(1)}) custom-call(bf16[1024,256]{1,0:T(8,128)(2,1)S(1)} %get-tuple-element.79.refs_0_, bf16[1024,256]{1,0:T(8,128)(2,1)S(1)} %get-tuple-element.80.refs_1_, bf16[1,6144,1024]{2,1,0:T(8,128)(2,1)S(1)} %bitcast.3, bf16[1,6144,1024]{2,1,0:T(8,128)(2,1)S(1)} %bitcast.5, ...), custom_call_target="tpu_custom_call" | custom-call | flops 1610612736 | bytes 7340032 | tf_op jit(solution)/shard_map/slot_part/pallas_call | solution.py:45
  43.9 0.4 collective-permute-start.12
  44.3 1.5 %collective-permute-start.16 = (bf16[2,64,768]{2,1,0:T(8,128)(2,1)S(1)}, bf16[2,64,768]{2,1,0:T(8,128)(2,1)S(1)}, u32[]{:S(2)}, u32[]{:S(2)}) collective-permute-start(bf16[2,64,768]{2,1,0:T(8,128)(2,1)S(1)} %get-tuple-element.96), channel_id=1, source_target_pairs={{0,8},{8,0},{16,24},{24,16},{1,9},{9,1},{17,25},{25,17},{2,10},{10... | collective-permute-start | bytes 589832 | tf_op jit(solution)/shard_map/ppermute | solution.py:484
  45.8 1.4 %collective-permute-start.17 = (bf16[2,64,768]{2,1,0:T(8,128)(2,1)S(1)}, bf16[2,64,768]{2,1,0:T(8,128)(2,1)S(1)}, u32[]{:S(2)}, u32[]{:S(2)}) collective-permute-start(bf16[2,64,768]{2,1,0:T(8,128)(2,1)S(1)} %get-tuple-element.97), channel_id=1, source_target_pairs={{0,16},{8,24},{16,0},{24,8},{1,17},{9,25},{17,1},{25,9},{2,18},{10... | collective-permute-start | bytes 589832 | tf_op jit(solution)/shard_map/ppermute | solution.py:484
  47.2 0.6 collective-permute-start.18
  47.8 2.0 %slot_part.7 = (f32[2,256,768]{2,1,0:T(8,128)S(1)}, f32[8,128]{1,0:T(8,128)S(1)}) custom-call(bf16[1024,256]{1,0:T(8,128)(2,1)S(1)} %get-tuple-element.79.refs_0_, bf16[1024,256]{1,0:T(8,128)(2,1)S(1)} %get-tuple-element.80.refs_1_, bf16[1,6144,1024]{2,1,0:T(8,128)(2,1)S(1)} %bitcast.3, bf16[1,6144,1024]{2,1,0:T(8,128)(2,1)S(1)} %bitcast.5, ...), custom_call_target="tpu_custom_call" | custom-call | flops 1610612736 | bytes 7340032 | tf_op jit(solution)/shard_map/slot_part/pallas_call | solution.py:45
  49.8 0.2 add_halves.3
  49.9 1.6 %collective-permute-start.13 = (bf16[2,64,768]{2,1,0:T(8,128)(2,1)S(1)}, bf16[2,64,768]{2,1,0:T(8,128)(2,1)S(1)}, u32[]{:S(2)}, u32[]{:S(2)}) collective-permute-start(bf16[2,64,768]{2,1,0:T(8,128)(2,1)S(1)} %get-tuple-element.92), channel_id=1, source_target_pairs={{0,8},{8,0},{16,24},{24,16},{1,9},{9,1},{17,25},{25,17},{2,10},{10... | collective-permute-start | bytes 589832 | tf_op jit(solution)/shard_map/ppermute | solution.py:484
  51.5 1.4 %collective-permute-start.14 = (bf16[2,64,768]{2,1,0:T(8,128)(2,1)S(1)}, bf16[2,64,768]{2,1,0:T(8,128)(2,1)S(1)}, u32[]{:S(2)}, u32[]{:S(2)}) collective-permute-start(bf16[2,64,768]{2,1,0:T(8,128)(2,1)S(1)} %get-tuple-element.93), channel_id=1, source_target_pairs={{0,16},{8,24},{16,0},{24,8},{1,17},{9,25},{17,1},{25,9},{2,18},{10... | collective-permute-start | bytes 589832 | tf_op jit(solution)/shard_map/ppermute | solution.py:484
  52.9 1.5 %collective-permute-start.15 = (bf16[2,64,768]{2,1,0:T(8,128)(2,1)S(1)}, bf16[2,64,768]{2,1,0:T(8,128)(2,1)S(1)}, u32[]{:S(2)}, u32[]{:S(2)}) collective-permute-start(bf16[2,64,768]{2,1,0:T(8,128)(2,1)S(1)} %get-tuple-element.94), channel_id=1, source_target_pairs={{0,24},{8,16},{16,8},{24,0},{1,25},{9,17},{17,9},{25,1},{2,26},{10... | collective-permute-start | bytes 589832 | tf_op jit(solution)/shard_map/ppermute | solution.py:484
  54.3 2.5 %collective-permute-done.17.refs_2_ = bf16[2,64,768]{2,1,0:T(8,128)(2,1)S(1)} collective-permute-done((bf16[2,64,768]{2,1,0:T(8,128)(2,1)S(1)}, bf16[2,64,768]{2,1,0:T(8,128)(2,1)S(1)}, u32[]{:S(2)}, u32[]{:S(2)}) %collective-permute-start.17) | collective-permute-done | bytes 196640 | tf_op jit(solution)/shard_map/ppermute | solution.py:484
  56.9 0.3 collective-permute-done.18.refs_3_
  57.1 0.3 combine.2
  57.4 1.0 %collective-permute-start.19 = (bf16[128,768]{1,0:T(8,128)(2,1)S(1)}, bf16[128,768]{1,0:T(8,128)(2,1)S(1)}, u32[]{:S(2)}, u32[]{:S(2)}) collective-permute-start(bf16[128,768]{1,0:T(8,128)(2,1)S(1)} %get-tuple-element.100), channel_id=1, source_target_pairs={{0,4},{1,5},{4,6},{5,7},{6,2},{7,3},{2,0},{3,1},{8,12},{9,13},{12,... | collective-permute-start | bytes 589832 | tf_op jit(solution)/shard_map/ppermute | solution.py:477
  58.4 1.3 %collective-permute-start.20 = (bf16[128,768]{1,0:T(8,128)(2,1)S(1)}, bf16[128,768]{1,0:T(8,128)(2,1)S(1)}, u32[]{:S(2)}, u32[]{:S(2)}) collective-permute-start(bf16[128,768]{1,0:T(8,128)(2,1)S(1)} %get-tuple-element.105), channel_id=1, source_target_pairs={{0,2},{1,3},{4,0},{5,1},{6,4},{7,5},{2,6},{3,7},{8,10},{9,11},{12,... | collective-permute-start | bytes 589832 | tf_op jit(solution)/shard_map/ppermute | solution.py:477
  59.7 3.3 %down_part.2 = (bf16[1,1024,6144]{2,1,0:T(8,128)(2,1)}, f32[8,128]{1,0:T(8,128)S(1)}) custom-call(bf16[1024,256]{1,0:T(8,128)(2,1)S(1)} %get-tuple-element.101.refs_0_, bf16[2,256,768]{2,1,0:T(8,128)(2,1)S(1)} %get-tuple-element.73.refs_0_.refs_1_, bf16[2,256,768]{2,1,0:T(8,128)(2,1)S(1)} %collective-permute-done.10.refs_1_.refs_2_, ...), custom_call_target="tpu_custom_call" | custom-call | flops 1610612736 | bytes 6291456 | tf_op jit(solution)/shard_map/down_part/pallas_call | solution.py:45
  63.0 2.2 %collective-permute-done.14.refs_2_ = bf16[2,64,768]{2,1,0:T(8,128)(2,1)S(1)} collective-permute-done((bf16[2,64,768]{2,1,0:T(8,128)(2,1)S(1)}, bf16[2,64,768]{2,1,0:T(8,128)(2,1)S(1)}, u32[]{:S(2)}, u32[]{:S(2)}) %collective-permute-start.14) | collective-permute-done | bytes 196640 | tf_op jit(solution)/shard_map/ppermute | solution.py:484
  65.2 0.2 collective-permute-done.19.refs_5_
  65.3 0.3 combine.3
  65.6 1.6 %collective-permute-start.21 = (bf16[128,768]{1,0:T(8,128)(2,1)S(1)}, bf16[128,768]{1,0:T(8,128)(2,1)S(1)}, u32[]{:S(2)}, u32[]{:S(2)}) collective-permute-start(bf16[128,768]{1,0:T(8,128)(2,1)S(1)} %get-tuple-element.106), channel_id=1, source_target_pairs={{0,4},{1,5},{4,6},{5,7},{6,2},{7,3},{2,0},{3,1},{8,12},{9,13},{12,... | collective-permute-start | bytes 589832 | tf_op jit(solution)/shard_map/ppermute | solution.py:477
  67.2 3.9 %down_part.3 = (bf16[1,1024,6144]{2,1,0:T(8,128)(2,1)}, f32[8,128]{1,0:T(8,128)}) custom-call(bf16[1024,256]{1,0:T(8,128)(2,1)S(1)} %get-tuple-element.101.refs_0_, bf16[2,256,768]{2,1,0:T(8,128)(2,1)S(1)} %get-tuple-element.72.refs_2_.refs_1_, bf16[2,256,768]{2,1,0:T(8,128)(2,1)S(1)} %collective-permute-done.9.refs_0_.refs_2_, ...), custom_call_target="tpu_custom_call", output_to_operand_aliasing={{0}: (3, {})} | custom-call | tf_op jit(solution)/shard_map/down_part/pallas_call | solution.py:45
  71.1 1.1 %collective-permute-done.21 = bf16[128,768]{1,0:T(8,128)(2,1)S(1)} collective-permute-done((bf16[128,768]{1,0:T(8,128)(2,1)S(1)}, bf16[128,768]{1,0:T(8,128)(2,1)S(1)}, u32[]{:S(2)}, u32[]{:S(2)}) %collective-permute-start.21) | collective-permute-done | bytes 196640 | tf_op jit(solution)/shard_map/ppermute | solution.py:477
  72.2 0.7 %add_convert_fusion = bf16[128,768]{1,0:T(8,128)(2,1)} fusion(bf16[128,768]{1,0:T(8,128)(2,1)S(1)} %collective-permute-done.21, f32[128,768]{1,0:T(8,128)S(1)} %get-tuple-element.104, bf16[128,768]{1,0:T(8,128)(2,1)S(1)} %collective-permute-done.20), kind=kLoop, calls=%fused_computation | loop fusion | flops 491520 | bytes 983040 | tf_op jit(solution)/shard_map/convert_element_type | solution.py:528
  (36 shorter events, 0.3 us)
Async XLA Ops:
  0.6 9.8 %collective-permute-start.1 = (bf16[128,768]{1,0:T(8,128)(2,1)}, bf16[128,768]{1,0:T(8,128)(2,1)S(1)}, u32[]{:S(2)}, u32[]{:S(2)}) collective-permute-start(bf16[128,768]{1,0:T(8,128)(2,1)} %refs_0_.2), channel_id=1, source_target_pairs={{0,4},{1,5},{4,6},{5,7},{6,2},{7,3},{2,0},{3,1},{8,12},{9,13},{12,... | collective-permute-start | bytes 589832 | tf_op jit(solution)/shard_map/ppermute | solution.py:477
  4.7 12.9 %collective-permute-start = (bf16[128,768]{1,0:T(8,128)(2,1)}, bf16[128,768]{1,0:T(8,128)(2,1)S(1)}, u32[]{:S(2)}, u32[]{:S(2)}) collective-permute-start(bf16[128,768]{1,0:T(8,128)(2,1)} %refs_0_.2), channel_id=1, source_target_pairs={{0,2},{1,3},{4,0},{5,1},{6,4},{7,5},{2,6},{3,7},{8,10},{9,11},{12,... | collective-permute-start | bytes 589832 | tf_op jit(solution)/shard_map/ppermute | solution.py:477
  10.4 8.5 %collective-permute-start.2 = (bf16[128,768]{1,0:T(8,128)(2,1)S(1)}, bf16[128,768]{1,0:T(8,128)(2,1)S(1)}, u32[]{:S(2)}, u32[]{:S(2)}) collective-permute-start(bf16[128,768]{1,0:T(8,128)(2,1)S(1)} %collective-permute-done.1.refs_1_), channel_id=1, source_target_pairs={{0,4},{1,5},{4,6},{5,7},{6,2},{7,3},{2,0},{3,1},{8,12},{9,13},{12,... | collective-permute-start | bytes 589832 | tf_op jit(solution)/shard_map/ppermute | solution.py:477
  14.0 8.3 %collective-permute-start.6 = (bf16[2,64,768]{2,1,0:T(8,128)(2,1)S(1)}, bf16[2,64,768]{2,1,0:T(8,128)(2,1)S(1)}, u32[]{:S(2)}, u32[]{:S(2)}) collective-permute-start(bf16[2,64,768]{2,1,0:T(8,128)(2,1)S(1)} %get-tuple-element.66), channel_id=1, source_target_pairs={{0,24},{8,16},{16,8},{24,0},{1,25},{9,17},{17,9},{25,1},{2,26},{10... | collective-permute-start | bytes 589832 | tf_op jit(solution)/shard_map/ppermute | solution.py:484
  16.5 8.9 %collective-permute-start.7 = (bf16[2,64,768]{2,1,0:T(8,128)(2,1)S(1)}, bf16[2,64,768]{2,1,0:T(8,128)(2,1)S(1)}, u32[]{:S(2)}, u32[]{:S(2)}) collective-permute-start(bf16[2,64,768]{2,1,0:T(8,128)(2,1)S(1)} %get-tuple-element.67), channel_id=1, source_target_pairs={{0,8},{8,0},{16,24},{24,16},{1,9},{9,1},{17,25},{25,17},{2,10},{10... | collective-permute-start | bytes 589832 | tf_op jit(solution)/shard_map/ppermute | solution.py:484
  17.1 10.1 %collective-permute-start.8 = (bf16[2,64,768]{2,1,0:T(8,128)(2,1)S(1)}, bf16[2,64,768]{2,1,0:T(8,128)(2,1)S(1)}, u32[]{:S(2)}, u32[]{:S(2)}) collective-permute-start(bf16[2,64,768]{2,1,0:T(8,128)(2,1)S(1)} %get-tuple-element.68), channel_id=1, source_target_pairs={{0,16},{8,24},{16,0},{24,8},{1,17},{9,25},{17,1},{25,9},{2,18},{10... | collective-permute-start | bytes 589832 | tf_op jit(solution)/shard_map/ppermute | solution.py:484
  18.9 13.3 %slice-start.6 = ((s8[12582912]{0:T(1024)(128)(4,1)}), s8[4194304]{0:T(1024)(128)(4,1)S(1)}, s32[]{:S(2)}) async-start(s8[12582912]{0:T(1024)(128)(4,1)} %bitcast.6), calls=%async_computation.6 | async-start | bytes 8388608
  19.3 9.6 %collective-permute-start.3 = (bf16[2,64,768]{2,1,0:T(8,128)(2,1)S(1)}, bf16[2,64,768]{2,1,0:T(8,128)(2,1)S(1)}, u32[]{:S(2)}, u32[]{:S(2)}) collective-permute-start(bf16[2,64,768]{2,1,0:T(8,128)(2,1)S(1)} %get-tuple-element.62), channel_id=1, source_target_pairs={{0,24},{8,16},{16,8},{24,0},{1,25},{9,17},{17,9},{25,1},{2,26},{10... | collective-permute-start | bytes 589832 | tf_op jit(solution)/shard_map/ppermute | solution.py:484
  21.8 10.3 %collective-permute-start.4 = (bf16[2,64,768]{2,1,0:T(8,128)(2,1)S(1)}, bf16[2,64,768]{2,1,0:T(8,128)(2,1)S(1)}, u32[]{:S(2)}, u32[]{:S(2)}) collective-permute-start(bf16[2,64,768]{2,1,0:T(8,128)(2,1)S(1)} %get-tuple-element.63), channel_id=1, source_target_pairs={{0,8},{8,0},{16,24},{24,16},{1,9},{9,1},{17,25},{25,17},{2,10},{10... | collective-permute-start | bytes 589832 | tf_op jit(solution)/shard_map/ppermute | solution.py:484
  22.4 9.8 %collective-permute-start.5 = (bf16[2,64,768]{2,1,0:T(8,128)(2,1)S(1)}, bf16[2,64,768]{2,1,0:T(8,128)(2,1)S(1)}, u32[]{:S(2)}, u32[]{:S(2)}) collective-permute-start(bf16[2,64,768]{2,1,0:T(8,128)(2,1)S(1)} %get-tuple-element.64), channel_id=1, source_target_pairs={{0,16},{8,24},{16,0},{24,8},{1,17},{9,25},{17,1},{25,9},{2,18},{10... | collective-permute-start | bytes 589832 | tf_op jit(solution)/shard_map/ppermute | solution.py:484
  23.1 11.9 %slice-start = ((s8[12582912]{0:T(1024)(128)(4,1)}), s8[4194304]{0:T(1024)(128)(4,1)S(1)}, s32[]{:S(2)}) async-start(s8[12582912]{0:T(1024)(128)(4,1)} %bitcast.2), calls=%async_computation | async-start | bytes 8388608
  23.1 9.2 %slice-start.7 = ((s8[12582912]{0:T(1024)(128)(4,1)}), s8[4194304]{0:T(1024)(128)(4,1)S(1)}, s32[]{:S(2)}) async-start(s8[12582912]{0:T(1024)(128)(4,1)} %bitcast.6), calls=%async_computation.7 | async-start | bytes 8388608
  23.1 9.2 %slice-start.8 = ((s8[12582912]{0:T(1024)(128)(4,1)}), s8[4194304]{0:T(1024)(128)(4,1)S(1)}, s32[]{:S(2)}) async-start(s8[12582912]{0:T(1024)(128)(4,1)} %bitcast.6), calls=%async_computation.8 | async-start | bytes 8388608
  23.1 11.9 %slice-start.1 = ((s8[12582912]{0:T(1024)(128)(4,1)}), s8[4194304]{0:T(1024)(128)(4,1)S(1)}, s32[]{:S(2)}) async-start(s8[12582912]{0:T(1024)(128)(4,1)} %bitcast.2), calls=%async_computation.1 | async-start | bytes 8388608
  23.1 11.9 %slice-start.2 = ((s8[12582912]{0:T(1024)(128)(4,1)}), s8[4194304]{0:T(1024)(128)(4,1)S(1)}, s32[]{:S(2)}) async-start(s8[12582912]{0:T(1024)(128)(4,1)} %bitcast.2), calls=%async_computation.2 | async-start | bytes 8388608
  27.3 5.0 %collective-permute-start.10 = (bf16[2,256,768]{2,1,0:T(8,128)(2,1)S(1)}, bf16[2,256,768]{2,1,0:T(8,128)(2,1)S(1)}, u32[]{:S(2)}, u32[]{:S(2)}) collective-permute-start(bf16[2,256,768]{2,1,0:T(8,128)(2,1)S(1)} %get-tuple-element.73.refs_0_.refs_1_), channel_id=1, source_target_pairs={{0,1},{1,0},{2,3},{3,2},{4,5},{5,4},{6,7},{7,6},{8,9},{9,8},{10,11... | collective-permute-start | bytes 2359304 | tf_op jit(solution)/shard_map/ppermute | solution.py:480
  32.2 2.8 %collective-permute-start.9 = (bf16[2,256,768]{2,1,0:T(8,128)(2,1)S(1)}, bf16[2,256,768]{2,1,0:T(8,128)(2,1)S(1)}, u32[]{:S(2)}, u32[]{:S(2)}) collective-permute-start(bf16[2,256,768]{2,1,0:T(8,128)(2,1)S(1)} %get-tuple-element.72.refs_2_.refs_1_), channel_id=1, source_target_pairs={{0,1},{1,0},{2,3},{3,2},{4,5},{5,4},{6,7},{7,6},{8,9},{9,8},{10,11... | collective-permute-start | bytes 2359304 | tf_op jit(solution)/shard_map/ppermute | solution.py:480
  32.3 3.8 %slice-start.3 = ((s8[12582912]{0:T(1024)(128)(4,1)}), s8[4194304]{0:T(1024)(128)(4,1)S(1)}, s32[]{:S(2)}) async-start(s8[12582912]{0:T(1024)(128)(4,1)} %bitcast.4), calls=%async_computation.3 | async-start | bytes 8388608
  32.3 3.8 %slice-start.4 = ((s8[12582912]{0:T(1024)(128)(4,1)}), s8[4194304]{0:T(1024)(128)(4,1)S(1)}, s32[]{:S(2)}) async-start(s8[12582912]{0:T(1024)(128)(4,1)} %bitcast.4), calls=%async_computation.4 | async-start | bytes 8388608
  35.0 2.4 %slice-start.5 = ((s8[12582912]{0:T(1024)(128)(4,1)}), s8[4194304]{0:T(1024)(128)(4,1)S(1)}, s32[]{:S(2)}) async-start(s8[12582912]{0:T(1024)(128)(4,1)} %bitcast.4), calls=%async_computation.5 | async-start | bytes 8388608
  39.3 2.5 %collective-permute-start.11 = (bf16[2,256,768]{2,1,0:T(8,128)(2,1)S(1)}, bf16[2,256,768]{2,1,0:T(8,128)(2,1)S(1)}, u32[]{:S(2)}, u32[]{:S(2)}) collective-permute-start(bf16[2,256,768]{2,1,0:T(8,128)(2,1)S(1)} %get-tuple-element.84), channel_id=1, source_target_pairs={{0,1},{1,0},{2,3},{3,2},{4,5},{5,4},{6,7},{7,6},{8,9},{9,8},{10,11... | collective-permute-start | bytes 2359304 | tf_op jit(solution)/shard_map/ppermute | solution.py:480
  43.9 5.8 %collective-permute-start.12 = (bf16[2,256,768]{2,1,0:T(8,128)(2,1)S(1)}, bf16[2,256,768]{2,1,0:T(8,128)(2,1)S(1)}, u32[]{:S(2)}, u32[]{:S(2)}) collective-permute-start(bf16[2,256,768]{2,1,0:T(8,128)(2,1)S(1)} %get-tuple-element.89), channel_id=1, source_target_pairs={{0,1},{1,0},{2,3},{3,2},{4,5},{5,4},{6,7},{7,6},{8,9},{9,8},{10,11... | collective-permute-start | bytes 2359304 | tf_op jit(solution)/shard_map/ppermute | solution.py:480
  44.3 8.5 %collective-permute-start.16 = (bf16[2,64,768]{2,1,0:T(8,128)(2,1)S(1)}, bf16[2,64,768]{2,1,0:T(8,128)(2,1)S(1)}, u32[]{:S(2)}, u32[]{:S(2)}) collective-permute-start(bf16[2,64,768]{2,1,0:T(8,128)(2,1)S(1)} %get-tuple-element.96), channel_id=1, source_target_pairs={{0,8},{8,0},{16,24},{24,16},{1,9},{9,1},{17,25},{25,17},{2,10},{10... | collective-permute-start | bytes 589832 | tf_op jit(solution)/shard_map/ppermute | solution.py:484
  45.8 11.0 %collective-permute-start.17 = (bf16[2,64,768]{2,1,0:T(8,128)(2,1)S(1)}, bf16[2,64,768]{2,1,0:T(8,128)(2,1)S(1)}, u32[]{:S(2)}, u32[]{:S(2)}) collective-permute-start(bf16[2,64,768]{2,1,0:T(8,128)(2,1)S(1)} %get-tuple-element.97), channel_id=1, source_target_pairs={{0,16},{8,24},{16,0},{24,8},{1,17},{9,25},{17,1},{25,9},{2,18},{10... | collective-permute-start | bytes 589832 | tf_op jit(solution)/shard_map/ppermute | solution.py:484
  47.2 9.9 %collective-permute-start.18 = (bf16[2,64,768]{2,1,0:T(8,128)(2,1)S(1)}, bf16[2,64,768]{2,1,0:T(8,128)(2,1)S(1)}, u32[]{:S(2)}, u32[]{:S(2)}) collective-permute-start(bf16[2,64,768]{2,1,0:T(8,128)(2,1)S(1)} %get-tuple-element.98), channel_id=1, source_target_pairs={{0,24},{8,16},{16,8},{24,0},{1,25},{9,17},{17,9},{25,1},{2,26},{10... | collective-permute-start | bytes 589832 | tf_op jit(solution)/shard_map/ppermute | solution.py:484
  49.9 13.0 %collective-permute-start.13 = (bf16[2,64,768]{2,1,0:T(8,128)(2,1)S(1)}, bf16[2,64,768]{2,1,0:T(8,128)(2,1)S(1)}, u32[]{:S(2)}, u32[]{:S(2)}) collective-permute-start(bf16[2,64,768]{2,1,0:T(8,128)(2,1)S(1)} %get-tuple-element.92), channel_id=1, source_target_pairs={{0,8},{8,0},{16,24},{24,16},{1,9},{9,1},{17,25},{25,17},{2,10},{10... | collective-permute-start | bytes 589832 | tf_op jit(solution)/shard_map/ppermute | solution.py:484
  51.5 13.7 %collective-permute-start.14 = (bf16[2,64,768]{2,1,0:T(8,128)(2,1)S(1)}, bf16[2,64,768]{2,1,0:T(8,128)(2,1)S(1)}, u32[]{:S(2)}, u32[]{:S(2)}) collective-permute-start(bf16[2,64,768]{2,1,0:T(8,128)(2,1)S(1)} %get-tuple-element.93), channel_id=1, source_target_pairs={{0,16},{8,24},{16,0},{24,8},{1,17},{9,25},{17,1},{25,9},{2,18},{10... | collective-permute-start | bytes 589832 | tf_op jit(solution)/shard_map/ppermute | solution.py:484
  52.9 12.3 %collective-permute-start.15 = (bf16[2,64,768]{2,1,0:T(8,128)(2,1)S(1)}, bf16[2,64,768]{2,1,0:T(8,128)(2,1)S(1)}, u32[]{:S(2)}, u32[]{:S(2)}) collective-permute-start(bf16[2,64,768]{2,1,0:T(8,128)(2,1)S(1)} %get-tuple-element.94), channel_id=1, source_target_pairs={{0,24},{8,16},{16,8},{24,0},{1,25},{9,17},{17,9},{25,1},{2,26},{10... | collective-permute-start | bytes 589832 | tf_op jit(solution)/shard_map/ppermute | solution.py:484
  57.4 7.9 %collective-permute-start.19 = (bf16[128,768]{1,0:T(8,128)(2,1)S(1)}, bf16[128,768]{1,0:T(8,128)(2,1)S(1)}, u32[]{:S(2)}, u32[]{:S(2)}) collective-permute-start(bf16[128,768]{1,0:T(8,128)(2,1)S(1)} %get-tuple-element.100), channel_id=1, source_target_pairs={{0,4},{1,5},{4,6},{5,7},{6,2},{7,3},{2,0},{3,1},{8,12},{9,13},{12,... | collective-permute-start | bytes 589832 | tf_op jit(solution)/shard_map/ppermute | solution.py:477
  58.4 12.7 %collective-permute-start.20 = (bf16[128,768]{1,0:T(8,128)(2,1)S(1)}, bf16[128,768]{1,0:T(8,128)(2,1)S(1)}, u32[]{:S(2)}, u32[]{:S(2)}) collective-permute-start(bf16[128,768]{1,0:T(8,128)(2,1)S(1)} %get-tuple-element.105), channel_id=1, source_target_pairs={{0,2},{1,3},{4,0},{5,1},{6,4},{7,5},{2,6},{3,7},{8,10},{9,11},{12,... | collective-permute-start | bytes 589832 | tf_op jit(solution)/shard_map/ppermute | solution.py:477
  65.6 6.6 %collective-permute-start.21 = (bf16[128,768]{1,0:T(8,128)(2,1)S(1)}, bf16[128,768]{1,0:T(8,128)(2,1)S(1)}, u32[]{:S(2)}, u32[]{:S(2)}) collective-permute-start(bf16[128,768]{1,0:T(8,128)(2,1)S(1)} %get-tuple-element.106), channel_id=1, source_target_pairs={{0,4},{1,5},{4,6},{5,7},{6,2},{7,3},{2,0},{3,1},{8,12},{9,13},{12,... | collective-permute-start | bytes 589832 | tf_op jit(solution)/shard_map/ppermute | solution.py:477

commit v6 on v5

--- a/solution.py
+++ b/solution.py
@@ -57,7 +57,7 @@
 
 
 def codes(experts):
-    return [0, *sorted(range(1, experts), key=lambda code: (-bin(code).count("1"), code))]
+    return list(range(experts))
 
 
 def route(raw, ids, probs, experts, capacity):
@@ -353,8 +353,6 @@
     experts = len(pieces)
     blocks, _, columns = pieces[0].shape
     tokens = sel.shape[1]
-    taken = sorted(range(experts), key=lambda r: codes(experts)[r])
-    place = [taken.index(r) for r in range(experts)]
     flat = [x for group in others for x in group]
 
     def kernel(*refs):
@@ -362,7 +360,7 @@
         other_refs = list(refs[experts + 1 : experts + 1 + len(flat)])
         out_refs = refs[experts + 1 + len(flat) :]
         for b in range(blocks):
-            rows = jnp.concatenate([piece_refs[i][b] for i in place], axis=0)
+            rows = jnp.concatenate([piece[b] for piece in piece_refs], axis=0)
             value = dot(sel_ref[...], rows, TN)
             for _ in others[b]:
                 value = value + other_refs.pop(0)[...].astype(F32)
@@ -371,7 +369,7 @@
     return call(
         kernel,
         "combine",
-        [*(pieces[r] for r in taken), sel, *flat],
+        [*pieces, sel, *flat],
         [shaped((tokens, columns), dtype) for dtype in dtypes],
         after,
         flops=2 * blocks * sel.shape[0] * tokens * columns,
@@ -509,19 +507,22 @@
 
     first, last = [2, 3], [1, 0]
     back = functools.partial(slot_part, gate_grad, up_grad, w_gate, w_up)
-    def exchanged(shifts, t):
+    def halves(shifts, t):
         part, t = back(shifts, line, True, [t])
-        arrived = swap(part)
-        part, t = back(shifts, line, False, [t])
-        *pieces, t = add_halves(part, arrived, experts, [t])
-        return exchange(pieces), t
-
-    got1, t = exchanged(first, t)
-    got2, t = exchanged(last, t)
+        return swap(part), t
+
+    other1, t = halves(first, t)
+    part, t = back(first, line, False, [t])
+    *pieces, t = add_halves(part, other1, experts, [t])
+    got1 = exchange(pieces)
+    other2, t = halves(last, t)
+    down, t = down_part(act, mine1, theirs1, one, line, None, w_down.shape, [t])
+    part, t = back(last, line, False, [t])
+    *pieces, t = add_halves(part, other2, experts, [t])
+    got2 = exchange(pieces)
     part2, part3, t = combine(got1, sel, [[], []], [BF16, BF16], [t])
     landed2 = along(part2, 1)
     landed3 = along(part3, 3)
-    down, t = down_part(act, mine1, theirs1, one, line, None, w_down.shape, [t])
     part1, part0, t = combine(got2, sel, [[landed2], []], [BF16, F32], [t])
     landed1 = along(part1, 1)
     down, t = down_part(act, mine2, theirs2, two, line, down, w_down.shape, [t], DOWN_WEIGHT)

time: 73.1 us -> 72.8 us (level)
    ppermute x12, starting transfers between devices: 15.2 us -> 14.3 us  [exchange(): lax.ppermute(piece, 'expert', [(i, i ^ code) for i in range(experts)])]
    ppermute x12, waiting for transfers between devices: 11.5 us -> 12.3 us  [exchange(): lax.ppermute(piece, 'expert', [(i, i ^ code) for i in range(experts)])]
    ppermute x6, waiting for transfers between devices: 7 us -> 6.24 us  [along(): return lax.ppermute(x, 'cuts', pairs)]
  transfers between devices with their start and end apart: 22 -> 22, of which waited for: 10 -> 8; matrix products, arithmetic and copies ran while one was open for 0% -> 0% of each run, Pallas kernels for 26% -> 26%
where the time goes in v6:
time: 72.8 us; the launch traced here: 72.6 us
  starting transfers between devices  26.9 us (37%)
  Pallas kernels  24.1 us (33%)
  waiting for transfers between devices  18.6 us (26%)
  local copies, waits for them, and re-layouts  1.29 us (2%)
  between operations  0.95 us (1%)
  other arithmetic  0.74 us (1%)
    pallas_call x18, Pallas kernels, call(): pl.pallas_call(body, out_shape=out_shape, in_specs=list(specs) + [VMEM] *...  24.1 us
    ppermute x12, starting transfers between devices, exchange(): lax.ppermute(piece, 'expert', [(i, i ^ code) for i in range(experts)])  14.3 us
    ppermute x12, waiting for transfers between devices, exchange(): lax.ppermute(piece, 'expert', [(i, i ^ code) for i in range(experts)])  12.3 us
    ppermute x6, starting transfers between devices, along(): return lax.ppermute(x, 'cuts', pairs)  11.6 us
    ppermute x6, waiting for transfers between devices, along(): return lax.ppermute(x, 'cuts', pairs)  6.24 us
  transfers between devices with their start and end apart: 22, of which 8 were waited for; matrix products, arithmetic and copies ran while one was open for 0% of the time, Pallas kernels for 26%

profile of v6, /device:TPU:0, one launch (start us, length us, event | category | flops | bytes accessed | tf_op | source)
XLA Modules:
  0.0 72.6 jit_solution(5355993817256988466)
XLA Ops:
  0.6 4.1 %collective-permute-start.1 = (bf16[128,768]{1,0:T(8,128)(2,1)}, bf16[128,768]{1,0:T(8,128)(2,1)S(1)}, u32[]{:S(2)}, u32[]{:S(2)}) collective-permute-start(bf16[128,768]{1,0:T(8,128)(2,1)} %refs_0_.2), channel_id=1, source_target_pairs={{0,4},{1,5},{4,6},{5,7},{6,2},{7,3},{2,0},{3,1},{8,12},{9,13},{12,... | collective-permute-start | bytes 589832 | tf_op jit(solution)/shard_map/ppermute | solution.py:475
  4.7 1.3 %route.1 = (bf16[256,128]{1,0:T(8,128)(2,1)S(1)}, f32[256,1]{1,0:T(8,128)S(1)}, bf16[128,768]{1,0:T(8,128)(2,1)S(1)}, f32[8,128]{1,0:T(8,128)S(1)}) custom-call(bf16[128,768]{1,0:T(8,128)(2,1)} %refs_0_.2, s32[2,128]{1,0:T(2,128)} %bitcast.8, f32[2,128]{1,0:T(2,128)} %bitcast.9), custom_call_target="tpu_custom_call" | custom-call | flops 1000 | bytes 1000 | tf_op jit(solution)/shard_map/route/pallas_call | solution.py:45
  6.0 4.4 %collective-permute-done.1.refs_1_ = bf16[128,768]{1,0:T(8,128)(2,1)S(1)} collective-permute-done((bf16[128,768]{1,0:T(8,128)(2,1)}, bf16[128,768]{1,0:T(8,128)(2,1)S(1)}, u32[]{:S(2)}, u32[]{:S(2)}) %collective-permute-start.1) | collective-permute-done | bytes 196640 | tf_op jit(solution)/shard_map/ppermute | solution.py:475
  10.4 3.3 %collective-permute-start.2 = (bf16[128,768]{1,0:T(8,128)(2,1)S(1)}, bf16[128,768]{1,0:T(8,128)(2,1)S(1)}, u32[]{:S(2)}, u32[]{:S(2)}) collective-permute-start(bf16[128,768]{1,0:T(8,128)(2,1)S(1)} %collective-permute-done.1.refs_1_), channel_id=1, source_target_pairs={{0,4},{1,5},{4,6},{5,7},{6,2},{7,3},{2,0},{3,1},{8,12},{9,13},{12,... | collective-permute-start | bytes 589832 | tf_op jit(solution)/shard_map/ppermute | solution.py:475
  13.7 0.4 pack.2
  14.0 1.6 %collective-permute-start.6 = (bf16[2,64,768]{2,1,0:T(8,128)(2,1)S(1)}, bf16[2,64,768]{2,1,0:T(8,128)(2,1)S(1)}, u32[]{:S(2)}, u32[]{:S(2)}) collective-permute-start(bf16[2,64,768]{2,1,0:T(8,128)(2,1)S(1)} %get-tuple-element.66), channel_id=1, source_target_pairs={{0,8},{8,0},{16,24},{24,16},{1,9},{9,1},{17,25},{25,17},{2,10},{10... | collective-permute-start | bytes 589832 | tf_op jit(solution)/shard_map/ppermute | solution.py:482
  15.6 1.5 %collective-permute-start.7 = (bf16[2,64,768]{2,1,0:T(8,128)(2,1)S(1)}, bf16[2,64,768]{2,1,0:T(8,128)(2,1)S(1)}, u32[]{:S(2)}, u32[]{:S(2)}) collective-permute-start(bf16[2,64,768]{2,1,0:T(8,128)(2,1)S(1)} %get-tuple-element.67), channel_id=1, source_target_pairs={{0,16},{8,24},{16,0},{24,8},{1,17},{9,25},{17,1},{25,9},{2,18},{10... | collective-permute-start | bytes 589832 | tf_op jit(solution)/shard_map/ppermute | solution.py:482
  17.1 0.5 collective-permute-start.8
  17.6 1.4 %collective-permute-done.2.refs_1_ = bf16[128,768]{1,0:T(8,128)(2,1)S(1)} collective-permute-done((bf16[128,768]{1,0:T(8,128)(2,1)S(1)}, bf16[128,768]{1,0:T(8,128)(2,1)S(1)}, u32[]{:S(2)}, u32[]{:S(2)}) %collective-permute-start.2) | collective-permute-done | bytes 196640 | tf_op jit(solution)/shard_map/ppermute | solution.py:475
  18.9 0.4 pack.3
  19.3 1.6 %collective-permute-start.3 = (bf16[2,64,768]{2,1,0:T(8,128)(2,1)S(1)}, bf16[2,64,768]{2,1,0:T(8,128)(2,1)S(1)}, u32[]{:S(2)}, u32[]{:S(2)}) collective-permute-start(bf16[2,64,768]{2,1,0:T(8,128)(2,1)S(1)} %get-tuple-element.62), channel_id=1, source_target_pairs={{0,8},{8,0},{16,24},{24,16},{1,9},{9,1},{17,25},{25,17},{2,10},{10... | collective-permute-start | bytes 589832 | tf_op jit(solution)/shard_map/ppermute | solution.py:482
  20.9 1.5 %collective-permute-start.4 = (bf16[2,64,768]{2,1,0:T(8,128)(2,1)S(1)}, bf16[2,64,768]{2,1,0:T(8,128)(2,1)S(1)}, u32[]{:S(2)}, u32[]{:S(2)}) collective-permute-start(bf16[2,64,768]{2,1,0:T(8,128)(2,1)S(1)} %get-tuple-element.63), channel_id=1, source_target_pairs={{0,16},{8,24},{16,0},{24,8},{1,17},{9,25},{17,1},{25,9},{2,18},{10... | collective-permute-start | bytes 589832 | tf_op jit(solution)/shard_map/ppermute | solution.py:482
  22.4 0.6 collective-permute-start.5
  23.0 2.4 %activations.1 = (f32[1024,256]{1,0:T(8,128)S(1)}, f32[1024,256]{1,0:T(8,128)S(1)}, bf16[1024,256]{1,0:T(8,128)(2,1)S(1)}, f32[8,128]{1,0:T(8,128)S(1)}) custom-call(bf16[1,4,64,1024]{3,2,1,0:T(8,128)(2,1)} %refs_0_.3, bf16[1,4,64,1024]{3,2,1,0:T(8,128)(2,1)} %refs_1_.2, f32[8,128]{1,0:T(8,128)S(1)} %get-tuple-element.69.refs_2_), custom_call_target="tpu_custom_call" | custom-call | flops 12000000000 | bytes 1000 | tf_op jit(solution)/shard_map/activations/pallas_call | solution.py:45
  25.4 0.1 join.2
  25.5 0.1 collective-permute-start.10
  25.5 3.1 %collective-permute-done.3.refs_1_ = bf16[2,64,768]{2,1,0:T(8,128)(2,1)S(1)} collective-permute-done((bf16[2,64,768]{2,1,0:T(8,128)(2,1)S(1)}, bf16[2,64,768]{2,1,0:T(8,128)(2,1)S(1)}, u32[]{:S(2)}, u32[]{:S(2)}) %collective-permute-start.3) | collective-permute-done | bytes 196640 | tf_op jit(solution)/shard_map/ppermute | solution.py:482
  28.6 4.0 %collective-permute-done.4.refs_2_ = bf16[2,64,768]{2,1,0:T(8,128)(2,1)S(1)} collective-permute-done((bf16[2,64,768]{2,1,0:T(8,128)(2,1)S(1)}, bf16[2,64,768]{2,1,0:T(8,128)(2,1)S(1)}, u32[]{:S(2)}, u32[]{:S(2)}) %collective-permute-start.4) | collective-permute-done | bytes 196640 | tf_op jit(solution)/shard_map/ppermute | solution.py:482
  32.6 0.1 collective-permute-start.9
  32.8 2.6 %hidden_part.2 = (f32[1024,256]{1,0:T(8,128)S(1)}, f32[8,128]{1,0:T(8,128)S(1)}) custom-call(bf16[2,256,768]{2,1,0:T(8,128)(2,1)S(1)} %get-tuple-element.73.refs_0_.refs_1_, bf16[2,256,768]{2,1,0:T(8,128)(2,1)S(1)} %collective-permute-done.10.refs_1_.refs_2_, bf16[2,256,768]{2,1,0:T(8,128)(2,1)S(1)} %get-tuple-element.72.refs_2_.refs_1_, ...), custom_call_target="tpu_custom_call" | custom-call | flops 1000 | bytes 1000 | tf_op jit(solution)/shard_map/hidden_part/pallas_call | solution.py:45
  35.5 1.1 %hidden_part.3 = (bf16[1024,256]{1,0:T(8,128)(2,1)S(1)}, bf16[1024,256]{1,0:T(8,128)(2,1)S(1)}, f32[8,128]{1,0:T(8,128)S(1)}) custom-call(bf16[2,256,768]{2,1,0:T(8,128)(2,1)S(1)} %collective-permute-done.9.refs_0_.refs_2_, bf16[1,1024,6144]{2,1,0:T(8,128)(2,1)S(1)} %bitcast.7, f32[1024,256]{1,0:T(8,128)S(1)} %get-tuple-element.75.refs_2_, ...), custom_call_target="tpu_custom_call" | custom-call | flops 1000 | bytes 1000 | tf_op jit(solution)/shard_map/hidden_part/pallas_call | solution.py:45
  36.6 1.3 %slice-done.5 = s8[4194304]{0:T(1024)(128)(4,1)S(1)} async-done(((s8[12582912]{0:T(1024)(128)(4,1)}), s8[4194304]{0:T(1024)(128)(4,1)S(1)}, s32[]{:S(2)}) %slice-start.5) | async-done | bytes 4194328
  37.9 1.9 %slot_part.4 = (bf16[2,256,768]{2,1,0:T(8,128)(2,1)S(1)}, f32[8,128]{1,0:T(8,128)S(1)}) custom-call(bf16[1024,256]{1,0:T(8,128)(2,1)S(1)} %get-tuple-element.79.refs_0_, bf16[1024,256]{1,0:T(8,128)(2,1)S(1)} %get-tuple-element.80.refs_1_, bf16[1,6144,1024]{2,1,0:T(8,128)(2,1)S(1)} %bitcast.3, bf16[1,6144,1024]{2,1,0:T(8,128)(2,1)S(1)} %bitcast.5, ...), custom_call_target="tpu_custom_call" | custom-call | flops 1610612736 | bytes 7340032 | tf_op jit(solution)/shard_map/slot_part/pallas_call | solution.py:45
  39.8 0.5 collective-permute-start.11
  40.3 1.9 %slot_part.5 = (f32[2,256,768]{2,1,0:T(8,128)S(1)}, f32[8,128]{1,0:T(8,128)S(1)}) custom-call(bf16[1024,256]{1,0:T(8,128)(2,1)S(1)} %get-tuple-element.79.refs_0_, bf16[1024,256]{1,0:T(8,128)(2,1)S(1)} %get-tuple-element.80.refs_1_, bf16[1,6144,1024]{2,1,0:T(8,128)(2,1)S(1)} %bitcast.3, bf16[1,6144,1024]{2,1,0:T(8,128)(2,1)S(1)} %bitcast.5, ...), custom_call_target="tpu_custom_call" | custom-call | flops 1610612736 | bytes 7340032 | tf_op jit(solution)/shard_map/slot_part/pallas_call | solution.py:45
  42.3 0.2 add_halves.2
  42.5 1.9 %slot_part.6 = (bf16[2,256,768]{2,1,0:T(8,128)(2,1)S(1)}, f32[8,128]{1,0:T(8,128)S(1)}) custom-call(bf16[1024,256]{1,0:T(8,128)(2,1)S(1)} %get-tuple-element.79.refs_0_, bf16[1024,256]{1,0:T(8,128)(2,1)S(1)} %get-tuple-element.80.refs_1_, bf16[1,6144,1024]{2,1,0:T(8,128)(2,1)S(1)} %bitcast.3, bf16[1,6144,1024]{2,1,0:T(8,128)(2,1)S(1)} %bitcast.5, ...), custom_call_target="tpu_custom_call" | custom-call | flops 1610612736 | bytes 7340032 | tf_op jit(solution)/shard_map/slot_part/pallas_call | solution.py:45
  44.4 0.4 collective-permute-start.12
  44.8 0.9 %collective-permute-start.16 = (bf16[2,64,768]{2,1,0:T(8,128)(2,1)S(1)}, bf16[2,64,768]{2,1,0:T(8,128)(2,1)S(1)}, u32[]{:S(2)}, u32[]{:S(2)}) collective-permute-start(bf16[2,64,768]{2,1,0:T(8,128)(2,1)S(1)} %get-tuple-element.98), channel_id=1, source_target_pairs={{0,8},{8,0},{16,24},{24,16},{1,9},{9,1},{17,25},{25,17},{2,10},{10... | collective-permute-start | bytes 589832 | tf_op jit(solution)/shard_map/ppermute | solution.py:482
  45.7 0.8 %collective-permute-start.17 = (bf16[2,64,768]{2,1,0:T(8,128)(2,1)S(1)}, bf16[2,64,768]{2,1,0:T(8,128)(2,1)S(1)}, u32[]{:S(2)}, u32[]{:S(2)}) collective-permute-start(bf16[2,64,768]{2,1,0:T(8,128)(2,1)S(1)} %get-tuple-element.99), channel_id=1, source_target_pairs={{0,16},{8,24},{16,0},{24,8},{1,17},{9,25},{17,1},{25,9},{2,18},{10... | collective-permute-start | bytes 589832 | tf_op jit(solution)/shard_map/ppermute | solution.py:482
  46.5 1.7 %collective-permute-start.18 = (bf16[2,64,768]{2,1,0:T(8,128)(2,1)S(1)}, bf16[2,64,768]{2,1,0:T(8,128)(2,1)S(1)}, u32[]{:S(2)}, u32[]{:S(2)}) collective-permute-start(bf16[2,64,768]{2,1,0:T(8,128)(2,1)S(1)} %get-tuple-element.100), channel_id=1, source_target_pairs={{0,24},{8,16},{16,8},{24,0},{1,25},{9,17},{17,9},{25,1},{2,26},{10... | collective-permute-start | bytes 589832 | tf_op jit(solution)/shard_map/ppermute | solution.py:482
  48.3 3.3 %down_part.2 = (bf16[1,1024,6144]{2,1,0:T(8,128)(2,1)}, f32[8,128]{1,0:T(8,128)S(1)}) custom-call(bf16[1024,256]{1,0:T(8,128)(2,1)S(1)} %get-tuple-element.81.refs_0_, bf16[2,256,768]{2,1,0:T(8,128)(2,1)S(1)} %get-tuple-element.73.refs_0_.refs_1_, bf16[2,256,768]{2,1,0:T(8,128)(2,1)S(1)} %collective-permute-done.10.refs_1_.refs_2_, ...), custom_call_target="tpu_custom_call" | custom-call | flops 1610612736 | bytes 6291456 | tf_op jit(solution)/shard_map/down_part/pallas_call | solution.py:45
  51.5 2.0 %slot_part.7 = (f32[2,256,768]{2,1,0:T(8,128)S(1)}, f32[8,128]{1,0:T(8,128)S(1)}) custom-call(bf16[1024,256]{1,0:T(8,128)(2,1)S(1)} %get-tuple-element.79.refs_0_, bf16[1024,256]{1,0:T(8,128)(2,1)S(1)} %get-tuple-element.80.refs_1_, bf16[1,6144,1024]{2,1,0:T(8,128)(2,1)S(1)} %bitcast.3, bf16[1,6144,1024]{2,1,0:T(8,128)(2,1)S(1)} %bitcast.5, ...), custom_call_target="tpu_custom_call" | custom-call | flops 1610612736 | bytes 7340032 | tf_op jit(solution)/shard_map/slot_part/pallas_call | solution.py:45
  53.5 0.2 add_halves.3
  53.7 1.0 %collective-permute-start.13 = (bf16[2,64,768]{2,1,0:T(8,128)(2,1)S(1)}, bf16[2,64,768]{2,1,0:T(8,128)(2,1)S(1)}, u32[]{:S(2)}, u32[]{:S(2)}) collective-permute-start(bf16[2,64,768]{2,1,0:T(8,128)(2,1)S(1)} %get-tuple-element.94), channel_id=1, source_target_pairs={{0,8},{8,0},{16,24},{24,16},{1,9},{9,1},{17,25},{25,17},{2,10},{10... | collective-permute-start | bytes 589832 | tf_op jit(solution)/shard_map/ppermute | solution.py:482
  54.7 0.8 %collective-permute-start.14 = (bf16[2,64,768]{2,1,0:T(8,128)(2,1)S(1)}, bf16[2,64,768]{2,1,0:T(8,128)(2,1)S(1)}, u32[]{:S(2)}, u32[]{:S(2)}) collective-permute-start(bf16[2,64,768]{2,1,0:T(8,128)(2,1)S(1)} %get-tuple-element.95), channel_id=1, source_target_pairs={{0,16},{8,24},{16,0},{24,8},{1,17},{9,25},{17,1},{25,9},{2,18},{10... | collective-permute-start | bytes 589832 | tf_op jit(solution)/shard_map/ppermute | solution.py:482
  55.5 1.7 %collective-permute-start.15 = (bf16[2,64,768]{2,1,0:T(8,128)(2,1)S(1)}, bf16[2,64,768]{2,1,0:T(8,128)(2,1)S(1)}, u32[]{:S(2)}, u32[]{:S(2)}) collective-permute-start(bf16[2,64,768]{2,1,0:T(8,128)(2,1)S(1)} %get-tuple-element.96), channel_id=1, source_target_pairs={{0,24},{8,16},{16,8},{24,0},{1,25},{9,17},{17,9},{25,1},{2,26},{10... | collective-permute-start | bytes 589832 | tf_op jit(solution)/shard_map/ppermute | solution.py:482
  57.2 0.5 combine.2
  57.7 0.8 %collective-permute-start.19 = (bf16[128,768]{1,0:T(8,128)(2,1)S(1)}, bf16[128,768]{1,0:T(8,128)(2,1)S(1)}, u32[]{:S(2)}, u32[]{:S(2)}) collective-permute-start(bf16[128,768]{1,0:T(8,128)(2,1)S(1)} %get-tuple-element.102), channel_id=1, source_target_pairs={{0,4},{1,5},{4,6},{5,7},{6,2},{7,3},{2,0},{3,1},{8,12},{9,13},{12,... | collective-permute-start | bytes 589832 | tf_op jit(solution)/shard_map/ppermute | solution.py:475
  58.5 1.3 %collective-permute-start.20 = (bf16[128,768]{1,0:T(8,128)(2,1)S(1)}, bf16[128,768]{1,0:T(8,128)(2,1)S(1)}, u32[]{:S(2)}, u32[]{:S(2)}) collective-permute-start(bf16[128,768]{1,0:T(8,128)(2,1)S(1)} %get-tuple-element.105), channel_id=1, source_target_pairs={{0,2},{1,3},{4,0},{5,1},{6,4},{7,5},{2,6},{3,7},{8,10},{9,11},{12,... | collective-permute-start | bytes 589832 | tf_op jit(solution)/shard_map/ppermute | solution.py:475
  59.8 1.8 %collective-permute-done.13.refs_1_ = bf16[2,64,768]{2,1,0:T(8,128)(2,1)S(1)} collective-permute-done((bf16[2,64,768]{2,1,0:T(8,128)(2,1)S(1)}, bf16[2,64,768]{2,1,0:T(8,128)(2,1)S(1)}, u32[]{:S(2)}, u32[]{:S(2)}) %collective-permute-start.13) | collective-permute-done | bytes 196640 | tf_op jit(solution)/shard_map/ppermute | solution.py:482
  61.6 0.7 collective-permute-done.14.refs_2_
  62.3 2.8 %collective-permute-done.15.refs_3_ = bf16[2,64,768]{2,1,0:T(8,128)(2,1)S(1)} collective-permute-done((bf16[2,64,768]{2,1,0:T(8,128)(2,1)S(1)}, bf16[2,64,768]{2,1,0:T(8,128)(2,1)S(1)}, u32[]{:S(2)}, u32[]{:S(2)}) %collective-permute-start.15) | collective-permute-done | bytes 196640 | tf_op jit(solution)/shard_map/ppermute | solution.py:482
  65.1 0.3 combine.3
  65.4 2.1 %collective-permute-start.21 = (bf16[128,768]{1,0:T(8,128)(2,1)S(1)}, bf16[128,768]{1,0:T(8,128)(2,1)S(1)}, u32[]{:S(2)}, u32[]{:S(2)}) collective-permute-start(bf16[128,768]{1,0:T(8,128)(2,1)S(1)} %get-tuple-element.106), channel_id=1, source_target_pairs={{0,4},{1,5},{4,6},{5,7},{6,2},{7,3},{2,0},{3,1},{8,12},{9,13},{12,... | collective-permute-start | bytes 589832 | tf_op jit(solution)/shard_map/ppermute | solution.py:475
  67.5 3.9 %down_part.3 = (bf16[1,1024,6144]{2,1,0:T(8,128)(2,1)}, f32[8,128]{1,0:T(8,128)}) custom-call(bf16[1024,256]{1,0:T(8,128)(2,1)S(1)} %get-tuple-element.81.refs_0_, bf16[2,256,768]{2,1,0:T(8,128)(2,1)S(1)} %get-tuple-element.72.refs_2_.refs_1_, bf16[2,256,768]{2,1,0:T(8,128)(2,1)S(1)} %collective-permute-done.9.refs_0_.refs_2_, ...), custom_call_target="tpu_custom_call", output_to_operand_aliasing={{0}: (3, {})} | custom-call | tf_op jit(solution)/shard_map/down_part/pallas_call | solution.py:45
  71.4 0.5 collective-permute-done.21
  71.9 0.7 %add_convert_fusion = bf16[128,768]{1,0:T(8,128)(2,1)} fusion(bf16[128,768]{1,0:T(8,128)(2,1)S(1)} %collective-permute-done.21, f32[128,768]{1,0:T(8,128)S(1)} %get-tuple-element.104, bf16[128,768]{1,0:T(8,128)(2,1)S(1)} %collective-permute-done.20), kind=kLoop, calls=%fused_computation | loop fusion | flops 491520 | bytes 983040 | tf_op jit(solution)/shard_map/convert_element_type | solution.py:529
  (36 shorter events, 0.1 us)
Async XLA Ops:
  0.6 9.8 %collective-permute-start.1 = (bf16[128,768]{1,0:T(8,128)(2,1)}, bf16[128,768]{1,0:T(8,128)(2,1)S(1)}, u32[]{:S(2)}, u32[]{:S(2)}) collective-permute-start(bf16[128,768]{1,0:T(8,128)(2,1)} %refs_0_.2), channel_id=1, source_target_pairs={{0,4},{1,5},{4,6},{5,7},{6,2},{7,3},{2,0},{3,1},{8,12},{9,13},{12,... | collective-permute-start | bytes 589832 | tf_op jit(solution)/shard_map/ppermute | solution.py:475
  4.7 12.9 %collective-permute-start = (bf16[128,768]{1,0:T(8,128)(2,1)}, bf16[128,768]{1,0:T(8,128)(2,1)S(1)}, u32[]{:S(2)}, u32[]{:S(2)}) collective-permute-start(bf16[128,768]{1,0:T(8,128)(2,1)} %refs_0_.2), channel_id=1, source_target_pairs={{0,2},{1,3},{4,0},{5,1},{6,4},{7,5},{2,6},{3,7},{8,10},{9,11},{12,... | collective-permute-start | bytes 589832 | tf_op jit(solution)/shard_map/ppermute | solution.py:475
  10.4 8.5 %collective-permute-start.2 = (bf16[128,768]{1,0:T(8,128)(2,1)S(1)}, bf16[128,768]{1,0:T(8,128)(2,1)S(1)}, u32[]{:S(2)}, u32[]{:S(2)}) collective-permute-start(bf16[128,768]{1,0:T(8,128)(2,1)S(1)} %collective-permute-done.1.refs_1_), channel_id=1, source_target_pairs={{0,4},{1,5},{4,6},{5,7},{6,2},{7,3},{2,0},{3,1},{8,12},{9,13},{12,... | collective-permute-start | bytes 589832 | tf_op jit(solution)/shard_map/ppermute | solution.py:475
  14.0 8.4 %collective-permute-start.6 = (bf16[2,64,768]{2,1,0:T(8,128)(2,1)S(1)}, bf16[2,64,768]{2,1,0:T(8,128)(2,1)S(1)}, u32[]{:S(2)}, u32[]{:S(2)}) collective-permute-start(bf16[2,64,768]{2,1,0:T(8,128)(2,1)S(1)} %get-tuple-element.66), channel_id=1, source_target_pairs={{0,8},{8,0},{16,24},{24,16},{1,9},{9,1},{17,25},{25,17},{2,10},{10... | collective-permute-start | bytes 589832 | tf_op jit(solution)/shard_map/ppermute | solution.py:482
  15.6 9.8 %collective-permute-start.7 = (bf16[2,64,768]{2,1,0:T(8,128)(2,1)S(1)}, bf16[2,64,768]{2,1,0:T(8,128)(2,1)S(1)}, u32[]{:S(2)}, u32[]{:S(2)}) collective-permute-start(bf16[2,64,768]{2,1,0:T(8,128)(2,1)S(1)} %get-tuple-element.67), channel_id=1, source_target_pairs={{0,16},{8,24},{16,0},{24,8},{1,17},{9,25},{17,1},{25,9},{2,18},{10... | collective-permute-start | bytes 589832 | tf_op jit(solution)/shard_map/ppermute | solution.py:482
  17.1 8.3 %collective-permute-start.8 = (bf16[2,64,768]{2,1,0:T(8,128)(2,1)S(1)}, bf16[2,64,768]{2,1,0:T(8,128)(2,1)S(1)}, u32[]{:S(2)}, u32[]{:S(2)}) collective-permute-start(bf16[2,64,768]{2,1,0:T(8,128)(2,1)S(1)} %get-tuple-element.68), channel_id=1, source_target_pairs={{0,24},{8,16},{16,8},{24,0},{1,25},{9,17},{17,9},{25,1},{2,26},{10... | collective-permute-start | bytes 589832 | tf_op jit(solution)/shard_map/ppermute | solution.py:482
  18.9 13.8 %slice-start.6 = ((s8[12582912]{0:T(1024)(128)(4,1)}), s8[4194304]{0:T(1024)(128)(4,1)S(1)}, s32[]{:S(2)}) async-start(s8[12582912]{0:T(1024)(128)(4,1)} %bitcast.6), calls=%async_computation.6 | async-start | bytes 8388608
  19.3 9.3 %collective-permute-start.3 = (bf16[2,64,768]{2,1,0:T(8,128)(2,1)S(1)}, bf16[2,64,768]{2,1,0:T(8,128)(2,1)S(1)}, u32[]{:S(2)}, u32[]{:S(2)}) collective-permute-start(bf16[2,64,768]{2,1,0:T(8,128)(2,1)S(1)} %get-tuple-element.62), channel_id=1, source_target_pairs={{0,8},{8,0},{16,24},{24,16},{1,9},{9,1},{17,25},{25,17},{2,10},{10... | collective-permute-start | bytes 589832 | tf_op jit(solution)/shard_map/ppermute | solution.py:482
  20.9 11.7 %collective-permute-start.4 = (bf16[2,64,768]{2,1,0:T(8,128)(2,1)S(1)}, bf16[2,64,768]{2,1,0:T(8,128)(2,1)S(1)}, u32[]{:S(2)}, u32[]{:S(2)}) collective-permute-start(bf16[2,64,768]{2,1,0:T(8,128)(2,1)S(1)} %get-tuple-element.63), channel_id=1, source_target_pairs={{0,16},{8,24},{16,0},{24,8},{1,17},{9,25},{17,1},{25,9},{2,18},{10... | collective-permute-start | bytes 589832 | tf_op jit(solution)/shard_map/ppermute | solution.py:482
  22.4 10.2 %collective-permute-start.5 = (bf16[2,64,768]{2,1,0:T(8,128)(2,1)S(1)}, bf16[2,64,768]{2,1,0:T(8,128)(2,1)S(1)}, u32[]{:S(2)}, u32[]{:S(2)}) collective-permute-start(bf16[2,64,768]{2,1,0:T(8,128)(2,1)S(1)} %get-tuple-element.64), channel_id=1, source_target_pairs={{0,24},{8,16},{16,8},{24,0},{1,25},{9,17},{17,9},{25,1},{2,26},{10... | collective-permute-start | bytes 589832 | tf_op jit(solution)/shard_map/ppermute | solution.py:482
  23.0 12.5 %slice-start = ((s8[12582912]{0:T(1024)(128)(4,1)}), s8[4194304]{0:T(1024)(128)(4,1)S(1)}, s32[]{:S(2)}) async-start(s8[12582912]{0:T(1024)(128)(4,1)} %bitcast.2), calls=%async_computation | async-start | bytes 8388608
  23.0 9.8 %slice-start.7 = ((s8[12582912]{0:T(1024)(128)(4,1)}), s8[4194304]{0:T(1024)(128)(4,1)S(1)}, s32[]{:S(2)}) async-start(s8[12582912]{0:T(1024)(128)(4,1)} %bitcast.6), calls=%async_computation.7 | async-start | bytes 8388608
  23.0 9.8 %slice-start.8 = ((s8[12582912]{0:T(1024)(128)(4,1)}), s8[4194304]{0:T(1024)(128)(4,1)S(1)}, s32[]{:S(2)}) async-start(s8[12582912]{0:T(1024)(128)(4,1)} %bitcast.6), calls=%async_computation.8 | async-start | bytes 8388608
  23.0 12.5 %slice-start.1 = ((s8[12582912]{0:T(1024)(128)(4,1)}), s8[4194304]{0:T(1024)(128)(4,1)S(1)}, s32[]{:S(2)}) async-start(s8[12582912]{0:T(1024)(128)(4,1)} %bitcast.2), calls=%async_computation.1 | async-start | bytes 8388608
  23.0 12.5 %slice-start.2 = ((s8[12582912]{0:T(1024)(128)(4,1)}), s8[4194304]{0:T(1024)(128)(4,1)S(1)}, s32[]{:S(2)}) async-start(s8[12582912]{0:T(1024)(128)(4,1)} %bitcast.2), calls=%async_computation.2 | async-start | bytes 8388608
  25.5 7.3 %collective-permute-start.10 = (bf16[2,256,768]{2,1,0:T(8,128)(2,1)S(1)}, bf16[2,256,768]{2,1,0:T(8,128)(2,1)S(1)}, u32[]{:S(2)}, u32[]{:S(2)}) collective-permute-start(bf16[2,256,768]{2,1,0:T(8,128)(2,1)S(1)} %get-tuple-element.73.refs_0_.refs_1_), channel_id=1, source_target_pairs={{0,1},{1,0},{2,3},{3,2},{4,5},{5,4},{6,7},{7,6},{8,9},{9,8},{10,11... | collective-permute-start | bytes 2359304 | tf_op jit(solution)/shard_map/ppermute | solution.py:478
  32.6 2.8 %collective-permute-start.9 = (bf16[2,256,768]{2,1,0:T(8,128)(2,1)S(1)}, bf16[2,256,768]{2,1,0:T(8,128)(2,1)S(1)}, u32[]{:S(2)}, u32[]{:S(2)}) collective-permute-start(bf16[2,256,768]{2,1,0:T(8,128)(2,1)S(1)} %get-tuple-element.72.refs_2_.refs_1_), channel_id=1, source_target_pairs={{0,1},{1,0},{2,3},{3,2},{4,5},{5,4},{6,7},{7,6},{8,9},{9,8},{10,11... | collective-permute-start | bytes 2359304 | tf_op jit(solution)/shard_map/ppermute | solution.py:478
  32.8 3.8 %slice-start.3 = ((s8[12582912]{0:T(1024)(128)(4,1)}), s8[4194304]{0:T(1024)(128)(4,1)S(1)}, s32[]{:S(2)}) async-start(s8[12582912]{0:T(1024)(128)(4,1)} %bitcast.4), calls=%async_computation.3 | async-start | bytes 8388608
  32.8 3.8 %slice-start.4 = ((s8[12582912]{0:T(1024)(128)(4,1)}), s8[4194304]{0:T(1024)(128)(4,1)S(1)}, s32[]{:S(2)}) async-start(s8[12582912]{0:T(1024)(128)(4,1)} %bitcast.4), calls=%async_computation.4 | async-start | bytes 8388608
  35.5 2.4 %slice-start.5 = ((s8[12582912]{0:T(1024)(128)(4,1)}), s8[4194304]{0:T(1024)(128)(4,1)S(1)}, s32[]{:S(2)}) async-start(s8[12582912]{0:T(1024)(128)(4,1)} %bitcast.4), calls=%async_computation.5 | async-start | bytes 8388608
  39.8 2.5 %collective-permute-start.11 = (bf16[2,256,768]{2,1,0:T(8,128)(2,1)S(1)}, bf16[2,256,768]{2,1,0:T(8,128)(2,1)S(1)}, u32[]{:S(2)}, u32[]{:S(2)}) collective-permute-start(bf16[2,256,768]{2,1,0:T(8,128)(2,1)S(1)} %get-tuple-element.85), channel_id=1, source_target_pairs={{0,1},{1,0},{2,3},{3,2},{4,5},{5,4},{6,7},{7,6},{8,9},{9,8},{10,11... | collective-permute-start | bytes 2359304 | tf_op jit(solution)/shard_map/ppermute | solution.py:478
  44.4 9.1 %collective-permute-start.12 = (bf16[2,256,768]{2,1,0:T(8,128)(2,1)S(1)}, bf16[2,256,768]{2,1,0:T(8,128)(2,1)S(1)}, u32[]{:S(2)}, u32[]{:S(2)}) collective-permute-start(bf16[2,256,768]{2,1,0:T(8,128)(2,1)S(1)} %get-tuple-element.91), channel_id=1, source_target_pairs={{0,1},{1,0},{2,3},{3,2},{4,5},{5,4},{6,7},{7,6},{8,9},{9,8},{10,11... | collective-permute-start | bytes 2359304 | tf_op jit(solution)/shard_map/ppermute | solution.py:478
  44.8 10.8 %collective-permute-start.16 = (bf16[2,64,768]{2,1,0:T(8,128)(2,1)S(1)}, bf16[2,64,768]{2,1,0:T(8,128)(2,1)S(1)}, u32[]{:S(2)}, u32[]{:S(2)}) collective-permute-start(bf16[2,64,768]{2,1,0:T(8,128)(2,1)S(1)} %get-tuple-element.98), channel_id=1, source_target_pairs={{0,8},{8,0},{16,24},{24,16},{1,9},{9,1},{17,25},{25,17},{2,10},{10... | collective-permute-start | bytes 589832 | tf_op jit(solution)/shard_map/ppermute | solution.py:482
  45.7 11.5 %collective-permute-start.17 = (bf16[2,64,768]{2,1,0:T(8,128)(2,1)S(1)}, bf16[2,64,768]{2,1,0:T(8,128)(2,1)S(1)}, u32[]{:S(2)}, u32[]{:S(2)}) collective-permute-start(bf16[2,64,768]{2,1,0:T(8,128)(2,1)S(1)} %get-tuple-element.99), channel_id=1, source_target_pairs={{0,16},{8,24},{16,0},{24,8},{1,17},{9,25},{17,1},{25,9},{2,18},{10... | collective-permute-start | bytes 589832 | tf_op jit(solution)/shard_map/ppermute | solution.py:482
  46.5 10.7 %collective-permute-start.18 = (bf16[2,64,768]{2,1,0:T(8,128)(2,1)S(1)}, bf16[2,64,768]{2,1,0:T(8,128)(2,1)S(1)}, u32[]{:S(2)}, u32[]{:S(2)}) collective-permute-start(bf16[2,64,768]{2,1,0:T(8,128)(2,1)S(1)} %get-tuple-element.100), channel_id=1, source_target_pairs={{0,24},{8,16},{16,8},{24,0},{1,25},{9,17},{17,9},{25,1},{2,26},{10... | collective-permute-start | bytes 589832 | tf_op jit(solution)/shard_map/ppermute | solution.py:482
  53.7 7.9 %collective-permute-start.13 = (bf16[2,64,768]{2,1,0:T(8,128)(2,1)S(1)}, bf16[2,64,768]{2,1,0:T(8,128)(2,1)S(1)}, u32[]{:S(2)}, u32[]{:S(2)}) collective-permute-start(bf16[2,64,768]{2,1,0:T(8,128)(2,1)S(1)} %get-tuple-element.94), channel_id=1, source_target_pairs={{0,8},{8,0},{16,24},{24,16},{1,9},{9,1},{17,25},{25,17},{2,10},{10... | collective-permute-start | bytes 589832 | tf_op jit(solution)/shard_map/ppermute | solution.py:482
  54.7 7.6 %collective-permute-start.14 = (bf16[2,64,768]{2,1,0:T(8,128)(2,1)S(1)}, bf16[2,64,768]{2,1,0:T(8,128)(2,1)S(1)}, u32[]{:S(2)}, u32[]{:S(2)}) collective-permute-start(bf16[2,64,768]{2,1,0:T(8,128)(2,1)S(1)} %get-tuple-element.95), channel_id=1, source_target_pairs={{0,16},{8,24},{16,0},{24,8},{1,17},{9,25},{17,1},{25,9},{2,18},{10... | collective-permute-start | bytes 589832 | tf_op jit(solution)/shard_map/ppermute | solution.py:482
  55.5 9.5 %collective-permute-start.15 = (bf16[2,64,768]{2,1,0:T(8,128)(2,1)S(1)}, bf16[2,64,768]{2,1,0:T(8,128)(2,1)S(1)}, u32[]{:S(2)}, u32[]{:S(2)}) collective-permute-start(bf16[2,64,768]{2,1,0:T(8,128)(2,1)S(1)} %get-tuple-element.96), channel_id=1, source_target_pairs={{0,24},{8,16},{16,8},{24,0},{1,25},{9,17},{17,9},{25,1},{2,26},{10... | collective-permute-start | bytes 589832 | tf_op jit(solution)/shard_map/ppermute | solution.py:482
  57.7 7.4 %collective-permute-start.19 = (bf16[128,768]{1,0:T(8,128)(2,1)S(1)}, bf16[128,768]{1,0:T(8,128)(2,1)S(1)}, u32[]{:S(2)}, u32[]{:S(2)}) collective-permute-start(bf16[128,768]{1,0:T(8,128)(2,1)S(1)} %get-tuple-element.102), channel_id=1, source_target_pairs={{0,4},{1,5},{4,6},{5,7},{6,2},{7,3},{2,0},{3,1},{8,12},{9,13},{12,... | collective-permute-start | bytes 589832 | tf_op jit(solution)/shard_map/ppermute | solution.py:475
  58.5 12.9 %collective-permute-start.20 = (bf16[128,768]{1,0:T(8,128)(2,1)S(1)}, bf16[128,768]{1,0:T(8,128)(2,1)S(1)}, u32[]{:S(2)}, u32[]{:S(2)}) collective-permute-start(bf16[128,768]{1,0:T(8,128)(2,1)S(1)} %get-tuple-element.105), channel_id=1, source_target_pairs={{0,2},{1,3},{4,0},{5,1},{6,4},{7,5},{2,6},{3,7},{8,10},{9,11},{12,... | collective-permute-start | bytes 589832 | tf_op jit(solution)/shard_map/ppermute | solution.py:475
  65.4 6.5 %collective-permute-start.21 = (bf16[128,768]{1,0:T(8,128)(2,1)S(1)}, bf16[128,768]{1,0:T(8,128)(2,1)S(1)}, u32[]{:S(2)}, u32[]{:S(2)}) collective-permute-start(bf16[128,768]{1,0:T(8,128)(2,1)S(1)} %get-tuple-element.106), channel_id=1, source_target_pairs={{0,4},{1,5},{4,6},{5,7},{6,2},{7,3},{2,0},{3,1},{8,12},{9,13},{12,... | collective-permute-start | bytes 589832 | tf_op jit(solution)/shard_map/ppermute | solution.py:475
